TPU v7x, 32 devices: a whole 2x2x4 slice. The times are simulated.
32 devices in a mesh: parts: 2 (over y), gx: 4 (over z), gy: 4 (over x, core).
Axes of the slice: x: 2, y: 2, z: 4, core: 2. Of those that a mesh axis runs over, the one named last changes fastest.
Arguments:
- tokens: bfloat16 [128, 12288], P(('parts', 'gx'), 'gy'), parts along dimension 0, may hold values from -6 to 6
- w_query: bfloat16 [12288, 12288], P('gy', 'gx'), may hold values from -0.0546875 to 0.0546875
- key_matrix: bfloat16 [12288, 1024], P('gy', 'gx'), may hold values from -0.0546875 to 0.0546875
- value_matrix: bfloat16 [12288, 1024], P('gy', 'gx'), may hold values from -0.0546875 to 0.0546875
- w_output: bfloat16 [12288, 12288], P('gy', 'gx'), may hold values from -0.0546875 to 0.0546875
- stored_keys: bfloat16 [128, 128, 1024], P(('parts', 'gy', 'gx')), parts along dimension 0, may hold values from -260 to 260
- stored_values: bfloat16 [128, 128, 1024], P(('parts', 'gy', 'gx')), parts along dimension 0, may hold values from -6 to 6
- lengths: int32 [128], P(('parts', 'gy', 'gx')), parts along dimension 0, may hold values from 1 to 128, as said below
- positions: int32 [128], P(('parts', 'gy', 'gx')), parts along dimension 0, may hold values from 128 to 4095
Outputs:
- attended: bfloat16 [128, 12288], P(('parts', 'gy'), 'gx'), parts along dimension 0
There are 2 independent parts, one for each index of `parts`. A program takes and returns all parts, laid end to end along the dimension named above; an argument that names none is the same for every part. Nothing has to cross between parts.
Inputs may be any that keep to these rules, and one draw needn't show every extreme that they name: `lengths`: every row has at least one live position, and in every draw some row has all 128.
All inputs are finite; a program needn't handle non-finite values.
Results may differ from a plain program's by a relative error of at most 0.012.
The roundings to bfloat16 on the way count: a program that leaves them out, or rounds other values in their place, can miss the bound.
Values may be sent and summed in bfloat16 or wider, within the bound.
No kernel may reach another device: no remote copies, remote signals or barrier semaphores. Data moves between devices by JAX's collectives and lax.ppermute only.
A program may use at most 128 MiB of HBM per device.

v0:
```python
import jax
import jax.numpy as jnp
from jax import lax
from jax.sharding import PartitionSpec as P

QUERY_HEADS = 96
KEY_VALUE_HEADS = 8
HEAD_WIDTH = 128
CONTEXT_LENGTH = 128


rope_theta = 1000000.0


def rotary_table(values, positions, heads):
    number_rows = values.shape[0]
    head_size = values.shape[1] // heads
    half_dim = head_size // 2
    wide = values.astype(jnp.float32).reshape(number_rows, heads, head_size)
    frequency = rope_theta ** (-(jnp.arange(half_dim, dtype=jnp.float32) * 2.0) / head_size)
    angles = positions.astype(jnp.float32)[:, None] * frequency[None, :]
    cosine = jnp.cos(angles)[:, None, :]
    sine = jnp.sin(angles)[:, None, :]
    lower_half = wide[..., :half_dim]
    upper_half = wide[..., half_dim:]
    turned = jnp.concatenate(
        [lower_half * cosine - upper_half * sine, upper_half * cosine + lower_half * sine], axis=-1
    )
    return turned.reshape(values.shape).astype(jnp.bfloat16)


def attend(rotated_query, rotated_key, fresh_value, device_keys, device_values, lengths):
    number_rows = rotated_query.shape[0]
    group_size = QUERY_HEADS // KEY_VALUE_HEADS
    logit_scale = 1.0 / HEAD_WIDTH**0.5
    per_head_queries = rotated_query.reshape(number_rows, KEY_VALUE_HEADS, group_size, HEAD_WIDTH)
    per_head_keys = device_keys.reshape(number_rows, CONTEXT_LENGTH, KEY_VALUE_HEADS, HEAD_WIDTH)
    scores = (
        jnp.einsum(
            "rgqd,rpgd->rgqp", per_head_queries, per_head_keys, preferred_element_type=jnp.float32
        )
        * logit_scale
    )
    live_mask = (jnp.arange(CONTEXT_LENGTH, dtype=jnp.int32)[None, :] < lengths[:, None])[
        :, None, None, :
    ]
    scores = jnp.where(live_mask, scores, -jnp.inf)
    self_score = (
        jnp.einsum(
            "uojn,uon->uoj",
            per_head_queries,
            rotated_key.reshape(number_rows, KEY_VALUE_HEADS, HEAD_WIDTH),
            preferred_element_type=jnp.float32,
        )
        * logit_scale
    )
    row_max = jnp.maximum(jnp.max(scores, axis=-1), self_score)
    cached_exp = jnp.exp(scores - row_max[..., None])
    own_exp = jnp.exp(self_score - row_max)
    totals = jnp.sum(cached_exp, axis=-1) + own_exp
    weights = (cached_exp / totals[..., None]).astype(jnp.bfloat16)
    self_weight = (own_exp / totals).astype(jnp.bfloat16)
    per_head_values = device_values.reshape(
        number_rows, CONTEXT_LENGTH, KEY_VALUE_HEADS, HEAD_WIDTH
    )
    context_window = jnp.einsum(
        "rgqp,rpgd->rgqd", weights, per_head_values, preferred_element_type=jnp.float32
    )
    context_window = context_window + self_weight.astype(jnp.float32)[
        ..., None
    ] * fresh_value.astype(jnp.float32).reshape(number_rows, KEY_VALUE_HEADS, 1, HEAD_WIDTH)
    return context_window.reshape(number_rows, QUERY_HEADS * HEAD_WIDTH).astype(jnp.bfloat16)


def shards(
    tokens,
    w_query,
    key_matrix,
    value_matrix,
    w_output,
    stored_keys,
    stored_values,
    lengths,
    positions,
):
    q_width = w_query.shape[1]
    kv_width = key_matrix.shape[1]
    piece = lax.all_gather(tokens, "gx", axis=0, tiled=True)
    partials = jnp.concatenate(
        [
            jnp.dot(piece, w_query, preferred_element_type=jnp.float32),
            jnp.dot(piece, key_matrix, preferred_element_type=jnp.float32),
            jnp.dot(piece, value_matrix, preferred_element_type=jnp.float32),
        ],
        axis=1,
    )
    summed = lax.psum_scatter(partials, "gy", scatter_dimension=0, tiled=True)
    query = summed[:, :q_width].astype(jnp.bfloat16)
    fresh_key = summed[:, q_width : q_width + kv_width].astype(jnp.bfloat16)
    fresh_value = summed[:, q_width + kv_width :].astype(jnp.bfloat16)
    query_rows, key_row_matrix, value_rows = (
        lax.all_to_all(query, "gx", split_axis=0, concat_axis=1, tiled=True),
        lax.all_to_all(fresh_key, "gx", split_axis=0, concat_axis=1, tiled=True),
        lax.all_to_all(fresh_value, "gx", split_axis=0, concat_axis=1, tiled=True),
    )
    rotated_query = rotary_table(query_rows, positions, QUERY_HEADS)
    rotated_key = rotary_table(key_row_matrix, positions, KEY_VALUE_HEADS)
    context_window = attend(
        rotated_query, rotated_key, value_rows, stored_keys, stored_values, lengths
    )
    out_width = w_output.shape[1]
    block_list = lax.all_to_all(context_window[None], "gy", split_axis=2, concat_axis=0, tiled=True)
    products = jnp.einsum(
        "jrd,de->jre",
        lax.all_gather(block_list, "gx", axis=1, tiled=True),
        w_output,
        preferred_element_type=jnp.float32,
    )
    products = products.reshape(-1, out_width)
    result = lax.psum_scatter(products, "gy", scatter_dimension=0, tiled=True)
    return result.astype(jnp.bfloat16)


def solution(mesh):
    in_specs = (
        P(("parts", "gx"), "gy"),
        P("gy", "gx"),
        P("gy", "gx"),
        P("gy", "gx"),
        P("gy", "gx"),
        P(("parts", "gy", "gx"), None, None),
        P(("parts", "gy", "gx"), None, None),
        P(("parts", "gy", "gx")),
        P(("parts", "gy", "gx")),
    )
    out_specs = P(("parts", "gy"), "gx")
    return jax.shard_map(shards, mesh=mesh, in_specs=in_specs, out_specs=out_specs, check_vma=False)
```

profile of v0, /device:TPU:0, one launch (start us, length us, event | category | flops | bytes accessed | tf_op | source)
XLA Modules:
  0.0 262.3 jit_solution(17255133400610415338)
XLA Ops:
  6.5 16.6 %all_gather.6 = bf16[64,3072]{1,0:T(8,128)(2,1)S(1)} all-gather(bf16[16,3072]{1,0:T(8,128)(2,1)} %param.9), channel_id=1, replica_groups=mesh['parts'=2,'gx'=4,'gy'=4] {'gx'}, dimensions={0}, use_global_device_ids=true | all-gather | bytes 491520 | tf_op jit(solution)/shard_map/all_gather | solution.py:88
  23.5 1.8 fusion.22
  25.3 8.1 %fusion.21 = f32[64,3072]{1,0:T(8,128)S(1)} fusion(bf16[64,3072]{1,0:T(8,128)(2,1)S(1)} %all_gather.6, bf16[3072,3072]{1,0:T(8,128)(2,1)} %param.10), kind=kOutput, calls=%fused_computation.42 | convolution fusion | flops 1207959552 | bytes 20054016 | tf_op jit(solution)/shard_map/dot_general | solution.py:91
  33.5 1.0 pad_maximum_fusion
  34.6 25.8 %reduce-scatter.3.cloned.1.call-done = f32[16,3584]{1,0:T(8,128)} async-done(((f32[64,3584]{1,0:T(8,128)}), f32[16,3584]{1,0:T(8,128)}) %reduce-scatter.3.cloned.1.call-update) | async-done | bytes 229392 | tf_op jit(solution)/shard_map/reduce_scatter | solution.py:97
  60.4 1.0 convert.23
  62.0 4.6 %all-to-all-start.1 = ((bf16[4,4,256]{2,1,0:T(4,128)(2,1)}), bf16[4,4,256]{2,1,0:T(4,128)(2,1)S(1)}, u32[]{:S(2)}, u32[]{:S(2)}) async-start(bf16[4,4,256]{2,1,0:T(4,128)(2,1)} %all_to_all.45), calls=%async_computation.2 | async-start | bytes 16384 | tf_op jit(solution)/shard_map/all_to_all | solution.py:103
  68.0 4.2 %all-to-all-done.1 = bf16[4,4,256]{2,1,0:T(4,128)(2,1)S(1)} async-done(((bf16[4,4,256]{2,1,0:T(4,128)(2,1)}), bf16[4,4,256]{2,1,0:T(4,128)(2,1)S(1)}, u32[]{:S(2)}, u32[]{:S(2)}) %all-to-all-start.1) | async-done | bytes 8224 | tf_op jit(solution)/shard_map/all_to_all | solution.py:103
  72.2 3.2 %all-to-all-start.2 = ((bf16[4,4,256]{2,1,0:T(4,128)(2,1)}), bf16[4,4,256]{2,1,0:T(4,128)(2,1)S(1)}, u32[]{:S(2)}, u32[]{:S(2)}) async-start(bf16[4,4,256]{2,1,0:T(4,128)(2,1)} %all_to_all.47), calls=%async_computation.3 | async-start | bytes 16384 | tf_op jit(solution)/shard_map/all_to_all | solution.py:104
  75.6 5.4 %all-to-all-done.2 = bf16[4,4,256]{2,1,0:T(4,128)(2,1)S(1)} async-done(((bf16[4,4,256]{2,1,0:T(4,128)(2,1)}), bf16[4,4,256]{2,1,0:T(4,128)(2,1)S(1)}, u32[]{:S(2)}, u32[]{:S(2)}) %all-to-all-start.2) | async-done | bytes 8224 | tf_op jit(solution)/shard_map/all_to_all | solution.py:104
  81.0 3.3 %all-to-all-start = ((bf16[4,4,3072]{2,1,0:T(4,128)(2,1)}), bf16[4,4,3072]{2,1,0:T(4,128)(2,1)S(1)}, u32[]{:S(2)}, u32[]{:S(2)}) async-start(bf16[4,4,3072]{2,1,0:T(4,128)(2,1)} %all_to_all.43), calls=%async_computation.1 | async-start | bytes 196608 | tf_op jit(solution)/shard_map/all_to_all | solution.py:102
  84.7 5.4 %all-to-all-done = bf16[4,4,3072]{2,1,0:T(4,128)(2,1)S(1)} async-done(((bf16[4,4,3072]{2,1,0:T(4,128)(2,1)}), bf16[4,4,3072]{2,1,0:T(4,128)(2,1)S(1)}, u32[]{:S(2)}, u32[]{:S(2)}) %all-to-all-start) | async-done | bytes 98336 | tf_op jit(solution)/shard_map/all_to_all | solution.py:102
  90.8 0.7 fusion.20
  91.9 1.7 fusion.3
  93.6 9.9 %copy.36 = bf16[1,4,12288]{1,0,2:T(2,128)(2,1)} copy(bf16[1,4,12288]{2,1,0:T(4,128)(2,1)S(1)} %convert_element_type.87) | data formatting | bytes 196608 | tf_op jit(solution)/shard_map/convert_element_type | solution.py:72
  104.1 68.7 %reduce = bf16[12288,4]{1,0:T(8,128)(2,1)} reduce(bf16[12288,1,4]{2,1,0:T(2,128)(2,1)} %bitcast.45, bf16[]{:T(256)} %broadcast.68), dimensions={1}, to_apply=%bitcast.29.reduce_sub_computation | reduce | bytes 196610
  172.8 7.3 %reshape.134 = bf16[4,2,6144]{2,1,0:T(2,128)(2,1)S(1)} reshape(bf16[12288,4]{1,0:T(8,128)(2,1)} %reduce) | data formatting | bytes 196608
  180.1 6.7 %all_to_all.57 = bf16[4,2,6144]{2,1,0:T(2,128)(2,1)S(1)} all-to-all(bf16[4,2,6144]{2,1,0:T(2,128)(2,1)S(1)} %reshape.134), channel_id=1, replica_groups=mesh['parts'=2,'gx'=4,'gy'=4] {'gy'}, dimensions={0} | all-to-all | bytes 196608 | tf_op jit(solution)/shard_map/all_to_all | solution.py:112
  186.8 8.5 %reshape.135 = bf16[12288,1,4]{2,1,0:T(2,128)(2,1)} reshape(bf16[4,2,6144]{2,1,0:T(2,128)(2,1)S(1)} %all_to_all.57) | data formatting | bytes 196608
  195.3 11.8 %copy.37 = bf16[1,4,12288]{2,1,0:T(4,128)(2,1)S(1)} copy(bf16[1,4,12288]{1,0,2:T(2,128)(2,1)} %bitcast.46) | data formatting | bytes 196608 | tf_op jit(solution)/shard_map/all_to_all | solution.py:112
  207.2 15.2 %all-gather = bf16[4,1,16,3072]{3,0,1,2:T(4,128)(2,1)S(1)} all-gather(bf16[4,1,4,3072]{3,0,1,2:T(4,128)(2,1)S(1)} %bitcast.50), channel_id=2, replica_groups=mesh['parts'=2,'gx'=4,'gy'=4] {'gx'}, dimensions={2}, use_global_device_ids=true | all-gather | bytes 491520 | tf_op jit(solution)/shard_map/all_gather | solution.py:115
  222.4 10.6 %fusion = f32[4,16,3072]{2,1,0:T(8,128)} fusion(bf16[3072,3072]{1,0:T(8,128)(2,1)} %param.13, bf16[4,1,16,3072]{3,0,1,2:T(4,128)(2,1)S(1)} %all-gather), kind=kOutput, calls=%fused_computation | convolution fusion | flops 1207959552 | bytes 20054016 | tf_op jit(solution)/shard_map/jrd,de->jre/dot_general | solution.py:113
  233.1 20.8 %reduce-scatter.5.cloned.1.call-done = f32[16,3072]{1,0:T(8,128)} async-done(((f32[64,3072]{1,0:T(8,128)}), f32[16,3072]{1,0:T(8,128)}) %reduce-scatter.5.cloned.1.call-update) | async-done | bytes 196624 | tf_op jit(solution)/shard_map/reduce_scatter | solution.py:120
  253.9 1.6 convert_element_type.88
  (43 shorter events, 4.6 us)
Async XLA Ops:
  6.5 16.6 %copy-start = (bf16[3072,256]{1,0:T(8,128)(2,1)S(1)}, bf16[3072,256]{1,0:T(8,128)(2,1)}, u32[]{:S(2)}) copy-start(bf16[3072,256]{1,0:T(8,128)(2,1)} %param.12) | copy-start | bytes 4718596
  6.5 53.9 %reduce-scatter.3.cloned.1.call-start = ((), (), s32[]{:S(2)}) async-start(), calls=%async_computation.6 | async-start | bytes 1146880 | tf_op jit(solution)/shard_map/reduce_scatter | solution.py:97
  25.3 9.2 %copy-start.2 = (s32[4]{0:T(128)S(1)}, s32[4]{0:T(128)}, u32[]{:S(2)}) copy-start(s32[4]{0:T(128)} %param.17) | copy-start | bytes 52
  25.3 41.3 %copy-start.3 = (s32[4]{0:T(128)S(1)}, s32[4]{0:T(128)}, u32[]{:S(2)}) copy-start(s32[4]{0:T(128)} %param.16) | copy-start | bytes 52
  33.4 57.4 %copy-start.1 = (bf16[4,128,1024]{2,1,0:T(8,128)(2,1)S(1)}, bf16[4,128,1024]{2,1,0:T(8,128)(2,1)}, u32[]{:S(2)}) copy-start(bf16[4,128,1024]{2,1,0:T(8,128)(2,1)} %param.14) | copy-start | bytes 3145732
  62.0 10.2 %all-to-all-start.1 = ((bf16[4,4,256]{2,1,0:T(4,128)(2,1)}), bf16[4,4,256]{2,1,0:T(4,128)(2,1)S(1)}, u32[]{:S(2)}, u32[]{:S(2)}) async-start(bf16[4,4,256]{2,1,0:T(4,128)(2,1)} %all_to_all.45), calls=%async_computation.2 | async-start | bytes 16384 | tf_op jit(solution)/shard_map/all_to_all | solution.py:103
  72.2 8.8 %all-to-all-start.2 = ((bf16[4,4,256]{2,1,0:T(4,128)(2,1)}), bf16[4,4,256]{2,1,0:T(4,128)(2,1)S(1)}, u32[]{:S(2)}, u32[]{:S(2)}) async-start(bf16[4,4,256]{2,1,0:T(4,128)(2,1)} %all_to_all.47), calls=%async_computation.3 | async-start | bytes 16384 | tf_op jit(solution)/shard_map/all_to_all | solution.py:104
  81.0 9.1 %all-to-all-start = ((bf16[4,4,3072]{2,1,0:T(4,128)(2,1)}), bf16[4,4,3072]{2,1,0:T(4,128)(2,1)S(1)}, u32[]{:S(2)}, u32[]{:S(2)}) async-start(bf16[4,4,3072]{2,1,0:T(4,128)(2,1)} %all_to_all.43), calls=%async_computation.1 | async-start | bytes 196608 | tf_op jit(solution)/shard_map/all_to_all | solution.py:102
  84.3 169.5 %reduce-scatter.5.cloned.1.call-start = ((), (), s32[]{:S(2)}) async-start(), calls=%async_computation.7 | async-start | bytes 983040 | tf_op jit(solution)/shard_map/reduce_scatter | solution.py:120
Sparse Core Ops, SparseCore 0:
  34.6 25.7 reduce-scatter.2
  233.2 20.5 reduce-scatter.4
where the time goes:
time: 263 us; the launch traced here: 262 us
  other arithmetic  73.1 us (28%)
  waiting for transfers between devices  61.7 us (23%)
  local copies, waits for them, and re-layouts  40.5 us (15%)
  blocking collectives  38.5 us (15%)
  matrix products  23.5 us (9%)
  between operations  13.7 us (5%)
  starting transfers between devices  11.3 us (4%)
    unnamed x1, other arithmetic  68.7 us
    reduce_scatter x1, waiting for transfers between devices, shards(): summed = lax.psum_scatter(partials, 'gy', scatter_dimension=0, tiled=True)  25.8 us
    reduce_scatter x1, waiting for transfers between devices, shards(): result = lax.psum_scatter(products, 'gy', scatter_dimension=0, tiled=True)  20.8 us
    all_gather x1, blocking collectives, shards(): piece = lax.all_gather(tokens, 'gx', axis=0, tiled=True)  16.6 us
    unnamed x11, local copies, waits for them, and re-layouts  16.4 us
    all_gather x1, blocking collectives, shards(): lax.all_gather(block_list, 'gx', axis=1, tiled=True)  15.2 us
    all_to_all x2, local copies, waits for them, and re-layouts, shards(): lax.all_to_all(context_window[None], 'gy', split_axis=2, concat_axis=0, t...  11.9 us
    dot_general x1, matrix products, shards(): jnp.einsum('jrd,de->jre', lax.all_gather(block_list, 'gx', axis=1, tiled=...  10.6 us
  transfers between devices with their start and end apart: 5, of which 5 were waited for; matrix products, arithmetic and copies ran while one was open for 0% of the time, Pallas kernels for 0%

commit v1 on v0

--- a/solution.py
+++ b/solution.py
@@ -1,15 +1,29 @@
+import functools
+
 import jax
 import jax.numpy as jnp
 from jax import lax
+from jax.experimental import pallas as pl
+from jax.experimental.pallas import tpu as pltpu
 from jax.sharding import PartitionSpec as P
 
 QUERY_HEADS = 96
 KEY_VALUE_HEADS = 8
 HEAD_WIDTH = 128
 CONTEXT_LENGTH = 128
+GROUP = QUERY_HEADS // KEY_VALUE_HEADS
 
 
 rope_theta = 1000000.0
+
+VMEM = pl.BlockSpec(memory_space=pltpu.VMEM)
+SMEM = pl.BlockSpec(memory_space=pltpu.SMEM)
+
+
+def rotary_angles(positions):
+    half_dim = HEAD_WIDTH // 2
+    frequency = rope_theta ** (-(jnp.arange(half_dim, dtype=jnp.float32) * 2.0) / HEAD_WIDTH)
+    return positions.astype(jnp.float32)[:, None] * frequency[None, :]
 
 
 def rotary_table(values, positions, heads):
@@ -17,8 +31,7 @@
     head_size = values.shape[1] // heads
     half_dim = head_size // 2
     wide = values.astype(jnp.float32).reshape(number_rows, heads, head_size)
-    frequency = rope_theta ** (-(jnp.arange(half_dim, dtype=jnp.float32) * 2.0) / head_size)
-    angles = positions.astype(jnp.float32)[:, None] * frequency[None, :]
+    angles = rotary_angles(positions)
     cosine = jnp.cos(angles)[:, None, :]
     sine = jnp.sin(angles)[:, None, :]
     lower_half = wide[..., :half_dim]
@@ -31,9 +44,8 @@
 
 def attend(rotated_query, rotated_key, fresh_value, device_keys, device_values, lengths):
     number_rows = rotated_query.shape[0]
-    group_size = QUERY_HEADS // KEY_VALUE_HEADS
     logit_scale = 1.0 / HEAD_WIDTH**0.5
-    per_head_queries = rotated_query.reshape(number_rows, KEY_VALUE_HEADS, group_size, HEAD_WIDTH)
+    per_head_queries = rotated_query.reshape(number_rows, KEY_VALUE_HEADS, GROUP, HEAD_WIDTH)
     per_head_keys = device_keys.reshape(number_rows, CONTEXT_LENGTH, KEY_VALUE_HEADS, HEAD_WIDTH)
     scores = (
         jnp.einsum(
@@ -72,7 +84,7 @@
     return context_window.reshape(number_rows, QUERY_HEADS * HEAD_WIDTH).astype(jnp.bfloat16)
 
 
-def shards(
+def general_shards(
     tokens,
     w_query,
     key_matrix,
@@ -121,6 +133,271 @@
     return result.astype(jnp.bfloat16)
 
 
+SIDE = 4
+ROWS = 4
+BLOCK = SIDE * ROWS
+SLOTS = 16
+OWNERS = (0, 2, 1, 3)
+
+
+def call(body, outs, args, specs, scratch=(), limit=8, flops=0, moved=0):
+    return pl.pallas_call(
+        body,
+        out_shape=outs,
+        in_specs=specs,
+        out_specs=jax.tree.map(lambda _: VMEM, outs),
+        scratch_shapes=list(scratch),
+        compiler_params=pltpu.CompilerParams(vmem_limit_bytes=limit << 20),
+        cost_estimate=pl.CostEstimate(flops=flops, bytes_accessed=moved, transcendentals=0),
+    )(*args)
+
+
+def partners(block, axis, distances=(3, 2, 1)):
+    got = {
+        k: lax.ppermute(block(k), axis, [(p, p ^ k) for p in range(SIDE)]) for k in distances
+    }
+    return [got[k] for k in (1, 2, 3)]
+
+
+def project_body(tile, x0, x1, x2, x3, wq, wk, wv, keep, send, rows):
+    m = lax.axis_index("gx") ^ lax.axis_index("gy")
+    for s, x in enumerate((x0, x1, x2, x3)):
+        d = s ^ m
+        place = ((d & 1) << 1) | (d >> 1)
+        rows[pl.ds(pl.multiple_of(place * BLOCK, BLOCK), BLOCK), :] = x[...]
+
+    def put(w, c, width, head):
+        acc = jnp.dot(rows[...], w[:, pl.ds(c, width)], preferred_element_type=jnp.float32)
+        for k in range(width // HEAD_WIDTH):
+            at = pl.ds(pl.multiple_of((head + k) * BLOCK, BLOCK), BLOCK)
+            part = acc[:, k * HEAD_WIDTH : (k + 1) * HEAD_WIDTH]
+            for b in range(2):
+                keep[b, at, :] = part[b * BLOCK : (b + 1) * BLOCK]
+                send[b, at, :] = part[(2 + b) * BLOCK : (3 + b) * BLOCK]
+
+    per = tile // HEAD_WIDTH
+
+    def step(n, _):
+        put(wq, pl.multiple_of(n * tile, tile), tile, n * per)
+        return 0
+
+    lax.fori_loop(0, wq.shape[1] // tile, step, 0)
+    qh, kh = wq.shape[1] // HEAD_WIDTH, wk.shape[1] // HEAD_WIDTH
+    put(wk, 0, wk.shape[1], qh)
+    put(wv, 0, wv.shape[1], qh + kh)
+
+
+def spread_body(groups, keep, got, across, out0, out1, out2, out3, slots):
+    j = lax.axis_index("gx")
+    qh = groups * GROUP
+    for g in range(groups):
+        for u in range(SLOTS):
+            if u < GROUP:
+                h = g * GROUP + u
+            elif u == GROUP:
+                h = qh + g
+            elif u == GROUP + 1:
+                h = qh + groups + g
+            else:
+                h = None
+            at = (g * SLOTS + u) * BLOCK
+            if h is None:
+                slots[at : at + BLOCK, :] = jnp.zeros((BLOCK, HEAD_WIDTH), jnp.float32)
+            else:
+                src = slice(h * BLOCK, (h + 1) * BLOCK)
+                total = (keep[0, src, :] + got[0, src, :]) + across[src, :]
+                slots[at : at + BLOCK, :] = total.astype(jnp.bfloat16).astype(jnp.float32)
+    wide = groups * SLOTS
+    for e, out in enumerate((out0, out1, out2, out3)):
+        for t in range(ROWS):
+            row = (j ^ e) * ROWS + t
+            out[t * wide : (t + 1) * wide, :] = slots[pl.ds(row, wide, stride=BLOCK), :].astype(
+                jnp.bfloat16
+            )
+
+
+def attend_body(
+    groups, lengths, a0, a1, a2, a3, cosine, sine, keys, values, c0, c1, c2, c3, held
+):
+    i, j = lax.axis_index("gy"), lax.axis_index("gx")
+    scale = 1.0 / HEAD_WIDTH**0.5
+    for e, a in enumerate((a0, a1, a2, a3)):
+        held[e] = a[...]
+    wide = groups * SLOTS
+    slot = lax.broadcasted_iota(jnp.int32, (wide, HEAD_WIDTH), 0) % SLOTS
+    is_value = slot == GROUP + 1
+    spot = lax.broadcasted_iota(jnp.int32, (SLOTS, CONTEXT_LENGTH), 1)
+    for f, c in enumerate((c0, c1, c2, c3)):
+        source = i ^ f
+        block = held.at[source ^ j]
+        for t in range(ROWS):
+            raw = block[t * wide : (t + 1) * wide, :].astype(jnp.float32)
+            turned = (
+                raw * cosine[t : t + 1, :]
+                + pltpu.roll(raw, HEAD_WIDTH // 2, 1) * sine[t : t + 1, :]
+            )
+            turned = jnp.where(is_value, raw, turned).astype(jnp.bfloat16)
+            live = spot < lengths[t]
+            for g in range(groups):
+                at = pl.ds(pl.multiple_of((source * groups + g) * HEAD_WIDTH, HEAD_WIDTH), HEAD_WIDTH)
+                q = turned[g * SLOTS : (g + 1) * SLOTS]
+                wide_q = q.astype(jnp.float32)
+                own_key = wide_q[GROUP : GROUP + 1]
+                own_value = wide_q[GROUP + 1 : GROUP + 2]
+                scores = lax.dot_general(
+                    q, keys[t, :, at], (((1,), (1,)), ((), ())), preferred_element_type=jnp.float32
+                )
+                scores = jnp.where(live, scores * scale, -jnp.inf)
+                own = jnp.sum(wide_q * own_key, axis=1, keepdims=True) * scale
+                top = jnp.maximum(jnp.max(scores, axis=1, keepdims=True), own)
+                cached = jnp.exp(scores - top)
+                own = jnp.exp(own - top)
+                total = jnp.sum(cached, axis=1, keepdims=True) + own
+                weights = (cached / total).astype(jnp.bfloat16)
+                own = (own / total).astype(jnp.bfloat16).astype(jnp.float32)
+                context = jnp.dot(weights, values[t, :, at], preferred_element_type=jnp.float32)
+                context = context + own * own_value
+                first = t * wide + g * SLOTS
+                c[first : first + SLOTS, :] = context.astype(jnp.bfloat16)
+
+
+def turn_body(groups, c0, c1, c2, c3, out, slots):
+    i = lax.axis_index("gy")
+    wide = groups * SLOTS
+    size = ROWS * wide
+    for f, c in enumerate((c0, c1, c2, c3)):
+        slots[pl.ds(pl.multiple_of((i ^ f) * size, size), size), :] = c[...].astype(jnp.float32)
+    for g in range(groups):
+        for u in range(GROUP):
+            h = g * GROUP + u
+            out[:, h * HEAD_WIDTH : (h + 1) * HEAD_WIDTH] = slots[
+                pl.ds(g * SLOTS + u, BLOCK, stride=wide), :
+            ].astype(jnp.bfloat16)
+
+
+def output_body(tile, x0, x1, x2, x3, w, keep, send, rows, ordered):
+    i, j = lax.axis_index("gy"), lax.axis_index("gx")
+    for s, x in enumerate((x0, x1, x2, x3)):
+        rows[pl.ds(pl.multiple_of((j ^ s) * BLOCK, BLOCK), BLOCK), :] = x[...]
+    count = SIDE * BLOCK
+    r = lax.broadcasted_iota(jnp.int32, (count, count), 0)
+    c = lax.broadcasted_iota(jnp.int32, (count, count), 1)
+    place = r >> 4
+    owner = i ^ (((place & 1) << 1) | (place >> 1))
+    wanted = ((r & 12) << 2) | (owner << 2) | (r & 3)
+    swap = jnp.where(c == wanted, 1.0, 0.0).astype(jnp.bfloat16)
+    ordered[...] = jnp.dot(swap, rows[...], preferred_element_type=jnp.float32).astype(
+        jnp.bfloat16
+    )
+
+    def step(n, _):
+        at = pl.ds(pl.multiple_of(n * tile, tile), tile)
+        acc = jnp.dot(ordered[...], w[:, at], preferred_element_type=jnp.float32)
+        keep[:, at] = acc[: 2 * BLOCK]
+        send[:, at] = acc[2 * BLOCK :]
+        return 0
+
+    lax.fori_loop(0, w.shape[1] // tile, step, 0)
+
+
+def square_shards(
+    tokens,
+    w_query,
+    key_matrix,
+    value_matrix,
+    w_output,
+    stored_keys,
+    stored_values,
+    lengths,
+    positions,
+):
+    f32, bf16 = jnp.float32, jnp.bfloat16
+    depth, q_width = w_query.shape
+    kv_width = key_matrix.shape[1]
+    groups = kv_width // HEAD_WIDTH
+    heads = (q_width + 2 * kv_width) // HEAD_WIDTH
+    wide = groups * SLOTS
+
+    angles = rotary_angles(positions)
+    cosine, sine = jnp.cos(angles), jnp.sin(angles)
+    cosine = jnp.concatenate([cosine, cosine], axis=1)
+    sine = jnp.concatenate([-sine, sine], axis=1)
+
+    near = partners(lambda k: tokens, "gx")
+    half = jax.ShapeDtypeStruct((2, heads * BLOCK, HEAD_WIDTH), f32)
+    tile = 512
+    keep, send = call(
+        functools.partial(project_body, tile),
+        [half, half],
+        (tokens, *near, w_query, key_matrix, value_matrix),
+        [VMEM] * 7,
+        [pltpu.VMEM((SIDE * BLOCK, depth), bf16)],
+        flops=2 * SIDE * BLOCK * depth * heads * HEAD_WIDTH,
+        moved=2 * depth * heads * HEAD_WIDTH,
+    )
+    got = lax.ppermute(send, "gy", [(p, p ^ 1) for p in range(SIDE)])
+    across = lax.ppermute(keep[1] + got[1], "gy", [(p, p ^ 2) for p in range(SIDE)])
+    piece = jax.ShapeDtypeStruct((ROWS * wide, HEAD_WIDTH), bf16)
+    mine = call(
+        functools.partial(spread_body, groups),
+        [piece] * SIDE,
+        (keep, got, across),
+        [VMEM] * 3,
+        [pltpu.VMEM((wide * BLOCK, HEAD_WIDTH), f32)],
+    )
+    others = partners(lambda k: mine[k], "gx")
+    context = call(
+        functools.partial(attend_body, groups),
+        [piece] * SIDE,
+        (lengths, mine[0], *others, cosine, sine, stored_keys, stored_values),
+        [SMEM] + [VMEM] * 8,
+        [pltpu.VMEM((SIDE, ROWS * wide, HEAD_WIDTH), bf16)],
+    )
+    others = partners(lambda k: context[k], "gy", (2, 3, 1))
+    rows = call(
+        functools.partial(turn_body, groups),
+        jax.ShapeDtypeStruct((BLOCK, groups * GROUP * HEAD_WIDTH), bf16),
+        (context[0], *others),
+        [VMEM] * 4,
+        [pltpu.VMEM((SIDE * ROWS * wide, HEAD_WIDTH), f32)],
+    )
+    near = partners(lambda k: rows, "gx")
+    depth, out_width = w_output.shape
+    half = jax.ShapeDtypeStruct((2 * BLOCK, out_width), f32)
+    keep, send = call(
+        functools.partial(output_body, tile),
+        [half, half],
+        (rows, *near, w_output),
+        [VMEM] * 5,
+        [pltpu.VMEM((SIDE * BLOCK, depth), bf16)] * 2,
+        flops=2 * SIDE * BLOCK * depth * out_width,
+        moved=2 * depth * out_width,
+    )
+    got = lax.ppermute(send, "gy", [(p, p ^ 1) for p in range(SIDE)])
+    across = lax.ppermute(
+        keep[BLOCK:] + got[BLOCK:], "gy", [(p, p ^ 2) for p in range(SIDE)]
+    )
+    return ((keep[:BLOCK] + got[:BLOCK]) + across).astype(bf16)
+
+
+def shards(*args):
+    tokens, w_query, key_matrix, _, w_output, stored_keys, _, lengths, _ = args
+    whole_heads = w_query.shape[1] % (GROUP * HEAD_WIDTH) == 0
+    groups = key_matrix.shape[1] // HEAD_WIDTH
+    square = (
+        lax.axis_size("gx") == SIDE
+        and lax.axis_size("gy") == SIDE
+        and lengths.shape[0] == ROWS
+        and tokens.shape[0] == BLOCK
+        and whole_heads
+        and groups * HEAD_WIDTH == key_matrix.shape[1]
+        and groups * GROUP * HEAD_WIDTH == w_query.shape[1] == w_output.shape[0]
+        and w_output.shape[1] % 512 == 0
+        and w_query.shape[1] % 512 == 0
+    )
+    return square_shards(*args) if square else general_shards(*args)
+
+
 def solution(mesh):
     in_specs = (
         P(("parts", "gx"), "gy"),

time: 263 us -> 87.9 us (0.33)
  other arithmetic: 73.1 us -> 0.93 us
  blocking collectives: 38.5 us -> 0 us
  local copies, waits for them, and re-layouts: 40.5 us -> 10.1 us
  waiting for transfers between devices: 61.7 us -> 37.4 us
  matrix products: 23.5 us -> 0 us
  Pallas kernels: 0 us -> 20.1 us
  between operations: 13.7 us -> 0.09 us
  starting transfers between devices: 11.3 us -> 19.1 us
    unnamed x1 -> x0, other arithmetic: 68.7 us -> none
    reduce_scatter x2 -> x0, waiting for transfers between devices: 46.6 us -> none  [the longest x1 25.8 us: shards(): summed = lax.psum_scatter(partials, 'gy', scatter_dimension=0, tiled=True)]
    ppermute x0 -> x16, waiting for transfers between devices: none -> 37.4 us  [the longest x12 21.8 us: partners(): lax.ppermute(block(k), axis, [(p, p ^ k) for p in range(SIDE)])]
    all_gather x2 -> x0, blocking collectives: 31.8 us -> none  [the longest x1 16.6 us: shards(): piece = lax.all_gather(tokens, 'gx', axis=0, tiled=True)]
    dot_general x7 -> x0, matrix products: 23.5 us -> none  [the longest x1 10.6 us: shards(): jnp.einsum('jrd,de->jre', lax.all_gather(block_list, 'gx', axis=1, tiled=...]
    pallas_call x0 -> x5, Pallas kernels: none -> 20.1 us  [call(): pl.pallas_call(body, out_shape=outs, in_specs=specs, out_specs=jax.tree.m...]
    ppermute x0 -> x16, starting transfers between devices: none -> 19.1 us  [the longest x12 16.4 us: partners(): lax.ppermute(block(k), axis, [(p, p ^ k) for p in range(SIDE)])]
    all_to_all x3 -> x0, waiting for transfers between devices: 15.1 us -> none  [the longest x1 5.45 us: shards(): lax.all_to_all(query, 'gx', split_axis=0, concat_axis=1, tiled=True)]
  transfers between devices with their start and end apart: 5 -> 16, of which waited for: 5 -> 12; matrix products, arithmetic and copies ran while one was open for 0% -> 0% of each run, Pallas kernels for 0% -> 0%
where the time goes in v1:
time: 87.9 us; the launch traced here: 87.7 us
  waiting for transfers between devices  37.4 us (43%)
  Pallas kernels  20.1 us (23%)
  starting transfers between devices  19.1 us (22%)
  local copies, waits for them, and re-layouts  10.1 us (11%)
  other arithmetic  0.93 us (1%)
    ppermute x12, waiting for transfers between devices, partners(): lax.ppermute(block(k), axis, [(p, p ^ k) for p in range(SIDE)])  21.8 us
    pallas_call x5, Pallas kernels, call(): pl.pallas_call(body, out_shape=outs, in_specs=specs, out_specs=jax.tree.m...  20.1 us
    ppermute x12, starting transfers between devices, partners(): lax.ppermute(block(k), axis, [(p, p ^ k) for p in range(SIDE)])  16.4 us
    unnamed x18, local copies, waits for them, and re-layouts  10.1 us
    ppermute x1, waiting for transfers between devices, square_shards(): lax.ppermute(keep[BLOCK:] + got[BLOCK:], 'gy', [(p, p ^ 2) for p in range...  6.04 us
    ppermute x1, waiting for transfers between devices, square_shards(): lax.ppermute(keep[1] + got[1], 'gy', [(p, p ^ 2) for p in range(SIDE)])  6.02 us
    ppermute x2, waiting for transfers between devices, square_shards(): got = lax.ppermute(send, 'gy', [(p, p ^ 1) for p in range(SIDE)])  3.51 us
  transfers between devices with their start and end apart: 16, of which 12 were waited for; matrix products, arithmetic and copies ran while one was open for 0% of the time, Pallas kernels for 0%

profile of v1, /device:TPU:0, one launch (start us, length us, event | category | flops | bytes accessed | tf_op | source)
XLA Modules:
  0.0 87.7 jit_solution(14209069198304509978)
XLA Ops:
  0.0 3.0 %collective-permute-start = (bf16[16,3072]{1,0:T(8,128)(2,1)}, bf16[16,3072]{1,0:T(8,128)(2,1)S(1)}, u32[]{:S(2)}, u32[]{:S(2)}) collective-permute-start(bf16[16,3072]{1,0:T(8,128)(2,1)} %x0.1), channel_id=1, source_target_pairs={{0,4},{4,0},{8,12},{12,8},{1,5},{5,1},{9,13},{13,9},{2,6},{6,2},{1... | collective-permute-start | bytes 294920 | tf_op jit(solution)/shard_map/ppermute | solution.py:157
  3.0 2.6 %collective-permute-start.1 = (bf16[16,3072]{1,0:T(8,128)(2,1)}, bf16[16,3072]{1,0:T(8,128)(2,1)S(1)}, u32[]{:S(2)}, u32[]{:S(2)}) collective-permute-start(bf16[16,3072]{1,0:T(8,128)(2,1)} %x0.1), channel_id=1, source_target_pairs={{0,8},{4,12},{8,0},{12,4},{1,9},{5,13},{9,1},{13,5},{2,10},{6,14},... | collective-permute-start | bytes 294920 | tf_op jit(solution)/shard_map/ppermute | solution.py:157
  6.0 7.6 %collective-permute-done.1.x2 = bf16[16,3072]{1,0:T(8,128)(2,1)S(1)} collective-permute-done((bf16[16,3072]{1,0:T(8,128)(2,1)}, bf16[16,3072]{1,0:T(8,128)(2,1)S(1)}, u32[]{:S(2)}, u32[]{:S(2)}) %collective-permute-start.1) | collective-permute-done | bytes 98336 | tf_op jit(solution)/shard_map/ppermute | solution.py:157
  13.7 6.4 %copy-done.1 = bf16[3072,3072]{1,0:T(8,128)(2,1)S(1)} copy-done((bf16[3072,3072]{1,0:T(8,128)(2,1)S(1)}, bf16[3072,3072]{1,0:T(8,128)(2,1)}, u32[]{:S(2)}) %copy-start.1) | copy-done | bytes 18874392
  20.1 1.4 %copy-done.2 = bf16[3072,256]{1,0:T(8,128)(2,1)S(1)} copy-done((bf16[3072,256]{1,0:T(8,128)(2,1)S(1)}, bf16[3072,256]{1,0:T(8,128)(2,1)}, u32[]{:S(2)}) %copy-start.2) | copy-done | bytes 1572888
  21.5 1.4 %copy-done.3 = bf16[3072,256]{1,0:T(8,128)(2,1)S(1)} copy-done((bf16[3072,256]{1,0:T(8,128)(2,1)S(1)}, bf16[3072,256]{1,0:T(8,128)(2,1)}, u32[]{:S(2)}) %copy-start.3) | copy-done | bytes 1572888
  23.8 4.7 %shard_map.91 = (f32[2,448,128]{2,1,0:T(8,128)S(1)}, f32[2,448,128]{2,1,0:T(8,128)S(1)}) custom-call(bf16[16,3072]{1,0:T(8,128)(2,1)S(1)} %copy-done.6, bf16[16,3072]{1,0:T(8,128)(2,1)S(1)} %collective-permute-done.x1, bf16[16,3072]{1,0:T(8,128)(2,1)S(1)} %collective-permute-done.1.x2, bf16[16,3072]{1,0:T(8,128)(2,1)S(1)} %collective-permute-done.2.x3, ...), custom_call_target="tpu_custom_call" | custom-call | flops 1409286144 | bytes 22020096 | tf_op jit(solution)/shard_map/pallas_call | solution.py:144
  28.5 1.8 %collective-permute-done.3.got = f32[2,448,128]{2,1,0:T(8,128)S(1)} collective-permute-done((f32[2,448,128]{2,1,0:T(8,128)S(1)}, f32[2,448,128]{2,1,0:T(8,128)S(1)}, u32[]{:S(2)}, u32[]{:S(2)}) %collective-permute-start.3) | collective-permute-done | bytes 458784 | tf_op jit(solution)/shard_map/ppermute | solution.py:338
  30.4 1.6 %collective-permute-start.4 = (f32[448,128]{1,0:T(8,128)S(1)}, f32[448,128]{1,0:T(8,128)S(1)}, u32[]{:S(2)}, u32[]{:S(2)}) collective-permute-start(f32[448,128]{1,0:T(8,128)S(1)} %fusion), channel_id=1, source_target_pairs={{0,2},{1,3},{2,0},{3,1},{4,6},{5,7},{6,4},{7,5},{8,10},{9,11},{10,... | collective-permute-start | bytes 688136 | tf_op jit(solution)/shard_map/ppermute | solution.py:339
  32.0 6.0 %collective-permute-done.4.across = f32[448,128]{1,0:T(8,128)S(1)} collective-permute-done((f32[448,128]{1,0:T(8,128)S(1)}, f32[448,128]{1,0:T(8,128)S(1)}, u32[]{:S(2)}, u32[]{:S(2)}) %collective-permute-start.4) | collective-permute-done | bytes 229408 | tf_op jit(solution)/shard_map/ppermute | solution.py:339
  38.2 1.7 %collective-permute-start.5 = (bf16[128,128]{1,0:T(8,128)(2,1)S(1)}, bf16[128,128]{1,0:T(8,128)(2,1)S(1)}, u32[]{:S(2)}, u32[]{:S(2)}) collective-permute-start(bf16[128,128]{1,0:T(8,128)(2,1)S(1)} %get-tuple-element.20), channel_id=1, source_target_pairs={{0,4},{4,0},{8,12},{12,8},{1,5},{5,1},{9,13},{13,9},{2,6},{6,2},{1... | collective-permute-start | bytes 98312 | tf_op jit(solution)/shard_map/ppermute | solution.py:157
  39.9 1.4 %collective-permute-start.6 = (bf16[128,128]{1,0:T(8,128)(2,1)S(1)}, bf16[128,128]{1,0:T(8,128)(2,1)S(1)}, u32[]{:S(2)}, u32[]{:S(2)}) collective-permute-start(bf16[128,128]{1,0:T(8,128)(2,1)S(1)} %get-tuple-element.21), channel_id=1, source_target_pairs={{0,8},{4,12},{8,0},{12,4},{1,9},{5,13},{9,1},{13,5},{2,10},{6,14},... | collective-permute-start | bytes 98312 | tf_op jit(solution)/shard_map/ppermute | solution.py:157
  42.7 2.5 %collective-permute-done.6.a2 = bf16[128,128]{1,0:T(8,128)(2,1)S(1)} collective-permute-done((bf16[128,128]{1,0:T(8,128)(2,1)S(1)}, bf16[128,128]{1,0:T(8,128)(2,1)S(1)}, u32[]{:S(2)}, u32[]{:S(2)}) %collective-permute-start.6) | collective-permute-done | bytes 32800 | tf_op jit(solution)/shard_map/ppermute | solution.py:157
  45.3 1.7 %collective-permute-done.7.a3 = bf16[128,128]{1,0:T(8,128)(2,1)S(1)} collective-permute-done((bf16[128,128]{1,0:T(8,128)(2,1)S(1)}, bf16[128,128]{1,0:T(8,128)(2,1)S(1)}, u32[]{:S(2)}, u32[]{:S(2)}) %collective-permute-start.7) | collective-permute-done | bytes 32800 | tf_op jit(solution)/shard_map/ppermute | solution.py:157
  47.0 10.9 %shard_map.93 = (bf16[128,128]{1,0:T(8,128)(2,1)S(1)}, bf16[128,128]{1,0:T(8,128)(2,1)S(1)}, bf16[128,128]{1,0:T(8,128)(2,1)S(1)}, bf16[128,128]{1,0:T(8,128)(2,1)S(1)}) custom-call(s32[4]{0:T(128)S(1)} %copy-done.7, bf16[128,128]{1,0:T(8,128)(2,1)S(1)} %get-tuple-element.19.a0, bf16[128,128]{1,0:T(8,128)(2,1)S(1)} %collective-permute-done.5.a1, ...), custom_call_target="tpu_custom_call" | custom-call | tf_op jit(solution)/shard_map/pallas_call | solution.py:144
  57.9 1.5 %collective-permute-start.9 = (bf16[128,128]{1,0:T(8,128)(2,1)S(1)}, bf16[128,128]{1,0:T(8,128)(2,1)S(1)}, u32[]{:S(2)}, u32[]{:S(2)}) collective-permute-start(bf16[128,128]{1,0:T(8,128)(2,1)S(1)} %get-tuple-element.25), channel_id=1, source_target_pairs={{0,2},{1,3},{2,0},{3,1},{4,6},{5,7},{6,4},{7,5},{8,10},{9,11},{10,... | collective-permute-start | bytes 98312 | tf_op jit(solution)/shard_map/ppermute | solution.py:157
  59.8 2.1 %collective-permute-done.9.c2 = bf16[128,128]{1,0:T(8,128)(2,1)S(1)} collective-permute-done((bf16[128,128]{1,0:T(8,128)(2,1)S(1)}, bf16[128,128]{1,0:T(8,128)(2,1)S(1)}, u32[]{:S(2)}, u32[]{:S(2)}) %collective-permute-start.9) | collective-permute-done | bytes 32800 | tf_op jit(solution)/shard_map/ppermute | solution.py:157
  63.0 1.9 %collective-permute-start.12 = (bf16[16,3072]{1,0:T(8,128)(2,1)S(1)}, bf16[16,3072]{1,0:T(8,128)(2,1)S(1)}, u32[]{:S(2)}, u32[]{:S(2)}) collective-permute-start(bf16[16,3072]{1,0:T(8,128)(2,1)S(1)} %shard_map.94.x0), channel_id=1, source_target_pairs={{0,8},{4,12},{8,0},{12,4},{1,9},{5,13},{9,1},{13,5},{2,10},{6,14},... | collective-permute-start | bytes 294920 | tf_op jit(solution)/shard_map/ppermute | solution.py:157
  64.9 2.5 %collective-permute-start.13 = (bf16[16,3072]{1,0:T(8,128)(2,1)S(1)}, bf16[16,3072]{1,0:T(8,128)(2,1)S(1)}, u32[]{:S(2)}, u32[]{:S(2)}) collective-permute-start(bf16[16,3072]{1,0:T(8,128)(2,1)S(1)} %shard_map.94.x0), channel_id=1, source_target_pairs={{0,12},{4,8},{8,4},{12,0},{1,13},{5,9},{9,5},{13,1},{2,14},{6,10},... | collective-permute-start | bytes 294920 | tf_op jit(solution)/shard_map/ppermute | solution.py:157
  67.4 1.7 %collective-permute-done.11.x1 = bf16[16,3072]{1,0:T(8,128)(2,1)S(1)} collective-permute-done((bf16[16,3072]{1,0:T(8,128)(2,1)S(1)}, bf16[16,3072]{1,0:T(8,128)(2,1)S(1)}, u32[]{:S(2)}, u32[]{:S(2)}) %collective-permute-start.11) | collective-permute-done | bytes 98336 | tf_op jit(solution)/shard_map/ppermute | solution.py:157
  69.0 4.8 %collective-permute-done.12.x2 = bf16[16,3072]{1,0:T(8,128)(2,1)S(1)} collective-permute-done((bf16[16,3072]{1,0:T(8,128)(2,1)S(1)}, bf16[16,3072]{1,0:T(8,128)(2,1)S(1)}, u32[]{:S(2)}, u32[]{:S(2)}) %collective-permute-start.12) | collective-permute-done | bytes 98336 | tf_op jit(solution)/shard_map/ppermute | solution.py:157
  73.9 4.3 %shard_map.95 = (f32[32,3072]{1,0:T(8,128)S(1)}, f32[32,3072]{1,0:T(8,128)S(1)}) custom-call(bf16[16,3072]{1,0:T(8,128)(2,1)S(1)} %shard_map.94.x0, bf16[16,3072]{1,0:T(8,128)(2,1)S(1)} %collective-permute-done.11.x1, bf16[16,3072]{1,0:T(8,128)(2,1)S(1)} %collective-permute-done.12.x2, bf16[16,3072]{1,0:T(8,128)(2,1)S(1)} %collective-permute-done.13.x3, ...), custom_call_target="tpu_custom_call" | custom-call | flops 1207959552 | bytes 18874368 | tf_op jit(solution)/shard_map/pallas_call | solution.py:144
  78.2 1.7 %collective-permute-done.14 = f32[32,3072]{1,0:T(8,128)S(1)} collective-permute-done((f32[32,3072]{1,0:T(8,128)S(1)}, f32[32,3072]{1,0:T(8,128)S(1)}, u32[]{:S(2)}, u32[]{:S(2)}) %collective-permute-start.14) | collective-permute-done | bytes 393248 | tf_op jit(solution)/shard_map/ppermute | solution.py:376
  80.9 6.0 %collective-permute-done.15 = f32[16,3072]{1,0:T(8,128)S(1)} collective-permute-done((f32[16,3072]{1,0:T(8,128)S(1)}, f32[16,3072]{1,0:T(8,128)S(1)}, u32[]{:S(2)}, u32[]{:S(2)}) %collective-permute-start.15) | collective-permute-done | bytes 196640 | tf_op jit(solution)/shard_map/ppermute | solution.py:377
  (38 shorter events, 6.4 us)
Async XLA Ops:
  0.0 73.9 %copy-start = (bf16[3072,3072]{1,0:T(8,128)(2,1)S(1)}, bf16[3072,3072]{1,0:T(8,128)(2,1)}, u32[]{:S(2)}) copy-start(bf16[3072,3072]{1,0:T(8,128)(2,1)} %w.1) | copy-start | bytes 56623108
  0.0 6.0 %collective-permute-start = (bf16[16,3072]{1,0:T(8,128)(2,1)}, bf16[16,3072]{1,0:T(8,128)(2,1)S(1)}, u32[]{:S(2)}, u32[]{:S(2)}) collective-permute-start(bf16[16,3072]{1,0:T(8,128)(2,1)} %x0.1), channel_id=1, source_target_pairs={{0,4},{4,0},{8,12},{12,8},{1,5},{5,1},{9,13},{13,9},{2,6},{6,2},{1... | collective-permute-start | bytes 294920 | tf_op jit(solution)/shard_map/ppermute | solution.py:157
  3.0 10.6 %collective-permute-start.1 = (bf16[16,3072]{1,0:T(8,128)(2,1)}, bf16[16,3072]{1,0:T(8,128)(2,1)S(1)}, u32[]{:S(2)}, u32[]{:S(2)}) collective-permute-start(bf16[16,3072]{1,0:T(8,128)(2,1)} %x0.1), channel_id=1, source_target_pairs={{0,8},{4,12},{8,0},{12,4},{1,9},{5,13},{9,1},{13,5},{2,10},{6,14},... | collective-permute-start | bytes 294920 | tf_op jit(solution)/shard_map/ppermute | solution.py:157
  5.6 8.1 %collective-permute-start.2 = (bf16[16,3072]{1,0:T(8,128)(2,1)}, bf16[16,3072]{1,0:T(8,128)(2,1)S(1)}, u32[]{:S(2)}, u32[]{:S(2)}) collective-permute-start(bf16[16,3072]{1,0:T(8,128)(2,1)} %x0.1), channel_id=1, source_target_pairs={{0,12},{4,8},{8,4},{12,0},{1,13},{5,9},{9,5},{13,1},{2,14},{6,10},... | collective-permute-start | bytes 294920 | tf_op jit(solution)/shard_map/ppermute | solution.py:157
  13.7 6.4 %copy-start.1 = (bf16[3072,3072]{1,0:T(8,128)(2,1)S(1)}, bf16[3072,3072]{1,0:T(8,128)(2,1)}, u32[]{:S(2)}) copy-start(bf16[3072,3072]{1,0:T(8,128)(2,1)} %wq.1) | copy-start | bytes 56623108
  20.0 1.4 %copy-start.2 = (bf16[3072,256]{1,0:T(8,128)(2,1)S(1)}, bf16[3072,256]{1,0:T(8,128)(2,1)}, u32[]{:S(2)}) copy-start(bf16[3072,256]{1,0:T(8,128)(2,1)} %wk.1) | copy-start | bytes 4718596
  21.5 1.4 %copy-start.3 = (bf16[3072,256]{1,0:T(8,128)(2,1)S(1)}, bf16[3072,256]{1,0:T(8,128)(2,1)}, u32[]{:S(2)}) copy-start(bf16[3072,256]{1,0:T(8,128)(2,1)} %wv.1) | copy-start | bytes 4718596
  23.8 8.2 %copy-start.8 = (s32[4]{0:T(128)S(1)}, s32[4]{0:T(128)}, u32[]{:S(2)}) copy-start(s32[4]{0:T(128)} %param.17) | copy-start | bytes 52
  23.8 23.2 %copy-start.4 = (bf16[4,128,1024]{2,1,0:T(8,128)(2,1)S(1)}, bf16[4,128,1024]{2,1,0:T(8,128)(2,1)}, u32[]{:S(2)}) copy-start(bf16[4,128,1024]{2,1,0:T(8,128)(2,1)} %keys.1) | copy-start | bytes 3145732
  23.8 23.2 %copy-start.5 = (bf16[4,128,1024]{2,1,0:T(8,128)(2,1)S(1)}, bf16[4,128,1024]{2,1,0:T(8,128)(2,1)}, u32[]{:S(2)}) copy-start(bf16[4,128,1024]{2,1,0:T(8,128)(2,1)} %values.1) | copy-start | bytes 3145732
  23.8 23.2 %copy-start.7 = (s32[4]{0:T(128)S(1)}, s32[4]{0:T(128)}, u32[]{:S(2)}) copy-start(s32[4]{0:T(128)} %lengths.1) | copy-start | bytes 52
  28.4 1.9 %collective-permute-start.3 = (f32[2,448,128]{2,1,0:T(8,128)S(1)}, f32[2,448,128]{2,1,0:T(8,128)S(1)}, u32[]{:S(2)}, u32[]{:S(2)}) collective-permute-start(f32[2,448,128]{2,1,0:T(8,128)S(1)} %get-tuple-element.18), channel_id=1, source_target_pairs={{0,1},{1,0},{2,3},{3,2},{4,5},{5,4},{6,7},{7,6},{8,9},{9,8},{10,11... | collective-permute-start | bytes 1376264 | tf_op jit(solution)/shard_map/ppermute | solution.py:338
  30.4 7.7 %collective-permute-start.4 = (f32[448,128]{1,0:T(8,128)S(1)}, f32[448,128]{1,0:T(8,128)S(1)}, u32[]{:S(2)}, u32[]{:S(2)}) collective-permute-start(f32[448,128]{1,0:T(8,128)S(1)} %fusion), channel_id=1, source_target_pairs={{0,2},{1,3},{2,0},{3,1},{4,6},{5,7},{6,4},{7,5},{8,10},{9,11},{10,... | collective-permute-start | bytes 688136 | tf_op jit(solution)/shard_map/ppermute | solution.py:339
  38.2 4.5 %collective-permute-start.5 = (bf16[128,128]{1,0:T(8,128)(2,1)S(1)}, bf16[128,128]{1,0:T(8,128)(2,1)S(1)}, u32[]{:S(2)}, u32[]{:S(2)}) collective-permute-start(bf16[128,128]{1,0:T(8,128)(2,1)S(1)} %get-tuple-element.20), channel_id=1, source_target_pairs={{0,4},{4,0},{8,12},{12,8},{1,5},{5,1},{9,13},{13,9},{2,6},{6,2},{1... | collective-permute-start | bytes 98312 | tf_op jit(solution)/shard_map/ppermute | solution.py:157
  39.9 5.4 %collective-permute-start.6 = (bf16[128,128]{1,0:T(8,128)(2,1)S(1)}, bf16[128,128]{1,0:T(8,128)(2,1)S(1)}, u32[]{:S(2)}, u32[]{:S(2)}) collective-permute-start(bf16[128,128]{1,0:T(8,128)(2,1)S(1)} %get-tuple-element.21), channel_id=1, source_target_pairs={{0,8},{4,12},{8,0},{12,4},{1,9},{5,13},{9,1},{13,5},{2,10},{6,14},... | collective-permute-start | bytes 98312 | tf_op jit(solution)/shard_map/ppermute | solution.py:157
  41.3 5.7 %collective-permute-start.7 = (bf16[128,128]{1,0:T(8,128)(2,1)S(1)}, bf16[128,128]{1,0:T(8,128)(2,1)S(1)}, u32[]{:S(2)}, u32[]{:S(2)}) collective-permute-start(bf16[128,128]{1,0:T(8,128)(2,1)S(1)} %get-tuple-element.22), channel_id=1, source_target_pairs={{0,12},{4,8},{8,4},{12,0},{1,13},{5,9},{9,5},{13,1},{2,14},{6,10},... | collective-permute-start | bytes 98312 | tf_op jit(solution)/shard_map/ppermute | solution.py:157
  57.9 1.9 %collective-permute-start.8 = (bf16[128,128]{1,0:T(8,128)(2,1)S(1)}, bf16[128,128]{1,0:T(8,128)(2,1)S(1)}, u32[]{:S(2)}, u32[]{:S(2)}) collective-permute-start(bf16[128,128]{1,0:T(8,128)(2,1)S(1)} %get-tuple-element.24), channel_id=1, source_target_pairs={{0,1},{1,0},{2,3},{3,2},{4,5},{5,4},{6,7},{7,6},{8,9},{9,8},{10,11... | collective-permute-start | bytes 98312 | tf_op jit(solution)/shard_map/ppermute | solution.py:157
  57.9 4.0 %collective-permute-start.9 = (bf16[128,128]{1,0:T(8,128)(2,1)S(1)}, bf16[128,128]{1,0:T(8,128)(2,1)S(1)}, u32[]{:S(2)}, u32[]{:S(2)}) collective-permute-start(bf16[128,128]{1,0:T(8,128)(2,1)S(1)} %get-tuple-element.25), channel_id=1, source_target_pairs={{0,2},{1,3},{2,0},{3,1},{4,6},{5,7},{6,4},{7,5},{8,10},{9,11},{10,... | collective-permute-start | bytes 98312 | tf_op jit(solution)/shard_map/ppermute | solution.py:157
  59.4 3.3 %collective-permute-start.10 = (bf16[128,128]{1,0:T(8,128)(2,1)S(1)}, bf16[128,128]{1,0:T(8,128)(2,1)S(1)}, u32[]{:S(2)}, u32[]{:S(2)}) collective-permute-start(bf16[128,128]{1,0:T(8,128)(2,1)S(1)} %get-tuple-element.26), channel_id=1, source_target_pairs={{0,3},{1,2},{2,1},{3,0},{4,7},{5,6},{6,5},{7,4},{8,11},{9,10},{10,... | collective-permute-start | bytes 98312 | tf_op jit(solution)/shard_map/ppermute | solution.py:157
  62.9 6.1 %collective-permute-start.11 = (bf16[16,3072]{1,0:T(8,128)(2,1)S(1)}, bf16[16,3072]{1,0:T(8,128)(2,1)S(1)}, u32[]{:S(2)}, u32[]{:S(2)}) collective-permute-start(bf16[16,3072]{1,0:T(8,128)(2,1)S(1)} %shard_map.94.x0), channel_id=1, source_target_pairs={{0,4},{4,0},{8,12},{12,8},{1,5},{5,1},{9,13},{13,9},{2,6},{6,2},{1... | collective-permute-start | bytes 294920 | tf_op jit(solution)/shard_map/ppermute | solution.py:157
  63.0 10.9 %collective-permute-start.12 = (bf16[16,3072]{1,0:T(8,128)(2,1)S(1)}, bf16[16,3072]{1,0:T(8,128)(2,1)S(1)}, u32[]{:S(2)}, u32[]{:S(2)}) collective-permute-start(bf16[16,3072]{1,0:T(8,128)(2,1)S(1)} %shard_map.94.x0), channel_id=1, source_target_pairs={{0,8},{4,12},{8,0},{12,4},{1,9},{5,13},{9,1},{13,5},{2,10},{6,14},... | collective-permute-start | bytes 294920 | tf_op jit(solution)/shard_map/ppermute | solution.py:157
  64.9 8.9 %collective-permute-start.13 = (bf16[16,3072]{1,0:T(8,128)(2,1)S(1)}, bf16[16,3072]{1,0:T(8,128)(2,1)S(1)}, u32[]{:S(2)}, u32[]{:S(2)}) collective-permute-start(bf16[16,3072]{1,0:T(8,128)(2,1)S(1)} %shard_map.94.x0), channel_id=1, source_target_pairs={{0,12},{4,8},{8,4},{12,0},{1,13},{5,9},{9,5},{13,1},{2,14},{6,10},... | collective-permute-start | bytes 294920 | tf_op jit(solution)/shard_map/ppermute | solution.py:157
  78.2 1.8 %collective-permute-start.14 = (f32[32,3072]{1,0:T(8,128)S(1)}, f32[32,3072]{1,0:T(8,128)S(1)}, u32[]{:S(2)}, u32[]{:S(2)}) collective-permute-start(f32[32,3072]{1,0:T(8,128)S(1)} %get-tuple-element.28), channel_id=1, source_target_pairs={{0,1},{1,0},{2,3},{3,2},{4,5},{5,4},{6,7},{7,6},{8,9},{9,8},{10,11... | collective-permute-start | bytes 1179656 | tf_op jit(solution)/shard_map/ppermute | solution.py:376
  80.0 7.0 %collective-permute-start.15 = (f32[16,3072]{1,0:T(8,128)S(1)}, f32[16,3072]{1,0:T(8,128)S(1)}, u32[]{:S(2)}, u32[]{:S(2)}) collective-permute-start(f32[16,3072]{1,0:T(8,128)S(1)} %slice_add_fusion.1), channel_id=1, source_target_pairs={{0,2},{1,3},{2,0},{3,1},{4,6},{5,7},{6,4},{7,5},{8,10},{9,11},{10,... | collective-permute-start | bytes 589832 | tf_op jit(solution)/shard_map/ppermute | solution.py:377
  (1 other events, 0.9 us)

commit v2 on v1

--- a/solution.py
+++ b/solution.py
@@ -1,4 +1,5 @@
 import functools
+import math
 
 import jax
 import jax.numpy as jnp
@@ -137,7 +138,7 @@
 ROWS = 4
 BLOCK = SIDE * ROWS
 SLOTS = 16
-OWNERS = (0, 2, 1, 3)
+FROM = (0, 3, 1, 2)
 
 
 def call(body, outs, args, specs, scratch=(), limit=8, flops=0, moved=0):
@@ -152,16 +153,58 @@
     )(*args)
 
 
-def partners(block, axis, distances=(3, 2, 1)):
-    got = {
-        k: lax.ppermute(block(k), axis, [(p, p ^ k) for p in range(SIDE)]) for k in distances
-    }
-    return [got[k] for k in (1, 2, 3)]
-
-
-def project_body(tile, x0, x1, x2, x3, wq, wk, wv, keep, send, rows):
+def fetch_body(parts, *refs):
+    sems, done = refs[-1], refs[-2]
+    targets = refs[-2 - len(parts) : -2]
+    copies = []
+    for n, (source, index, pieces) in enumerate(parts):
+        size = refs[source].shape[0] // pieces
+        for k in range(pieces):
+            at = pl.ds(k * size, size)
+            copies.append(
+                pltpu.make_async_copy(
+                    refs[source].at[(at, *index)], targets[n].at[at], sems.at[len(copies)]
+                )
+            )
+    for copy in copies:
+        copy.start()
+    done[...] = jnp.zeros_like(done)
+    for copy in copies:
+        copy.wait()
+
+
+def fetch(parts, *after):
+    sources, plan, outs = [], [], []
+    for array, *columns in parts:
+        if not any(array is s for s in sources):
+            sources.append(array)
+        at = next(n for n, s in enumerate(sources) if s is array)
+        index = (slice(None), pl.ds(*columns)) if columns else ()
+        shape = (array.shape[0], columns[1]) if columns else array.shape
+        plan.append((at, index[1:], 4))
+        outs.append(pltpu.VMEM(shape, array.dtype))
+    moved = 2 * sum(math.prod(out.shape) for out in outs)
+    done = jax.ShapeDtypeStruct((8, HEAD_WIDTH), jnp.float32)
+    return pl.pallas_call(
+        functools.partial(fetch_body, plan),
+        out_shape=[*outs, done],
+        in_specs=[pl.BlockSpec(memory_space=pltpu.HBM)] * len(sources) + [VMEM] * len(after),
+        out_specs=[VMEM] * (len(outs) + 1),
+        scratch_shapes=[pltpu.SemaphoreType.DMA((4 * len(outs),))],
+        compiler_params=pltpu.CompilerParams(vmem_limit_bytes=36 << 20),
+        cost_estimate=pl.CostEstimate(flops=0, bytes_accessed=moved, transcendentals=0),
+    )(*sources, *after)
+
+
+def partners(block, axis):
+    return [lax.ppermute(block(k), axis, [(p, p ^ k) for p in range(SIDE)]) for k in FROM[1:]]
+
+
+def project_body(tile, count, x0, x1, x2, x3, *refs):
+    weights = refs[:count]
+    keep, send, rows = refs[count:]
     m = lax.axis_index("gx") ^ lax.axis_index("gy")
-    for s, x in enumerate((x0, x1, x2, x3)):
+    for s, x in zip(FROM, (x0, x1, x2, x3)):
         d = s ^ m
         place = ((d & 1) << 1) | (d >> 1)
         rows[pl.ds(pl.multiple_of(place * BLOCK, BLOCK), BLOCK), :] = x[...]
@@ -175,20 +218,23 @@
                 keep[b, at, :] = part[b * BLOCK : (b + 1) * BLOCK]
                 send[b, at, :] = part[(2 + b) * BLOCK : (3 + b) * BLOCK]
 
-    per = tile // HEAD_WIDTH
-
-    def step(n, _):
-        put(wq, pl.multiple_of(n * tile, tile), tile, n * per)
-        return 0
-
-    lax.fori_loop(0, wq.shape[1] // tile, step, 0)
-    qh, kh = wq.shape[1] // HEAD_WIDTH, wk.shape[1] // HEAD_WIDTH
-    put(wk, 0, wk.shape[1], qh)
-    put(wv, 0, wv.shape[1], qh + kh)
-
-
-def spread_body(groups, keep, got, across, out0, out1, out2, out3, slots):
+    head = 0
+    for w in weights:
+        width = min(tile, w.shape[1])
+        per = width // HEAD_WIDTH
+
+        def step(n, _):
+            put(w, pl.multiple_of(n * width, width), width, head + n * per)
+            return 0
+
+        lax.fori_loop(0, w.shape[1] // width, step, 0)
+        head += w.shape[1] // HEAD_WIDTH
+
+
+def spread_body(groups, keep0, got0, across0, keep1, got1, across1, ready, *refs):
+    outs, slots = refs[:-1], refs[-1]
     j = lax.axis_index("gx")
+    first = keep0.shape[1] // BLOCK
     qh = groups * GROUP
     for g in range(groups):
         for u in range(SLOTS):
@@ -203,12 +249,14 @@
             at = (g * SLOTS + u) * BLOCK
             if h is None:
                 slots[at : at + BLOCK, :] = jnp.zeros((BLOCK, HEAD_WIDTH), jnp.float32)
-            else:
-                src = slice(h * BLOCK, (h + 1) * BLOCK)
-                total = (keep[0, src, :] + got[0, src, :]) + across[src, :]
-                slots[at : at + BLOCK, :] = total.astype(jnp.bfloat16).astype(jnp.float32)
+                continue
+            keep, got, across = (keep0, got0, across0) if h < first else (keep1, got1, across1)
+            h = h if h < first else h - first
+            src = slice(h * BLOCK, (h + 1) * BLOCK)
+            total = (keep[0, src, :] + got[0, src, :]) + across[src, :]
+            slots[at : at + BLOCK, :] = total.astype(jnp.bfloat16).astype(jnp.float32)
     wide = groups * SLOTS
-    for e, out in enumerate((out0, out1, out2, out3)):
+    for e, out in enumerate(outs):
         for t in range(ROWS):
             row = (j ^ e) * ROWS + t
             out[t * wide : (t + 1) * wide, :] = slots[pl.ds(row, wide, stride=BLOCK), :].astype(
@@ -219,53 +267,78 @@
 def attend_body(
     groups, lengths, a0, a1, a2, a3, cosine, sine, keys, values, c0, c1, c2, c3, held
 ):
-    i, j = lax.axis_index("gy"), lax.axis_index("gx")
+    j = lax.axis_index("gx")
+    m = j ^ lax.axis_index("gy")
     scale = 1.0 / HEAD_WIDTH**0.5
-    for e, a in enumerate((a0, a1, a2, a3)):
-        held[e] = a[...]
     wide = groups * SLOTS
-    slot = lax.broadcasted_iota(jnp.int32, (wide, HEAD_WIDTH), 0) % SLOTS
-    is_value = slot == GROUP + 1
-    spot = lax.broadcasted_iota(jnp.int32, (SLOTS, CONTEXT_LENGTH), 1)
+    span = groups * HEAD_WIDTH
+    slot = lax.broadcasted_iota(jnp.int32, (wide, HEAD_WIDTH), 0)
+    is_value = slot % SLOTS == GROUP + 1
+    of_group = [slot // SLOTS == g for g in range(groups)]
+    spot = lax.broadcasted_iota(jnp.int32, (wide, CONTEXT_LENGTH), 1)
+    pieces = [(e, t) for e in range(SIDE) for t in range(ROWS)]
+    heads = dict(zip(FROM, (a0, a1, a2, a3)))
+
+    def lanes(e):
+        return pl.ds(pl.multiple_of((j ^ e) * span, span), span)
+
+    def each_group(block, row):
+        out = block[row : row + 1]
+        for g in range(1, groups):
+            at = g * SLOTS + row
+            out = jnp.where(of_group[g], block[at : at + 1], out)
+        return out
+
+    scores, owns, fresh = [], [], []
+    for e, t in pieces:
+        raw = heads[e][t * wide : (t + 1) * wide, :].astype(jnp.float32)
+        turned = (
+            raw * cosine[t : t + 1, :] + pltpu.roll(raw, HEAD_WIDTH // 2, 1) * sine[t : t + 1, :]
+        )
+        q = jnp.where(is_value, raw, turned).astype(jnp.bfloat16)
+        wide_q = q.astype(jnp.float32)
+        spread = jnp.concatenate(
+            [jnp.where(of_group[g], wide_q, 0.0) for g in range(groups)], axis=1
+        ).astype(jnp.bfloat16)
+        found = lax.dot_general(
+            spread,
+            keys[t, :, lanes(e)],
+            (((1,), (1,)), ((), ())),
+            preferred_element_type=jnp.float32,
+        )
+        scores.append(jnp.where(spot < lengths[t], found * scale, -jnp.inf))
+        owns.append(
+            jnp.sum(wide_q * each_group(wide_q, GROUP), axis=1, keepdims=True) * scale
+        )
+        fresh.append(each_group(wide_q, GROUP + 1))
+    tops = [
+        jnp.maximum(jnp.max(s, axis=1, keepdims=True), own) for s, own in zip(scores, owns)
+    ]
+    cached = [jnp.exp(s - top) for s, top in zip(scores, tops)]
+    owns = [jnp.exp(own - top) for own, top in zip(owns, tops)]
+    totals = [jnp.sum(w, axis=1, keepdims=True) + own for w, own in zip(cached, owns)]
+    weights = [(w / total).astype(jnp.bfloat16) for w, total in zip(cached, totals)]
+    owns = [
+        (own / total).astype(jnp.bfloat16).astype(jnp.float32) for own, total in zip(owns, totals)
+    ]
+    for n, (e, t) in enumerate(pieces):
+        found = jnp.dot(weights[n], values[t, :, lanes(e)], preferred_element_type=jnp.float32)
+        context = found[:, :HEAD_WIDTH]
+        for g in range(1, groups):
+            context = jnp.where(
+                of_group[g], found[:, g * HEAD_WIDTH : (g + 1) * HEAD_WIDTH], context
+            )
+        context = context + owns[n] * fresh[n]
+        held[e ^ m, t * wide : (t + 1) * wide, :] = context.astype(jnp.bfloat16)
     for f, c in enumerate((c0, c1, c2, c3)):
-        source = i ^ f
-        block = held.at[source ^ j]
-        for t in range(ROWS):
-            raw = block[t * wide : (t + 1) * wide, :].astype(jnp.float32)
-            turned = (
-                raw * cosine[t : t + 1, :]
-                + pltpu.roll(raw, HEAD_WIDTH // 2, 1) * sine[t : t + 1, :]
-            )
-            turned = jnp.where(is_value, raw, turned).astype(jnp.bfloat16)
-            live = spot < lengths[t]
-            for g in range(groups):
-                at = pl.ds(pl.multiple_of((source * groups + g) * HEAD_WIDTH, HEAD_WIDTH), HEAD_WIDTH)
-                q = turned[g * SLOTS : (g + 1) * SLOTS]
-                wide_q = q.astype(jnp.float32)
-                own_key = wide_q[GROUP : GROUP + 1]
-                own_value = wide_q[GROUP + 1 : GROUP + 2]
-                scores = lax.dot_general(
-                    q, keys[t, :, at], (((1,), (1,)), ((), ())), preferred_element_type=jnp.float32
-                )
-                scores = jnp.where(live, scores * scale, -jnp.inf)
-                own = jnp.sum(wide_q * own_key, axis=1, keepdims=True) * scale
-                top = jnp.maximum(jnp.max(scores, axis=1, keepdims=True), own)
-                cached = jnp.exp(scores - top)
-                own = jnp.exp(own - top)
-                total = jnp.sum(cached, axis=1, keepdims=True) + own
-                weights = (cached / total).astype(jnp.bfloat16)
-                own = (own / total).astype(jnp.bfloat16).astype(jnp.float32)
-                context = jnp.dot(weights, values[t, :, at], preferred_element_type=jnp.float32)
-                context = context + own * own_value
-                first = t * wide + g * SLOTS
-                c[first : first + SLOTS, :] = context.astype(jnp.bfloat16)
+        c[...] = held[f]
 
 
 def turn_body(groups, c0, c1, c2, c3, out, slots):
     i = lax.axis_index("gy")
     wide = groups * SLOTS
     size = ROWS * wide
-    for f, c in enumerate((c0, c1, c2, c3)):
+    for f, c in zip(FROM, (c0, c1, c2, c3)):
         slots[pl.ds(pl.multiple_of((i ^ f) * size, size), size), :] = c[...].astype(jnp.float32)
     for g in range(groups):
         for u in range(GROUP):
@@ -275,9 +348,9 @@
             ].astype(jnp.bfloat16)
 
 
-def output_body(tile, x0, x1, x2, x3, w, keep, send, rows, ordered):
+def output_body(tile, x0, x1, x2, x3, w0, w1, keep, send, rows, ordered):
     i, j = lax.axis_index("gy"), lax.axis_index("gx")
-    for s, x in enumerate((x0, x1, x2, x3)):
+    for s, x in zip(FROM, (x0, x1, x2, x3)):
         rows[pl.ds(pl.multiple_of((j ^ s) * BLOCK, BLOCK), BLOCK), :] = x[...]
     count = SIDE * BLOCK
     r = lax.broadcasted_iota(jnp.int32, (count, count), 0)
@@ -290,14 +363,17 @@
         jnp.bfloat16
     )
 
-    def step(n, _):
-        at = pl.ds(pl.multiple_of(n * tile, tile), tile)
-        acc = jnp.dot(ordered[...], w[:, at], preferred_element_type=jnp.float32)
-        keep[:, at] = acc[: 2 * BLOCK]
-        send[:, at] = acc[2 * BLOCK :]
-        return 0
-
-    lax.fori_loop(0, w.shape[1] // tile, step, 0)
+    for w, first in ((w0, 0), (w1, w0.shape[1])):
+
+        def step(n, _):
+            c = pl.multiple_of(n * tile, tile)
+            acc = jnp.dot(ordered[...], w[:, pl.ds(c, tile)], preferred_element_type=jnp.float32)
+            at = pl.ds(pl.multiple_of(first + n * tile, tile), tile)
+            keep[:, at] = acc[: 2 * BLOCK]
+            send[:, at] = acc[2 * BLOCK :]
+            return 0
+
+        lax.fori_loop(0, w.shape[1] // tile, step, 0)
 
 
 def square_shards(
@@ -315,7 +391,6 @@
     depth, q_width = w_query.shape
     kv_width = key_matrix.shape[1]
     groups = kv_width // HEAD_WIDTH
-    heads = (q_width + 2 * kv_width) // HEAD_WIDTH
     wide = groups * SLOTS
 
     angles = rotary_angles(positions)
@@ -324,25 +399,38 @@
     sine = jnp.concatenate([-sine, sine], axis=1)
 
     near = partners(lambda k: tokens, "gx")
-    half = jax.ShapeDtypeStruct((2, heads * BLOCK, HEAD_WIDTH), f32)
     tile = 512
-    keep, send = call(
-        functools.partial(project_body, tile),
-        [half, half],
-        (tokens, *near, w_query, key_matrix, value_matrix),
-        [VMEM] * 7,
-        [pltpu.VMEM((SIDE * BLOCK, depth), bf16)],
-        flops=2 * SIDE * BLOCK * depth * heads * HEAD_WIDTH,
-        moved=2 * depth * heads * HEAD_WIDTH,
-    )
-    got = lax.ppermute(send, "gy", [(p, p ^ 1) for p in range(SIDE)])
-    across = lax.ppermute(keep[1] + got[1], "gy", [(p, p ^ 2) for p in range(SIDE)])
+    part = q_width // 2
+    w_first, w_second, key_matrix, value_matrix, _ = fetch(
+        [(w_query, 0, part), (w_query, part, part), (key_matrix,), (value_matrix,)]
+    )
+    sums = []
+    for weights in ((w_first,), (w_second, key_matrix, value_matrix)):
+        columns = sum(w.shape[1] for w in weights)
+        half = jax.ShapeDtypeStruct((2, columns // HEAD_WIDTH * BLOCK, HEAD_WIDTH), f32)
+        keep, send = call(
+            functools.partial(project_body, tile, len(weights)),
+            [half, half],
+            (tokens, *near, *weights),
+            [VMEM] * (4 + len(weights)),
+            [pltpu.VMEM((SIDE * BLOCK, depth), bf16)],
+            flops=2 * SIDE * BLOCK * depth * columns,
+            moved=2 * depth * columns,
+        )
+        got = lax.ppermute(send, "gy", [(p, p ^ 1) for p in range(SIDE)])
+        summed = keep[1] + got[1]
+        sums += [keep, got, lax.ppermute(summed, "gy", [(p, p ^ 2) for p in range(SIDE)])]
+    depth, out_width = w_output.shape
+    part = out_width // 2
+    stored_keys, stored_values, w_first, ready = fetch(
+        [(stored_keys,), (stored_values,), (w_output, 0, part)], summed
+    )
     piece = jax.ShapeDtypeStruct((ROWS * wide, HEAD_WIDTH), bf16)
     mine = call(
         functools.partial(spread_body, groups),
         [piece] * SIDE,
-        (keep, got, across),
-        [VMEM] * 3,
+        (*sums, ready),
+        [VMEM] * 7,
         [pltpu.VMEM((wide * BLOCK, HEAD_WIDTH), f32)],
     )
     others = partners(lambda k: mine[k], "gx")
@@ -353,7 +441,7 @@
         [SMEM] + [VMEM] * 8,
         [pltpu.VMEM((SIDE, ROWS * wide, HEAD_WIDTH), bf16)],
     )
-    others = partners(lambda k: context[k], "gy", (2, 3, 1))
+    others = partners(lambda k: context[k], "gy")
     rows = call(
         functools.partial(turn_body, groups),
         jax.ShapeDtypeStruct((BLOCK, groups * GROUP * HEAD_WIDTH), bf16),
@@ -362,20 +450,20 @@
         [pltpu.VMEM((SIDE * ROWS * wide, HEAD_WIDTH), f32)],
     )
     near = partners(lambda k: rows, "gx")
-    depth, out_width = w_output.shape
+    w_second, _ = fetch([(w_output, part, part)], rows)
     half = jax.ShapeDtypeStruct((2 * BLOCK, out_width), f32)
     keep, send = call(
         functools.partial(output_body, tile),
         [half, half],
-        (rows, *near, w_output),
-        [VMEM] * 5,
+        (rows, *near, w_first, w_second),
+        [VMEM] * 6,
         [pltpu.VMEM((SIDE * BLOCK, depth), bf16)] * 2,
         flops=2 * SIDE * BLOCK * depth * out_width,
         moved=2 * depth * out_width,
     )
     got = lax.ppermute(send, "gy", [(p, p ^ 1) for p in range(SIDE)])
     across = lax.ppermute(
-        keep[BLOCK:] + got[BLOCK:], "gy", [(p, p ^ 2) for p in range(SIDE)]
+        (keep[BLOCK:] + got[BLOCK:]).astype(bf16), "gy", [(p, p ^ 2) for p in range(SIDE)]
     )
     return ((keep[:BLOCK] + got[:BLOCK]) + across).astype(bf16)
 
@@ -392,8 +480,8 @@
         and whole_heads
         and groups * HEAD_WIDTH == key_matrix.shape[1]
         and groups * GROUP * HEAD_WIDTH == w_query.shape[1] == w_output.shape[0]
-        and w_output.shape[1] % 512 == 0
-        and w_query.shape[1] % 512 == 0
+        and w_output.shape[1] % 1024 == 0
+        and w_query.shape[1] % 1024 == 0
     )
     return square_shards(*args) if square else general_shards(*args)
 

time: 87.9 us -> 65.8 us (0.75)
  waiting for transfers between devices: 37.4 us -> 16.5 us
  local copies, waits for them, and re-layouts: 10.1 us -> 0.03 us
  Pallas kernels: 20.1 us -> 26.9 us
  starting transfers between devices: 19.1 us -> 21 us
    pallas_call x0 -> x3, Pallas kernels: none -> 16.4 us  [fetch(): pl.pallas_call(functools.partial(fetch_body, plan), out_shape=[*outs, don...]
    ppermute x12, waiting for transfers between devices: 21.8 us -> 10 us  [partners(): lax.ppermute(block(k), axis, [(p, p ^ k) for p in range(SIDE)])]
    unnamed x18 -> x10, local copies, waits for them, and re-layouts: 10.1 us -> 0.03 us
    pallas_call x5 -> x6, Pallas kernels: 20.1 us -> 10.6 us  [call(): pl.pallas_call(body, out_shape=outs, in_specs=specs, out_specs=jax.tree.m...]
    ppermute x2 -> x3, waiting for transfers between devices: 12.1 us -> 4.78 us  [the longest x1 4.21 us: square_shards(): lax.ppermute((keep[BLOCK:] + got[BLOCK:]).astype(bf16), 'gy', [(p, p ^ 2)...]
    ppermute x2 -> x3, waiting for transfers between devices: 3.51 us -> 1.71 us  [square_shards(): got = lax.ppermute(send, 'gy', [(p, p ^ 1) for p in range(SIDE)])]
    ppermute x2 -> x3, starting transfers between devices: 2.52 us -> 3.52 us  [the longest x2 2.83 us: square_shards(): lax.ppermute(summed, 'gy', [(p, p ^ 2) for p in range(SIDE)])]
  transfers between devices with their start and end apart: 16 -> 18, of which waited for: 12 -> 9; matrix products, arithmetic and copies ran while one was open for 0% -> 0% of each run, Pallas kernels for 0% -> 29%
where the time goes in v2:
time: 65.8 us; the launch traced here: 65.6 us
  Pallas kernels  26.9 us (41%)
  starting transfers between devices  21 us (32%)
  waiting for transfers between devices  16.5 us (25%)
  other arithmetic  0.93 us (1%)
    ppermute x12, starting transfers between devices, partners(): lax.ppermute(block(k), axis, [(p, p ^ k) for p in range(SIDE)])  16.8 us
    pallas_call x3, Pallas kernels, fetch(): pl.pallas_call(functools.partial(fetch_body, plan), out_shape=[*outs, don...  16.4 us
    pallas_call x6, Pallas kernels, call(): pl.pallas_call(body, out_shape=outs, in_specs=specs, out_specs=jax.tree.m...  10.6 us
    ppermute x12, waiting for transfers between devices, partners(): lax.ppermute(block(k), axis, [(p, p ^ k) for p in range(SIDE)])  10 us
    ppermute x1, waiting for transfers between devices, square_shards(): lax.ppermute((keep[BLOCK:] + got[BLOCK:]).astype(bf16), 'gy', [(p, p ^ 2)...  4.21 us
    ppermute x2, starting transfers between devices, square_shards(): lax.ppermute(summed, 'gy', [(p, p ^ 2) for p in range(SIDE)])  2.83 us
    ppermute x3, waiting for transfers between devices, square_shards(): got = lax.ppermute(send, 'gy', [(p, p ^ 1) for p in range(SIDE)])  1.71 us
  transfers between devices with their start and end apart: 18, of which 9 were waited for; matrix products, arithmetic and copies ran while one was open for 0% of the time, Pallas kernels for 29%

profile of v2, /device:TPU:0, one launch (start us, length us, event | category | flops | bytes accessed | tf_op | source)
XLA Modules:
  0.0 65.6 jit_solution(3012464443244705050)
XLA Ops:
  0.0 5.0 %collective-permute-start = (bf16[16,3072]{1,0:T(8,128)(2,1)}, bf16[16,3072]{1,0:T(8,128)(2,1)S(1)}, u32[]{:S(2)}, u32[]{:S(2)}) collective-permute-start(bf16[16,3072]{1,0:T(8,128)(2,1)} %x0.3), channel_id=1, source_target_pairs={{0,12},{4,8},{8,4},{12,0},{1,13},{5,9},{9,5},{13,1},{2,14},{6,10},... | collective-permute-start | bytes 294920 | tf_op jit(solution)/shard_map/ppermute | solution.py:200
  5.7 8.0 %shard_map.91 = (bf16[3072,1536]{1,0:T(8,128)(2,1)S(1)}, bf16[3072,1536]{1,0:T(8,128)(2,1)S(1)}, bf16[3072,256]{1,0:T(8,128)(2,1)S(1)}, bf16[3072,256]{1,0:T(8,128)(2,1)S(1)}, f32[8,128]{1,0:T(8,128)}) custom-call(bf16[3072,3072]{1,0:T(8,128)(2,1)} %refs_0_.3, bf16[3072,256]{1,0:T(8,128)(2,1)} %refs_1_.2, bf16[3072,256]{1,0:T(8,128)(2,1)} %refs_2_.2), custom_call_target="tpu_custom_call" | custom-call | bytes 22020096 | tf_op jit(solution)/shard_map/pallas_call | solution.py:188
  13.7 2.0 %shard_map.92 = (f32[2,192,128]{2,1,0:T(8,128)S(1)}, f32[2,192,128]{2,1,0:T(8,128)S(1)}) custom-call(bf16[16,3072]{1,0:T(8,128)(2,1)S(1)} %copy-done.2, bf16[16,3072]{1,0:T(8,128)(2,1)S(1)} %collective-permute-done.x1, bf16[16,3072]{1,0:T(8,128)(2,1)S(1)} %collective-permute-done.1.x2, bf16[16,3072]{1,0:T(8,128)(2,1)S(1)} %collective-permute-done.2.x3, ...), custom_call_target="tpu_custom_call" | custom-call | flops 603979776 | bytes 9437184 | tf_op jit(solution)/shard_map/pallas_call | solution.py:145
  15.8 2.6 %shard_map.93 = (f32[2,256,128]{2,1,0:T(8,128)S(1)}, f32[2,256,128]{2,1,0:T(8,128)S(1)}) custom-call(bf16[16,3072]{1,0:T(8,128)(2,1)S(1)} %copy-done.2, bf16[16,3072]{1,0:T(8,128)(2,1)S(1)} %collective-permute-done.x1, bf16[16,3072]{1,0:T(8,128)(2,1)S(1)} %collective-permute-done.1.x2, bf16[16,3072]{1,0:T(8,128)(2,1)S(1)} %collective-permute-done.2.x3, ...), custom_call_target="tpu_custom_call" | custom-call | flops 805306368 | bytes 12582912 | tf_op jit(solution)/shard_map/pallas_call | solution.py:145
  19.1 1.7 %collective-permute-start.4 = (f32[192,128]{1,0:T(8,128)S(1)}, f32[192,128]{1,0:T(8,128)S(1)}, u32[]{:S(2)}, u32[]{:S(2)}) collective-permute-start(f32[192,128]{1,0:T(8,128)S(1)} %fusion.4), channel_id=1, source_target_pairs={{0,2},{1,3},{2,0},{3,1},{4,6},{5,7},{6,4},{7,5},{8,10},{9,11},{10,... | collective-permute-start | bytes 294920 | tf_op jit(solution)/shard_map/ppermute | solution.py:422
  20.8 1.1 %collective-permute-start.6 = (f32[256,128]{1,0:T(8,128)S(1)}, f32[256,128]{1,0:T(8,128)S(1)}, u32[]{:S(2)}, u32[]{:S(2)}) collective-permute-start(f32[256,128]{1,0:T(8,128)S(1)} %fusion.3.refs_3_), channel_id=1, source_target_pairs={{0,2},{1,3},{2,0},{3,1},{4,6},{5,7},{6,4},{7,5},{8,10},{9,11},{10,... | collective-permute-start | bytes 393224 | tf_op jit(solution)/shard_map/ppermute | solution.py:422
  22.1 4.0 %shard_map.94 = (bf16[4,128,1024]{2,1,0:T(8,128)(2,1)S(1)}, bf16[4,128,1024]{2,1,0:T(8,128)(2,1)S(1)}, bf16[3072,1536]{1,0:T(8,128)(2,1)S(1)}, f32[8,128]{1,0:T(8,128)S(1)}) custom-call(bf16[4,128,1024]{2,1,0:T(8,128)(2,1)S(1)} %copy-done, bf16[4,128,1024]{2,1,0:T(8,128)(2,1)S(1)} %copy-done.1, bf16[3072,3072]{1,0:T(8,128)(2,1)} %refs_0_.5, ...), custom_call_target="tpu_custom_call" | custom-call | bytes 11534336 | tf_op jit(solution)/shard_map/pallas_call | solution.py:188
  26.8 3.8 %collective-permute-start.7 = (bf16[128,128]{1,0:T(8,128)(2,1)S(1)}, bf16[128,128]{1,0:T(8,128)(2,1)S(1)}, u32[]{:S(2)}, u32[]{:S(2)}) collective-permute-start(bf16[128,128]{1,0:T(8,128)(2,1)S(1)} %get-tuple-element.38), channel_id=1, source_target_pairs={{0,12},{4,8},{8,4},{12,0},{1,13},{5,9},{9,5},{13,1},{2,14},{6,10},... | collective-permute-start | bytes 98312 | tf_op jit(solution)/shard_map/ppermute | solution.py:200
  31.3 1.3 %collective-permute-done.7.a1 = bf16[128,128]{1,0:T(8,128)(2,1)S(1)} collective-permute-done((bf16[128,128]{1,0:T(8,128)(2,1)S(1)}, bf16[128,128]{1,0:T(8,128)(2,1)S(1)}, u32[]{:S(2)}, u32[]{:S(2)}) %collective-permute-start.7) | collective-permute-done | bytes 32800 | tf_op jit(solution)/shard_map/ppermute | solution.py:200
  32.6 1.9 %collective-permute-done.8.a2 = bf16[128,128]{1,0:T(8,128)(2,1)S(1)} collective-permute-done((bf16[128,128]{1,0:T(8,128)(2,1)S(1)}, bf16[128,128]{1,0:T(8,128)(2,1)S(1)}, u32[]{:S(2)}, u32[]{:S(2)}) %collective-permute-start.8) | collective-permute-done | bytes 32800 | tf_op jit(solution)/shard_map/ppermute | solution.py:200
  34.5 0.9 %collective-permute-done.9.a3 = bf16[128,128]{1,0:T(8,128)(2,1)S(1)} collective-permute-done((bf16[128,128]{1,0:T(8,128)(2,1)S(1)}, bf16[128,128]{1,0:T(8,128)(2,1)S(1)}, u32[]{:S(2)}, u32[]{:S(2)}) %collective-permute-start.9) | collective-permute-done | bytes 32800 | tf_op jit(solution)/shard_map/ppermute | solution.py:200
  35.4 1.4 %shard_map.96 = (bf16[128,128]{1,0:T(8,128)(2,1)S(1)}, bf16[128,128]{1,0:T(8,128)(2,1)S(1)}, bf16[128,128]{1,0:T(8,128)(2,1)S(1)}, bf16[128,128]{1,0:T(8,128)(2,1)S(1)}) custom-call(s32[4]{0:T(128)S(1)} %copy-done.3, bf16[128,128]{1,0:T(8,128)(2,1)S(1)} %get-tuple-element.37.a0, bf16[128,128]{1,0:T(8,128)(2,1)S(1)} %collective-permute-done.7.a1, ...), custom_call_target="tpu_custom_call" | custom-call | tf_op jit(solution)/shard_map/pallas_call | solution.py:145
  36.9 1.6 %collective-permute-start.11 = (bf16[128,128]{1,0:T(8,128)(2,1)S(1)}, bf16[128,128]{1,0:T(8,128)(2,1)S(1)}, u32[]{:S(2)}, u32[]{:S(2)}) collective-permute-start(bf16[128,128]{1,0:T(8,128)(2,1)S(1)} %get-tuple-element.45), channel_id=1, source_target_pairs={{0,1},{1,0},{2,3},{3,2},{4,5},{5,4},{6,7},{7,6},{8,9},{9,8},{10,11... | collective-permute-start | bytes 98312 | tf_op jit(solution)/shard_map/ppermute | solution.py:200
  39.1 1.5 %collective-permute-done.10.c1 = bf16[128,128]{1,0:T(8,128)(2,1)S(1)} collective-permute-done((bf16[128,128]{1,0:T(8,128)(2,1)S(1)}, bf16[128,128]{1,0:T(8,128)(2,1)S(1)}, u32[]{:S(2)}, u32[]{:S(2)}) %collective-permute-start.10) | collective-permute-done | bytes 32800 | tf_op jit(solution)/shard_map/ppermute | solution.py:200
  40.6 1.9 %collective-permute-done.12.c3 = bf16[128,128]{1,0:T(8,128)(2,1)S(1)} collective-permute-done((bf16[128,128]{1,0:T(8,128)(2,1)S(1)}, bf16[128,128]{1,0:T(8,128)(2,1)S(1)}, u32[]{:S(2)}, u32[]{:S(2)}) %collective-permute-start.12) | collective-permute-done | bytes 32800 | tf_op jit(solution)/shard_map/ppermute | solution.py:200
  42.6 1.9 %collective-permute-start.13 = (bf16[16,3072]{1,0:T(8,128)(2,1)S(1)}, bf16[16,3072]{1,0:T(8,128)(2,1)S(1)}, u32[]{:S(2)}, u32[]{:S(2)}) collective-permute-start(bf16[16,3072]{1,0:T(8,128)(2,1)S(1)} %shard_map.97.refs_1_.x0), channel_id=1, source_target_pairs={{0,12},{4,8},{8,4},{12,0},{1,13},{5,9},{9,5},{13,1},{2,14},{6,10},... | collective-permute-start | bytes 294920 | tf_op jit(solution)/shard_map/ppermute | solution.py:200
  44.7 2.3 %collective-permute-start.15 = (bf16[16,3072]{1,0:T(8,128)(2,1)S(1)}, bf16[16,3072]{1,0:T(8,128)(2,1)S(1)}, u32[]{:S(2)}, u32[]{:S(2)}) collective-permute-start(bf16[16,3072]{1,0:T(8,128)(2,1)S(1)} %shard_map.97.refs_1_.x0), channel_id=1, source_target_pairs={{0,8},{4,12},{8,0},{12,4},{1,9},{5,13},{9,1},{13,5},{2,10},{6,14},... | collective-permute-start | bytes 294920 | tf_op jit(solution)/shard_map/ppermute | solution.py:200
  47.0 4.4 %shard_map.98 = (bf16[3072,1536]{1,0:T(8,128)(2,1)S(1)}, f32[8,128]{1,0:T(8,128)}) custom-call(bf16[3072,3072]{1,0:T(8,128)(2,1)} %refs_0_.5, bf16[16,3072]{1,0:T(8,128)(2,1)S(1)} %shard_map.97.refs_1_.x0), custom_call_target="tpu_custom_call" | custom-call | bytes 9437184 | tf_op jit(solution)/shard_map/pallas_call | solution.py:188
  51.5 2.5 %collective-permute-done.15.x3 = bf16[16,3072]{1,0:T(8,128)(2,1)S(1)} collective-permute-done((bf16[16,3072]{1,0:T(8,128)(2,1)S(1)}, bf16[16,3072]{1,0:T(8,128)(2,1)S(1)}, u32[]{:S(2)}, u32[]{:S(2)}) %collective-permute-start.15) | collective-permute-done | bytes 98336 | tf_op jit(solution)/shard_map/ppermute | solution.py:200
  54.0 4.3 %shard_map.99 = (f32[32,3072]{1,0:T(8,128)S(1)}, f32[32,3072]{1,0:T(8,128)S(1)}) custom-call(bf16[16,3072]{1,0:T(8,128)(2,1)S(1)} %shard_map.97.refs_1_.x0, bf16[16,3072]{1,0:T(8,128)(2,1)S(1)} %collective-permute-done.13.x1, bf16[16,3072]{1,0:T(8,128)(2,1)S(1)} %collective-permute-done.14.x2, bf16[16,3072]{1,0:T(8,128)(2,1)S(1)} %collective-permute-done.15.x3, ...), custom_call_target="tpu_custom_call" | custom-call | flops 1207959552 | bytes 18874368 | tf_op jit(solution)/shard_map/pallas_call | solution.py:145
  58.3 1.7 %collective-permute-done.16 = f32[32,3072]{1,0:T(8,128)S(1)} collective-permute-done((f32[32,3072]{1,0:T(8,128)S(1)}, f32[32,3072]{1,0:T(8,128)S(1)}, u32[]{:S(2)}, u32[]{:S(2)}) %collective-permute-start.16) | collective-permute-done | bytes 393248 | tf_op jit(solution)/shard_map/ppermute | solution.py:464
  60.1 0.7 %collective-permute-start.17 = (bf16[16,3072]{1,0:T(8,128)(2,1)S(1)}, bf16[16,3072]{1,0:T(8,128)(2,1)S(1)}, u32[]{:S(2)}, u32[]{:S(2)}) collective-permute-start(bf16[16,3072]{1,0:T(8,128)(2,1)S(1)} %fusion), channel_id=1, source_target_pairs={{0,2},{1,3},{2,0},{3,1},{4,6},{5,7},{6,4},{7,5},{8,10},{9,11},{10,... | collective-permute-start | bytes 294920 | tf_op jit(solution)/shard_map/ppermute | solution.py:465
  60.7 4.2 %collective-permute-done.17 = bf16[16,3072]{1,0:T(8,128)(2,1)S(1)} collective-permute-done((bf16[16,3072]{1,0:T(8,128)(2,1)S(1)}, bf16[16,3072]{1,0:T(8,128)(2,1)S(1)}, u32[]{:S(2)}, u32[]{:S(2)}) %collective-permute-start.17) | collective-permute-done | bytes 98336 | tf_op jit(solution)/shard_map/ppermute | solution.py:465
  65.0 0.7 %fusion.2 = bf16[16,3072]{1,0:T(8,128)(2,1)} fusion(f32[32,3072]{1,0:T(8,128)S(1)} %collective-permute-done.16, bf16[16,3072]{1,0:T(8,128)(2,1)S(1)} %collective-permute-done.17, f32[32,3072]{1,0:T(8,128)S(1)} %get-tuple-element.49), kind=kLoop, calls=%fused_computation.4 | loop fusion | flops 196608 | bytes 589824 | tf_op jit(solution)/shard_map/convert_element_type | solution.py:468
  (39 shorter events, 4.0 us)
Async XLA Ops:
  0.0 13.7 %copy-start.2 = (bf16[16,3072]{1,0:T(8,128)(2,1)S(1)}, bf16[16,3072]{1,0:T(8,128)(2,1)}, u32[]{:S(2)}) copy-start(bf16[16,3072]{1,0:T(8,128)(2,1)} %x0.3) | copy-start | bytes 294916
  0.0 13.6 %collective-permute-start = (bf16[16,3072]{1,0:T(8,128)(2,1)}, bf16[16,3072]{1,0:T(8,128)(2,1)S(1)}, u32[]{:S(2)}, u32[]{:S(2)}) collective-permute-start(bf16[16,3072]{1,0:T(8,128)(2,1)} %x0.3), channel_id=1, source_target_pairs={{0,12},{4,8},{8,4},{12,0},{1,13},{5,9},{9,5},{13,1},{2,14},{6,10},... | collective-permute-start | bytes 294920 | tf_op jit(solution)/shard_map/ppermute | solution.py:200
  5.1 8.6 %collective-permute-start.1 = (bf16[16,3072]{1,0:T(8,128)(2,1)}, bf16[16,3072]{1,0:T(8,128)(2,1)S(1)}, u32[]{:S(2)}, u32[]{:S(2)}) collective-permute-start(bf16[16,3072]{1,0:T(8,128)(2,1)} %x0.3), channel_id=1, source_target_pairs={{0,4},{4,0},{8,12},{12,8},{1,5},{5,1},{9,13},{13,9},{2,6},{6,2},{1... | collective-permute-start | bytes 294920 | tf_op jit(solution)/shard_map/ppermute | solution.py:200
  5.1 8.6 %collective-permute-start.2 = (bf16[16,3072]{1,0:T(8,128)(2,1)}, bf16[16,3072]{1,0:T(8,128)(2,1)S(1)}, u32[]{:S(2)}, u32[]{:S(2)}) collective-permute-start(bf16[16,3072]{1,0:T(8,128)(2,1)} %x0.3), channel_id=1, source_target_pairs={{0,8},{4,12},{8,0},{12,4},{1,9},{5,13},{9,1},{13,5},{2,10},{6,14},... | collective-permute-start | bytes 294920 | tf_op jit(solution)/shard_map/ppermute | solution.py:200
  13.7 5.3 %copy-start.4 = (s32[4]{0:T(128)S(1)}, s32[4]{0:T(128)}, u32[]{:S(2)}) copy-start(s32[4]{0:T(128)} %param.17) | copy-start | bytes 52
  13.7 8.3 %copy-start = (bf16[4,128,1024]{2,1,0:T(8,128)(2,1)S(1)}, bf16[4,128,1024]{2,1,0:T(8,128)(2,1)}, u32[]{:S(2)}) copy-start(bf16[4,128,1024]{2,1,0:T(8,128)(2,1)} %refs_0_.4) | copy-start | bytes 3145732
  13.7 8.3 %copy-start.1 = (bf16[4,128,1024]{2,1,0:T(8,128)(2,1)S(1)}, bf16[4,128,1024]{2,1,0:T(8,128)(2,1)}, u32[]{:S(2)}) copy-start(bf16[4,128,1024]{2,1,0:T(8,128)(2,1)} %refs_1_.3) | copy-start | bytes 3145732
  15.7 3.3 %collective-permute-start.3 = (f32[2,192,128]{2,1,0:T(8,128)S(1)}, f32[2,192,128]{2,1,0:T(8,128)S(1)}, u32[]{:S(2)}, u32[]{:S(2)}) collective-permute-start(f32[2,192,128]{2,1,0:T(8,128)S(1)} %get-tuple-element.30), channel_id=1, source_target_pairs={{0,1},{1,0},{2,3},{3,2},{4,5},{5,4},{6,7},{7,6},{8,9},{9,8},{10,11... | collective-permute-start | bytes 589832 | tf_op jit(solution)/shard_map/ppermute | solution.py:420
  18.5 2.3 %collective-permute-start.5 = (f32[2,256,128]{2,1,0:T(8,128)S(1)}, f32[2,256,128]{2,1,0:T(8,128)S(1)}, u32[]{:S(2)}, u32[]{:S(2)}) collective-permute-start(f32[2,256,128]{2,1,0:T(8,128)S(1)} %get-tuple-element.35), channel_id=1, source_target_pairs={{0,1},{1,0},{2,3},{3,2},{4,5},{5,4},{6,7},{7,6},{8,9},{9,8},{10,11... | collective-permute-start | bytes 786440 | tf_op jit(solution)/shard_map/ppermute | solution.py:420
  19.1 7.0 %collective-permute-start.4 = (f32[192,128]{1,0:T(8,128)S(1)}, f32[192,128]{1,0:T(8,128)S(1)}, u32[]{:S(2)}, u32[]{:S(2)}) collective-permute-start(f32[192,128]{1,0:T(8,128)S(1)} %fusion.4), channel_id=1, source_target_pairs={{0,2},{1,3},{2,0},{3,1},{4,6},{5,7},{6,4},{7,5},{8,10},{9,11},{10,... | collective-permute-start | bytes 294920 | tf_op jit(solution)/shard_map/ppermute | solution.py:422
  20.8 5.9 %collective-permute-start.6 = (f32[256,128]{1,0:T(8,128)S(1)}, f32[256,128]{1,0:T(8,128)S(1)}, u32[]{:S(2)}, u32[]{:S(2)}) collective-permute-start(f32[256,128]{1,0:T(8,128)S(1)} %fusion.3.refs_3_), channel_id=1, source_target_pairs={{0,2},{1,3},{2,0},{3,1},{4,6},{5,7},{6,4},{7,5},{8,10},{9,11},{10,... | collective-permute-start | bytes 393224 | tf_op jit(solution)/shard_map/ppermute | solution.py:422
  22.0 13.4 %copy-start.3 = (s32[4]{0:T(128)S(1)}, s32[4]{0:T(128)}, u32[]{:S(2)}) copy-start(s32[4]{0:T(128)} %lengths.1) | copy-start | bytes 52
  26.8 5.8 %collective-permute-start.7 = (bf16[128,128]{1,0:T(8,128)(2,1)S(1)}, bf16[128,128]{1,0:T(8,128)(2,1)S(1)}, u32[]{:S(2)}, u32[]{:S(2)}) collective-permute-start(bf16[128,128]{1,0:T(8,128)(2,1)S(1)} %get-tuple-element.38), channel_id=1, source_target_pairs={{0,12},{4,8},{8,4},{12,0},{1,13},{5,9},{9,5},{13,1},{2,14},{6,10},... | collective-permute-start | bytes 98312 | tf_op jit(solution)/shard_map/ppermute | solution.py:200
  30.6 3.9 %collective-permute-start.8 = (bf16[128,128]{1,0:T(8,128)(2,1)S(1)}, bf16[128,128]{1,0:T(8,128)(2,1)S(1)}, u32[]{:S(2)}, u32[]{:S(2)}) collective-permute-start(bf16[128,128]{1,0:T(8,128)(2,1)S(1)} %get-tuple-element.39), channel_id=1, source_target_pairs={{0,4},{4,0},{8,12},{12,8},{1,5},{5,1},{9,13},{13,9},{2,6},{6,2},{1... | collective-permute-start | bytes 98312 | tf_op jit(solution)/shard_map/ppermute | solution.py:200
  30.6 4.8 %collective-permute-start.9 = (bf16[128,128]{1,0:T(8,128)(2,1)S(1)}, bf16[128,128]{1,0:T(8,128)(2,1)S(1)}, u32[]{:S(2)}, u32[]{:S(2)}) collective-permute-start(bf16[128,128]{1,0:T(8,128)(2,1)S(1)} %get-tuple-element.40), channel_id=1, source_target_pairs={{0,8},{4,12},{8,0},{12,4},{1,9},{5,13},{9,1},{13,5},{2,10},{6,14},... | collective-permute-start | bytes 98312 | tf_op jit(solution)/shard_map/ppermute | solution.py:200
  36.8 3.7 %collective-permute-start.10 = (bf16[128,128]{1,0:T(8,128)(2,1)S(1)}, bf16[128,128]{1,0:T(8,128)(2,1)S(1)}, u32[]{:S(2)}, u32[]{:S(2)}) collective-permute-start(bf16[128,128]{1,0:T(8,128)(2,1)S(1)} %get-tuple-element.44), channel_id=1, source_target_pairs={{0,3},{1,2},{2,1},{3,0},{4,7},{5,6},{6,5},{7,4},{8,11},{9,10},{10,... | collective-permute-start | bytes 98312 | tf_op jit(solution)/shard_map/ppermute | solution.py:200
  36.9 3.6 %collective-permute-start.11 = (bf16[128,128]{1,0:T(8,128)(2,1)S(1)}, bf16[128,128]{1,0:T(8,128)(2,1)S(1)}, u32[]{:S(2)}, u32[]{:S(2)}) collective-permute-start(bf16[128,128]{1,0:T(8,128)(2,1)S(1)} %get-tuple-element.45), channel_id=1, source_target_pairs={{0,1},{1,0},{2,3},{3,2},{4,5},{5,4},{6,7},{7,6},{8,9},{9,8},{10,11... | collective-permute-start | bytes 98312 | tf_op jit(solution)/shard_map/ppermute | solution.py:200
  38.5 3.9 %collective-permute-start.12 = (bf16[128,128]{1,0:T(8,128)(2,1)S(1)}, bf16[128,128]{1,0:T(8,128)(2,1)S(1)}, u32[]{:S(2)}, u32[]{:S(2)}) collective-permute-start(bf16[128,128]{1,0:T(8,128)(2,1)S(1)} %get-tuple-element.46), channel_id=1, source_target_pairs={{0,2},{1,3},{2,0},{3,1},{4,6},{5,7},{6,4},{7,5},{8,10},{9,11},{10,... | collective-permute-start | bytes 98312 | tf_op jit(solution)/shard_map/ppermute | solution.py:200
  42.6 8.9 %collective-permute-start.13 = (bf16[16,3072]{1,0:T(8,128)(2,1)S(1)}, bf16[16,3072]{1,0:T(8,128)(2,1)S(1)}, u32[]{:S(2)}, u32[]{:S(2)}) collective-permute-start(bf16[16,3072]{1,0:T(8,128)(2,1)S(1)} %shard_map.97.refs_1_.x0), channel_id=1, source_target_pairs={{0,12},{4,8},{8,4},{12,0},{1,13},{5,9},{9,5},{13,1},{2,14},{6,10},... | collective-permute-start | bytes 294920 | tf_op jit(solution)/shard_map/ppermute | solution.py:200
  44.5 7.0 %collective-permute-start.14 = (bf16[16,3072]{1,0:T(8,128)(2,1)S(1)}, bf16[16,3072]{1,0:T(8,128)(2,1)S(1)}, u32[]{:S(2)}, u32[]{:S(2)}) collective-permute-start(bf16[16,3072]{1,0:T(8,128)(2,1)S(1)} %shard_map.97.refs_1_.x0), channel_id=1, source_target_pairs={{0,4},{4,0},{8,12},{12,8},{1,5},{5,1},{9,13},{13,9},{2,6},{6,2},{1... | collective-permute-start | bytes 294920 | tf_op jit(solution)/shard_map/ppermute | solution.py:200
  44.7 9.2 %collective-permute-start.15 = (bf16[16,3072]{1,0:T(8,128)(2,1)S(1)}, bf16[16,3072]{1,0:T(8,128)(2,1)S(1)}, u32[]{:S(2)}, u32[]{:S(2)}) collective-permute-start(bf16[16,3072]{1,0:T(8,128)(2,1)S(1)} %shard_map.97.refs_1_.x0), channel_id=1, source_target_pairs={{0,8},{4,12},{8,0},{12,4},{1,9},{5,13},{9,1},{13,5},{2,10},{6,14},... | collective-permute-start | bytes 294920 | tf_op jit(solution)/shard_map/ppermute | solution.py:200
  58.2 1.8 %collective-permute-start.16 = (f32[32,3072]{1,0:T(8,128)S(1)}, f32[32,3072]{1,0:T(8,128)S(1)}, u32[]{:S(2)}, u32[]{:S(2)}) collective-permute-start(f32[32,3072]{1,0:T(8,128)S(1)} %get-tuple-element.50), channel_id=1, source_target_pairs={{0,1},{1,0},{2,3},{3,2},{4,5},{5,4},{6,7},{7,6},{8,9},{9,8},{10,11... | collective-permute-start | bytes 1179656 | tf_op jit(solution)/shard_map/ppermute | solution.py:464
  60.1 4.9 %collective-permute-start.17 = (bf16[16,3072]{1,0:T(8,128)(2,1)S(1)}, bf16[16,3072]{1,0:T(8,128)(2,1)S(1)}, u32[]{:S(2)}, u32[]{:S(2)}) collective-permute-start(bf16[16,3072]{1,0:T(8,128)(2,1)S(1)} %fusion), channel_id=1, source_target_pairs={{0,2},{1,3},{2,0},{3,1},{4,6},{5,7},{6,4},{7,5},{8,10},{9,11},{10,... | collective-permute-start | bytes 294920 | tf_op jit(solution)/shard_map/ppermute | solution.py:465

commit v3 on v2

--- a/solution.py
+++ b/solution.py
@@ -139,6 +139,8 @@
 BLOCK = SIDE * ROWS
 SLOTS = 16
 FROM = (0, 3, 1, 2)
+HEADS_FROM = (0, 2, 3, 1)
+CONTEXT_FROM = (0, 2, 3, 1)
 
 
 def call(body, outs, args, specs, scratch=(), limit=8, flops=0, moved=0):
@@ -196,8 +198,8 @@
     )(*sources, *after)
 
 
-def partners(block, axis):
-    return [lax.ppermute(block(k), axis, [(p, p ^ k) for p in range(SIDE)]) for k in FROM[1:]]
+def partners(block, axis, order):
+    return [lax.ppermute(block(k), axis, [(p, p ^ k) for p in range(SIDE)]) for k in order[1:]]
 
 
 def project_body(tile, count, x0, x1, x2, x3, *refs):
@@ -277,7 +279,7 @@
     of_group = [slot // SLOTS == g for g in range(groups)]
     spot = lax.broadcasted_iota(jnp.int32, (wide, CONTEXT_LENGTH), 1)
     pieces = [(e, t) for e in range(SIDE) for t in range(ROWS)]
-    heads = dict(zip(FROM, (a0, a1, a2, a3)))
+    heads = dict(zip(HEADS_FROM, (a0, a1, a2, a3)))
 
     def lanes(e):
         return pl.ds(pl.multiple_of((j ^ e) * span, span), span)
@@ -338,7 +340,7 @@
     i = lax.axis_index("gy")
     wide = groups * SLOTS
     size = ROWS * wide
-    for f, c in zip(FROM, (c0, c1, c2, c3)):
+    for f, c in zip(CONTEXT_FROM, (c0, c1, c2, c3)):
         slots[pl.ds(pl.multiple_of((i ^ f) * size, size), size), :] = c[...].astype(jnp.float32)
     for g in range(groups):
         for u in range(GROUP):
@@ -348,9 +350,9 @@
             ].astype(jnp.bfloat16)
 
 
-def output_body(tile, x0, x1, x2, x3, w0, w1, keep, send, rows, ordered):
+def order_rows(blocks, rows, ordered):
     i, j = lax.axis_index("gy"), lax.axis_index("gx")
-    for s, x in zip(FROM, (x0, x1, x2, x3)):
+    for s, x in zip(FROM, blocks):
         rows[pl.ds(pl.multiple_of((j ^ s) * BLOCK, BLOCK), BLOCK), :] = x[...]
     count = SIDE * BLOCK
     r = lax.broadcasted_iota(jnp.int32, (count, count), 0)
@@ -363,17 +365,31 @@
         jnp.bfloat16
     )
 
-    for w, first in ((w0, 0), (w1, w0.shape[1])):
-
-        def step(n, _):
-            c = pl.multiple_of(n * tile, tile)
-            acc = jnp.dot(ordered[...], w[:, pl.ds(c, tile)], preferred_element_type=jnp.float32)
-            at = pl.ds(pl.multiple_of(first + n * tile, tile), tile)
-            keep[:, at] = acc[: 2 * BLOCK]
-            send[:, at] = acc[2 * BLOCK :]
-            return 0
-
-        lax.fori_loop(0, w.shape[1] // tile, step, 0)
+
+def multiply(tile, ordered, w, keep, send):
+    def step(n, _):
+        at = pl.ds(pl.multiple_of(n * tile, tile), tile)
+        acc = jnp.dot(ordered[...], w[:, at], preferred_element_type=jnp.float32)
+        keep[:, at] = acc[: 2 * BLOCK]
+        send[:, at] = acc[2 * BLOCK :]
+        return 0
+
+    lax.fori_loop(0, w.shape[1] // tile, step, 0)
+
+
+def first_output_body(tile, x0, x1, x2, x3, w, ready, keep, send, ordered, rows):
+    order_rows((x0, x1, x2, x3), rows, ordered)
+    multiply(tile, ordered, w, keep, send)
+
+
+def finish_body(keep0, got0, across0, keep1, got1, across1, out):
+    first = keep0.shape[1]
+    for keep, got, across, at in (
+        (keep0, got0, across0, slice(0, first)),
+        (keep1, got1, across1, slice(first, None)),
+    ):
+        total = (keep[:BLOCK, :] + got[:BLOCK, :]) + across[...].astype(jnp.float32)
+        out[:, at] = total.astype(jnp.bfloat16)
 
 
 def square_shards(
@@ -398,7 +414,7 @@
     cosine = jnp.concatenate([cosine, cosine], axis=1)
     sine = jnp.concatenate([-sine, sine], axis=1)
 
-    near = partners(lambda k: tokens, "gx")
+    near = partners(lambda k: tokens, "gx", FROM)
     tile = 512
     part = q_width // 2
     w_first, w_second, key_matrix, value_matrix, _ = fetch(
@@ -433,7 +449,7 @@
         [VMEM] * 7,
         [pltpu.VMEM((wide * BLOCK, HEAD_WIDTH), f32)],
     )
-    others = partners(lambda k: mine[k], "gx")
+    others = partners(lambda k: mine[k], "gx", HEADS_FROM)
     context = call(
         functools.partial(attend_body, groups),
         [piece] * SIDE,
@@ -441,7 +457,7 @@
         [SMEM] + [VMEM] * 8,
         [pltpu.VMEM((SIDE, ROWS * wide, HEAD_WIDTH), bf16)],
     )
-    others = partners(lambda k: context[k], "gy")
+    others = partners(lambda k: context[k], "gy", CONTEXT_FROM)
     rows = call(
         functools.partial(turn_body, groups),
         jax.ShapeDtypeStruct((BLOCK, groups * GROUP * HEAD_WIDTH), bf16),
@@ -449,23 +465,38 @@
         [VMEM] * 4,
         [pltpu.VMEM((SIDE * ROWS * wide, HEAD_WIDTH), f32)],
     )
-    near = partners(lambda k: rows, "gx")
-    w_second, _ = fetch([(w_output, part, part)], rows)
-    half = jax.ShapeDtypeStruct((2 * BLOCK, out_width), f32)
-    keep, send = call(
-        functools.partial(output_body, tile),
-        [half, half],
-        (rows, *near, w_first, w_second),
-        [VMEM] * 6,
-        [pltpu.VMEM((SIDE * BLOCK, depth), bf16)] * 2,
-        flops=2 * SIDE * BLOCK * depth * out_width,
-        moved=2 * depth * out_width,
-    )
-    got = lax.ppermute(send, "gy", [(p, p ^ 1) for p in range(SIDE)])
-    across = lax.ppermute(
-        (keep[BLOCK:] + got[BLOCK:]).astype(bf16), "gy", [(p, p ^ 2) for p in range(SIDE)]
-    )
-    return ((keep[:BLOCK] + got[:BLOCK]) + across).astype(bf16)
+    near = partners(lambda k: rows, "gx", FROM)
+    w_second, ready = fetch([(w_output, part, part)], rows)
+    sums = []
+    for w in (w_first, w_second):
+        columns = w.shape[1]
+        half = jax.ShapeDtypeStruct((2 * BLOCK, columns), f32)
+        flops, moved = 2 * SIDE * BLOCK * depth * columns, 2 * depth * columns
+        if not sums:
+            keep, send, ordered = call(
+                functools.partial(first_output_body, tile),
+                [half, half, jax.ShapeDtypeStruct((SIDE * BLOCK, depth), bf16)],
+                (rows, *near, w, ready),
+                [VMEM] * 6,
+                [pltpu.VMEM((SIDE * BLOCK, depth), bf16)],
+                flops=flops,
+                moved=moved,
+            )
+        else:
+            keep, send = call(
+                functools.partial(multiply, tile),
+                [half, half],
+                (ordered, w),
+                [VMEM] * 2,
+                flops=flops,
+                moved=moved,
+            )
+        got = lax.ppermute(send, "gy", [(p, p ^ 1) for p in range(SIDE)])
+        summed = (keep[BLOCK:] + got[BLOCK:]).astype(bf16)
+        sums += [keep, got, lax.ppermute(summed, "gy", [(p, p ^ 2) for p in range(SIDE)])]
+    return call(
+        finish_body, jax.ShapeDtypeStruct((BLOCK, out_width), bf16), sums, [VMEM] * 6
+    )
 
 
 def shards(*args):

time: 65.8 us -> 63.4 us (0.964)
  waiting for transfers between devices: 16.5 us -> 12.4 us
  starting transfers between devices: 21 us -> 23.4 us
  other arithmetic: 0.93 us -> 0.25 us
    ppermute x1 -> x0, waiting for transfers between devices: 4.21 us -> none  [square_shards(): lax.ppermute((keep[BLOCK:] + got[BLOCK:]).astype(bf16), 'gy', [(p, p ^ 2)...]
    ppermute x2 -> x4, waiting for transfers between devices: 0.56 us -> 3.66 us  [square_shards(): lax.ppermute(summed, 'gy', [(p, p ^ 2) for p in range(SIDE)])]
    ppermute x2 -> x4, starting transfers between devices: 2.83 us -> 5.37 us  [square_shards(): lax.ppermute(summed, 'gy', [(p, p ^ 2) for p in range(SIDE)])]
    ppermute x3 -> x4, waiting for transfers between devices: 1.71 us -> 0.01 us  [square_shards(): got = lax.ppermute(send, 'gy', [(p, p ^ 1) for p in range(SIDE)])]
    ppermute x12, waiting for transfers between devices: 10 us -> 8.71 us  [partners(): lax.ppermute(block(k), axis, [(p, p ^ k) for p in range(SIDE)])]
    ppermute x1 -> x0, starting transfers between devices: 0.69 us -> none  [square_shards(): lax.ppermute((keep[BLOCK:] + got[BLOCK:]).astype(bf16), 'gy', [(p, p ^ 2)...]
    convert_element_type x2, other arithmetic: 0.7 us -> 0.03 us  [square_shards(): summed = (keep[BLOCK:] + got[BLOCK:]).astype(bf16)]
    pallas_call x6 -> x8, Pallas kernels: 10.6 us -> 11.2 us  [call(): pl.pallas_call(body, out_shape=outs, in_specs=specs, out_specs=jax.tree.m...]
  transfers between devices with their start and end apart: 18 -> 20, of which waited for: 9 -> 9; matrix products, arithmetic and copies ran while one was open for 0% -> 0% of each run, Pallas kernels for 29% -> 32%
where the time goes in v3:
time: 63.4 us; the launch traced here: 63.3 us
  Pallas kernels  27 us (43%)
  starting transfers between devices  23.4 us (37%)
  waiting for transfers between devices  12.4 us (20%)
    ppermute x12, starting transfers between devices, partners(): lax.ppermute(block(k), axis, [(p, p ^ k) for p in range(SIDE)])  16.7 us
    pallas_call x3, Pallas kernels, fetch(): pl.pallas_call(functools.partial(fetch_body, plan), out_shape=[*outs, don...  15.8 us
    pallas_call x8, Pallas kernels, call(): pl.pallas_call(body, out_shape=outs, in_specs=specs, out_specs=jax.tree.m...  11.2 us
    ppermute x12, waiting for transfers between devices, partners(): lax.ppermute(block(k), axis, [(p, p ^ k) for p in range(SIDE)])  8.71 us
    ppermute x4, starting transfers between devices, square_shards(): lax.ppermute(summed, 'gy', [(p, p ^ 2) for p in range(SIDE)])  5.37 us
    ppermute x4, waiting for transfers between devices, square_shards(): lax.ppermute(summed, 'gy', [(p, p ^ 2) for p in range(SIDE)])  3.66 us
  transfers between devices with their start and end apart: 20, of which 9 were waited for; matrix products, arithmetic and copies ran while one was open for 0% of the time, Pallas kernels for 32%

profile of v3, /device:TPU:0, one launch (start us, length us, event | category | flops | bytes accessed | tf_op | source)
XLA Modules:
  0.0 63.3 jit_solution(7026840221264205742)
XLA Ops:
  0.0 5.0 %collective-permute-start = (bf16[16,3072]{1,0:T(8,128)(2,1)}, bf16[16,3072]{1,0:T(8,128)(2,1)S(1)}, u32[]{:S(2)}, u32[]{:S(2)}) collective-permute-start(bf16[16,3072]{1,0:T(8,128)(2,1)} %x0.3), channel_id=1, source_target_pairs={{0,12},{4,8},{8,4},{12,0},{1,13},{5,9},{9,5},{13,1},{2,14},{6,10},... | collective-permute-start | bytes 294920 | tf_op jit(solution)/shard_map/ppermute | solution.py:202
  5.7 8.0 %shard_map.91 = (bf16[3072,1536]{1,0:T(8,128)(2,1)S(1)}, bf16[3072,1536]{1,0:T(8,128)(2,1)S(1)}, bf16[3072,256]{1,0:T(8,128)(2,1)S(1)}, bf16[3072,256]{1,0:T(8,128)(2,1)S(1)}, f32[8,128]{1,0:T(8,128)}) custom-call(bf16[3072,3072]{1,0:T(8,128)(2,1)} %refs_0_.3, bf16[3072,256]{1,0:T(8,128)(2,1)} %refs_1_.2, bf16[3072,256]{1,0:T(8,128)(2,1)} %refs_2_.2), custom_call_target="tpu_custom_call" | custom-call | bytes 22020096 | tf_op jit(solution)/shard_map/pallas_call | solution.py:190
  13.7 2.0 %shard_map.92 = (f32[2,192,128]{2,1,0:T(8,128)S(1)}, f32[2,192,128]{2,1,0:T(8,128)S(1)}) custom-call(bf16[16,3072]{1,0:T(8,128)(2,1)S(1)} %copy-done.2, bf16[16,3072]{1,0:T(8,128)(2,1)S(1)} %collective-permute-done.x1, bf16[16,3072]{1,0:T(8,128)(2,1)S(1)} %collective-permute-done.1.x2, bf16[16,3072]{1,0:T(8,128)(2,1)S(1)} %collective-permute-done.2.x3, ...), custom_call_target="tpu_custom_call" | custom-call | flops 603979776 | bytes 9437184 | tf_op jit(solution)/shard_map/pallas_call | solution.py:147
  15.8 2.6 %shard_map.93 = (f32[2,256,128]{2,1,0:T(8,128)S(1)}, f32[2,256,128]{2,1,0:T(8,128)S(1)}) custom-call(bf16[16,3072]{1,0:T(8,128)(2,1)S(1)} %copy-done.2, bf16[16,3072]{1,0:T(8,128)(2,1)S(1)} %collective-permute-done.x1, bf16[16,3072]{1,0:T(8,128)(2,1)S(1)} %collective-permute-done.1.x2, bf16[16,3072]{1,0:T(8,128)(2,1)S(1)} %collective-permute-done.2.x3, ...), custom_call_target="tpu_custom_call" | custom-call | flops 805306368 | bytes 12582912 | tf_op jit(solution)/shard_map/pallas_call | solution.py:147
  19.1 1.7 %collective-permute-start.4 = (f32[192,128]{1,0:T(8,128)S(1)}, f32[192,128]{1,0:T(8,128)S(1)}, u32[]{:S(2)}, u32[]{:S(2)}) collective-permute-start(f32[192,128]{1,0:T(8,128)S(1)} %fusion.3), channel_id=1, source_target_pairs={{0,2},{1,3},{2,0},{3,1},{4,6},{5,7},{6,4},{7,5},{8,10},{9,11},{10,... | collective-permute-start | bytes 294920 | tf_op jit(solution)/shard_map/ppermute | solution.py:438
  20.8 1.1 %collective-permute-start.6 = (f32[256,128]{1,0:T(8,128)S(1)}, f32[256,128]{1,0:T(8,128)S(1)}, u32[]{:S(2)}, u32[]{:S(2)}) collective-permute-start(f32[256,128]{1,0:T(8,128)S(1)} %fusion.refs_3_), channel_id=1, source_target_pairs={{0,2},{1,3},{2,0},{3,1},{4,6},{5,7},{6,4},{7,5},{8,10},{9,11},{10,... | collective-permute-start | bytes 393224 | tf_op jit(solution)/shard_map/ppermute | solution.py:438
  22.1 4.0 %shard_map.94 = (bf16[4,128,1024]{2,1,0:T(8,128)(2,1)S(1)}, bf16[4,128,1024]{2,1,0:T(8,128)(2,1)S(1)}, bf16[3072,1536]{1,0:T(8,128)(2,1)S(1)}, f32[8,128]{1,0:T(8,128)S(1)}) custom-call(bf16[4,128,1024]{2,1,0:T(8,128)(2,1)S(1)} %copy-done, bf16[4,128,1024]{2,1,0:T(8,128)(2,1)S(1)} %copy-done.1, bf16[3072,3072]{1,0:T(8,128)(2,1)} %refs_0_.5, ...), custom_call_target="tpu_custom_call" | custom-call | bytes 11534336 | tf_op jit(solution)/shard_map/pallas_call | solution.py:190
  26.8 2.4 %collective-permute-start.7 = (bf16[128,128]{1,0:T(8,128)(2,1)S(1)}, bf16[128,128]{1,0:T(8,128)(2,1)S(1)}, u32[]{:S(2)}, u32[]{:S(2)}) collective-permute-start(bf16[128,128]{1,0:T(8,128)(2,1)S(1)} %get-tuple-element.42), channel_id=1, source_target_pairs={{0,8},{4,12},{8,0},{12,4},{1,9},{5,13},{9,1},{13,5},{2,10},{6,14},... | collective-permute-start | bytes 98312 | tf_op jit(solution)/shard_map/ppermute | solution.py:202
  29.2 1.5 %collective-permute-start.8 = (bf16[128,128]{1,0:T(8,128)(2,1)S(1)}, bf16[128,128]{1,0:T(8,128)(2,1)S(1)}, u32[]{:S(2)}, u32[]{:S(2)}) collective-permute-start(bf16[128,128]{1,0:T(8,128)(2,1)S(1)} %get-tuple-element.43), channel_id=1, source_target_pairs={{0,12},{4,8},{8,4},{12,0},{1,13},{5,9},{9,5},{13,1},{2,14},{6,10},... | collective-permute-start | bytes 98312 | tf_op jit(solution)/shard_map/ppermute | solution.py:202
  31.7 3.3 %collective-permute-done.8.a2 = bf16[128,128]{1,0:T(8,128)(2,1)S(1)} collective-permute-done((bf16[128,128]{1,0:T(8,128)(2,1)S(1)}, bf16[128,128]{1,0:T(8,128)(2,1)S(1)}, u32[]{:S(2)}, u32[]{:S(2)}) %collective-permute-start.8) | collective-permute-done | bytes 32800 | tf_op jit(solution)/shard_map/ppermute | solution.py:202
  35.0 1.4 %shard_map.96 = (bf16[128,128]{1,0:T(8,128)(2,1)S(1)}, bf16[128,128]{1,0:T(8,128)(2,1)S(1)}, bf16[128,128]{1,0:T(8,128)(2,1)S(1)}, bf16[128,128]{1,0:T(8,128)(2,1)S(1)}) custom-call(s32[4]{0:T(128)S(1)} %copy-done.3, bf16[128,128]{1,0:T(8,128)(2,1)S(1)} %get-tuple-element.41.a0, bf16[128,128]{1,0:T(8,128)(2,1)S(1)} %collective-permute-done.7.a1, ...), custom_call_target="tpu_custom_call" | custom-call | tf_op jit(solution)/shard_map/pallas_call | solution.py:147
  36.4 1.6 %collective-permute-start.10 = (bf16[128,128]{1,0:T(8,128)(2,1)S(1)}, bf16[128,128]{1,0:T(8,128)(2,1)S(1)}, u32[]{:S(2)}, u32[]{:S(2)}) collective-permute-start(bf16[128,128]{1,0:T(8,128)(2,1)S(1)} %get-tuple-element.48), channel_id=1, source_target_pairs={{0,2},{1,3},{2,0},{3,1},{4,6},{5,7},{6,4},{7,5},{8,10},{9,11},{10,... | collective-permute-start | bytes 98312 | tf_op jit(solution)/shard_map/ppermute | solution.py:202
  38.6 1.8 %collective-permute-done.10.c1 = bf16[128,128]{1,0:T(8,128)(2,1)S(1)} collective-permute-done((bf16[128,128]{1,0:T(8,128)(2,1)S(1)}, bf16[128,128]{1,0:T(8,128)(2,1)S(1)}, u32[]{:S(2)}, u32[]{:S(2)}) %collective-permute-start.10) | collective-permute-done | bytes 32800 | tf_op jit(solution)/shard_map/ppermute | solution.py:202
  41.4 2.0 %collective-permute-start.13 = (bf16[16,3072]{1,0:T(8,128)(2,1)S(1)}, bf16[16,3072]{1,0:T(8,128)(2,1)S(1)}, u32[]{:S(2)}, u32[]{:S(2)}) collective-permute-start(bf16[16,3072]{1,0:T(8,128)(2,1)S(1)} %shard_map.97.refs_1_.x0), channel_id=1, source_target_pairs={{0,12},{4,8},{8,4},{12,0},{1,13},{5,9},{9,5},{13,1},{2,14},{6,10},... | collective-permute-start | bytes 294920 | tf_op jit(solution)/shard_map/ppermute | solution.py:202
  43.6 2.2 %collective-permute-start.15 = (bf16[16,3072]{1,0:T(8,128)(2,1)S(1)}, bf16[16,3072]{1,0:T(8,128)(2,1)S(1)}, u32[]{:S(2)}, u32[]{:S(2)}) collective-permute-start(bf16[16,3072]{1,0:T(8,128)(2,1)S(1)} %shard_map.97.refs_1_.x0), channel_id=1, source_target_pairs={{0,8},{4,12},{8,0},{12,4},{1,9},{5,13},{9,1},{13,5},{2,10},{6,14},... | collective-permute-start | bytes 294920 | tf_op jit(solution)/shard_map/ppermute | solution.py:202
  45.9 3.8 %shard_map.98 = (bf16[3072,1536]{1,0:T(8,128)(2,1)S(1)}, f32[8,128]{1,0:T(8,128)S(1)}) custom-call(bf16[3072,3072]{1,0:T(8,128)(2,1)} %refs_0_.5, bf16[16,3072]{1,0:T(8,128)(2,1)S(1)} %shard_map.97.refs_1_.x0), custom_call_target="tpu_custom_call" | custom-call | bytes 9437184 | tf_op jit(solution)/shard_map/pallas_call | solution.py:190
  49.7 1.3 %collective-permute-done.14.x2 = bf16[16,3072]{1,0:T(8,128)(2,1)S(1)} collective-permute-done((bf16[16,3072]{1,0:T(8,128)(2,1)S(1)}, bf16[16,3072]{1,0:T(8,128)(2,1)S(1)}, u32[]{:S(2)}, u32[]{:S(2)}) %collective-permute-start.14) | collective-permute-done | bytes 98336 | tf_op jit(solution)/shard_map/ppermute | solution.py:202
  51.0 1.0 %collective-permute-done.15.x3 = bf16[16,3072]{1,0:T(8,128)(2,1)S(1)} collective-permute-done((bf16[16,3072]{1,0:T(8,128)(2,1)S(1)}, bf16[16,3072]{1,0:T(8,128)(2,1)S(1)}, u32[]{:S(2)}, u32[]{:S(2)}) %collective-permute-start.15) | collective-permute-done | bytes 98336 | tf_op jit(solution)/shard_map/ppermute | solution.py:202
  52.0 2.3 %shard_map.99 = (f32[32,1536]{1,0:T(8,128)S(1)}, f32[32,1536]{1,0:T(8,128)S(1)}, bf16[64,3072]{1,0:T(8,128)(2,1)S(1)}) custom-call(bf16[16,3072]{1,0:T(8,128)(2,1)S(1)} %shard_map.97.refs_1_.x0, bf16[16,3072]{1,0:T(8,128)(2,1)S(1)} %collective-permute-done.13.x1, bf16[16,3072]{1,0:T(8,128)(2,1)S(1)} %collective-permute-done.14.x2, ...), custom_call_target="tpu_custom_call" | custom-call | flops 603979776 | bytes 9437184 | tf_op jit(solution)/shard_map/pallas_call | solution.py:147
  54.4 2.0 %shard_map.100 = (f32[32,1536]{1,0:T(8,128)S(1)}, f32[32,1536]{1,0:T(8,128)S(1)}) custom-call(bf16[64,3072]{1,0:T(8,128)(2,1)S(1)} %get-tuple-element.55.ordered, bf16[3072,1536]{1,0:T(8,128)(2,1)S(1)} %get-tuple-element.56.w), custom_call_target="tpu_custom_call" | custom-call | flops 603979776 | bytes 9437184 | tf_op jit(solution)/shard_map/pallas_call | solution.py:147
  56.9 1.5 %collective-permute-start.17 = (bf16[16,1536]{1,0:T(8,128)(2,1)S(1)}, bf16[16,1536]{1,0:T(8,128)(2,1)S(1)}, u32[]{:S(2)}, u32[]{:S(2)}) collective-permute-start(bf16[16,1536]{1,0:T(8,128)(2,1)S(1)} %fusion.2), channel_id=1, source_target_pairs={{0,2},{1,3},{2,0},{3,1},{4,6},{5,7},{6,4},{7,5},{8,10},{9,11},{10,... | collective-permute-start | bytes 147464 | tf_op jit(solution)/shard_map/ppermute | solution.py:496
  58.4 1.1 %collective-permute-start.19 = (bf16[16,1536]{1,0:T(8,128)(2,1)S(1)}, bf16[16,1536]{1,0:T(8,128)(2,1)S(1)}, u32[]{:S(2)}, u32[]{:S(2)}) collective-permute-start(bf16[16,1536]{1,0:T(8,128)(2,1)S(1)} %fusion.1), channel_id=1, source_target_pairs={{0,2},{1,3},{2,0},{3,1},{4,6},{5,7},{6,4},{7,5},{8,10},{9,11},{10,... | collective-permute-start | bytes 147464 | tf_op jit(solution)/shard_map/ppermute | solution.py:496
  59.5 1.7 %collective-permute-done.17.across0 = bf16[16,1536]{1,0:T(8,128)(2,1)S(1)} collective-permute-done((bf16[16,1536]{1,0:T(8,128)(2,1)S(1)}, bf16[16,1536]{1,0:T(8,128)(2,1)S(1)}, u32[]{:S(2)}, u32[]{:S(2)}) %collective-permute-start.17) | collective-permute-done | bytes 49184 | tf_op jit(solution)/shard_map/ppermute | solution.py:496
  61.2 1.4 %collective-permute-done.19.across1 = bf16[16,1536]{1,0:T(8,128)(2,1)S(1)} collective-permute-done((bf16[16,1536]{1,0:T(8,128)(2,1)S(1)}, bf16[16,1536]{1,0:T(8,128)(2,1)S(1)}, u32[]{:S(2)}, u32[]{:S(2)}) %collective-permute-start.19) | collective-permute-done | bytes 49184 | tf_op jit(solution)/shard_map/ppermute | solution.py:496
  (45 shorter events, 6.4 us)
Async XLA Ops:
  0.0 13.7 %copy-start.2 = (bf16[16,3072]{1,0:T(8,128)(2,1)S(1)}, bf16[16,3072]{1,0:T(8,128)(2,1)}, u32[]{:S(2)}) copy-start(bf16[16,3072]{1,0:T(8,128)(2,1)} %x0.3) | copy-start | bytes 294916
  0.0 13.6 %collective-permute-start = (bf16[16,3072]{1,0:T(8,128)(2,1)}, bf16[16,3072]{1,0:T(8,128)(2,1)S(1)}, u32[]{:S(2)}, u32[]{:S(2)}) collective-permute-start(bf16[16,3072]{1,0:T(8,128)(2,1)} %x0.3), channel_id=1, source_target_pairs={{0,12},{4,8},{8,4},{12,0},{1,13},{5,9},{9,5},{13,1},{2,14},{6,10},... | collective-permute-start | bytes 294920 | tf_op jit(solution)/shard_map/ppermute | solution.py:202
  5.1 8.6 %collective-permute-start.1 = (bf16[16,3072]{1,0:T(8,128)(2,1)}, bf16[16,3072]{1,0:T(8,128)(2,1)S(1)}, u32[]{:S(2)}, u32[]{:S(2)}) collective-permute-start(bf16[16,3072]{1,0:T(8,128)(2,1)} %x0.3), channel_id=1, source_target_pairs={{0,4},{4,0},{8,12},{12,8},{1,5},{5,1},{9,13},{13,9},{2,6},{6,2},{1... | collective-permute-start | bytes 294920 | tf_op jit(solution)/shard_map/ppermute | solution.py:202
  5.1 8.6 %collective-permute-start.2 = (bf16[16,3072]{1,0:T(8,128)(2,1)}, bf16[16,3072]{1,0:T(8,128)(2,1)S(1)}, u32[]{:S(2)}, u32[]{:S(2)}) collective-permute-start(bf16[16,3072]{1,0:T(8,128)(2,1)} %x0.3), channel_id=1, source_target_pairs={{0,8},{4,12},{8,0},{12,4},{1,9},{5,13},{9,1},{13,5},{2,10},{6,14},... | collective-permute-start | bytes 294920 | tf_op jit(solution)/shard_map/ppermute | solution.py:202
  13.7 8.3 %copy-start = (bf16[4,128,1024]{2,1,0:T(8,128)(2,1)S(1)}, bf16[4,128,1024]{2,1,0:T(8,128)(2,1)}, u32[]{:S(2)}) copy-start(bf16[4,128,1024]{2,1,0:T(8,128)(2,1)} %refs_0_.4) | copy-start | bytes 3145732
  13.7 8.3 %copy-start.1 = (bf16[4,128,1024]{2,1,0:T(8,128)(2,1)S(1)}, bf16[4,128,1024]{2,1,0:T(8,128)(2,1)}, u32[]{:S(2)}) copy-start(bf16[4,128,1024]{2,1,0:T(8,128)(2,1)} %refs_1_.3) | copy-start | bytes 3145732
  15.7 3.3 %collective-permute-start.3 = (f32[2,192,128]{2,1,0:T(8,128)S(1)}, f32[2,192,128]{2,1,0:T(8,128)S(1)}, u32[]{:S(2)}, u32[]{:S(2)}) collective-permute-start(f32[2,192,128]{2,1,0:T(8,128)S(1)} %get-tuple-element.34), channel_id=1, source_target_pairs={{0,1},{1,0},{2,3},{3,2},{4,5},{5,4},{6,7},{7,6},{8,9},{9,8},{10,11... | collective-permute-start | bytes 589832 | tf_op jit(solution)/shard_map/ppermute | solution.py:436
  18.5 2.3 %collective-permute-start.5 = (f32[2,256,128]{2,1,0:T(8,128)S(1)}, f32[2,256,128]{2,1,0:T(8,128)S(1)}, u32[]{:S(2)}, u32[]{:S(2)}) collective-permute-start(f32[2,256,128]{2,1,0:T(8,128)S(1)} %get-tuple-element.39), channel_id=1, source_target_pairs={{0,1},{1,0},{2,3},{3,2},{4,5},{5,4},{6,7},{7,6},{8,9},{9,8},{10,11... | collective-permute-start | bytes 786440 | tf_op jit(solution)/shard_map/ppermute | solution.py:436
  19.1 7.0 %collective-permute-start.4 = (f32[192,128]{1,0:T(8,128)S(1)}, f32[192,128]{1,0:T(8,128)S(1)}, u32[]{:S(2)}, u32[]{:S(2)}) collective-permute-start(f32[192,128]{1,0:T(8,128)S(1)} %fusion.3), channel_id=1, source_target_pairs={{0,2},{1,3},{2,0},{3,1},{4,6},{5,7},{6,4},{7,5},{8,10},{9,11},{10,... | collective-permute-start | bytes 294920 | tf_op jit(solution)/shard_map/ppermute | solution.py:438
  20.8 5.9 %collective-permute-start.6 = (f32[256,128]{1,0:T(8,128)S(1)}, f32[256,128]{1,0:T(8,128)S(1)}, u32[]{:S(2)}, u32[]{:S(2)}) collective-permute-start(f32[256,128]{1,0:T(8,128)S(1)} %fusion.refs_3_), channel_id=1, source_target_pairs={{0,2},{1,3},{2,0},{3,1},{4,6},{5,7},{6,4},{7,5},{8,10},{9,11},{10,... | collective-permute-start | bytes 393224 | tf_op jit(solution)/shard_map/ppermute | solution.py:438
  22.0 12.9 %copy-start.3 = (s32[4]{0:T(128)S(1)}, s32[4]{0:T(128)}, u32[]{:S(2)}) copy-start(s32[4]{0:T(128)} %lengths.1) | copy-start | bytes 52
  26.8 4.9 %collective-permute-start.7 = (bf16[128,128]{1,0:T(8,128)(2,1)S(1)}, bf16[128,128]{1,0:T(8,128)(2,1)S(1)}, u32[]{:S(2)}, u32[]{:S(2)}) collective-permute-start(bf16[128,128]{1,0:T(8,128)(2,1)S(1)} %get-tuple-element.42), channel_id=1, source_target_pairs={{0,8},{4,12},{8,0},{12,4},{1,9},{5,13},{9,1},{13,5},{2,10},{6,14},... | collective-permute-start | bytes 98312 | tf_op jit(solution)/shard_map/ppermute | solution.py:202
  29.2 5.8 %collective-permute-start.8 = (bf16[128,128]{1,0:T(8,128)(2,1)S(1)}, bf16[128,128]{1,0:T(8,128)(2,1)S(1)}, u32[]{:S(2)}, u32[]{:S(2)}) collective-permute-start(bf16[128,128]{1,0:T(8,128)(2,1)S(1)} %get-tuple-element.43), channel_id=1, source_target_pairs={{0,12},{4,8},{8,4},{12,0},{1,13},{5,9},{9,5},{13,1},{2,14},{6,10},... | collective-permute-start | bytes 98312 | tf_op jit(solution)/shard_map/ppermute | solution.py:202
  30.7 4.3 %collective-permute-start.9 = (bf16[128,128]{1,0:T(8,128)(2,1)S(1)}, bf16[128,128]{1,0:T(8,128)(2,1)S(1)}, u32[]{:S(2)}, u32[]{:S(2)}) collective-permute-start(bf16[128,128]{1,0:T(8,128)(2,1)S(1)} %get-tuple-element.44), channel_id=1, source_target_pairs={{0,4},{4,0},{8,12},{12,8},{1,5},{5,1},{9,13},{13,9},{2,6},{6,2},{1... | collective-permute-start | bytes 98312 | tf_op jit(solution)/shard_map/ppermute | solution.py:202
  36.4 4.0 %collective-permute-start.10 = (bf16[128,128]{1,0:T(8,128)(2,1)S(1)}, bf16[128,128]{1,0:T(8,128)(2,1)S(1)}, u32[]{:S(2)}, u32[]{:S(2)}) collective-permute-start(bf16[128,128]{1,0:T(8,128)(2,1)S(1)} %get-tuple-element.48), channel_id=1, source_target_pairs={{0,2},{1,3},{2,0},{3,1},{4,6},{5,7},{6,4},{7,5},{8,10},{9,11},{10,... | collective-permute-start | bytes 98312 | tf_op jit(solution)/shard_map/ppermute | solution.py:202
  37.9 3.3 %collective-permute-start.11 = (bf16[128,128]{1,0:T(8,128)(2,1)S(1)}, bf16[128,128]{1,0:T(8,128)(2,1)S(1)}, u32[]{:S(2)}, u32[]{:S(2)}) collective-permute-start(bf16[128,128]{1,0:T(8,128)(2,1)S(1)} %get-tuple-element.49), channel_id=1, source_target_pairs={{0,3},{1,2},{2,1},{3,0},{4,7},{5,6},{6,5},{7,4},{8,11},{9,10},{10,... | collective-permute-start | bytes 98312 | tf_op jit(solution)/shard_map/ppermute | solution.py:202
  37.9 3.3 %collective-permute-start.12 = (bf16[128,128]{1,0:T(8,128)(2,1)S(1)}, bf16[128,128]{1,0:T(8,128)(2,1)S(1)}, u32[]{:S(2)}, u32[]{:S(2)}) collective-permute-start(bf16[128,128]{1,0:T(8,128)(2,1)S(1)} %get-tuple-element.50), channel_id=1, source_target_pairs={{0,1},{1,0},{2,3},{3,2},{4,5},{5,4},{6,7},{7,6},{8,9},{9,8},{10,11... | collective-permute-start | bytes 98312 | tf_op jit(solution)/shard_map/ppermute | solution.py:202
  41.4 8.3 %collective-permute-start.13 = (bf16[16,3072]{1,0:T(8,128)(2,1)S(1)}, bf16[16,3072]{1,0:T(8,128)(2,1)S(1)}, u32[]{:S(2)}, u32[]{:S(2)}) collective-permute-start(bf16[16,3072]{1,0:T(8,128)(2,1)S(1)} %shard_map.97.refs_1_.x0), channel_id=1, source_target_pairs={{0,12},{4,8},{8,4},{12,0},{1,13},{5,9},{9,5},{13,1},{2,14},{6,10},... | collective-permute-start | bytes 294920 | tf_op jit(solution)/shard_map/ppermute | solution.py:202
  43.4 7.5 %collective-permute-start.14 = (bf16[16,3072]{1,0:T(8,128)(2,1)S(1)}, bf16[16,3072]{1,0:T(8,128)(2,1)S(1)}, u32[]{:S(2)}, u32[]{:S(2)}) collective-permute-start(bf16[16,3072]{1,0:T(8,128)(2,1)S(1)} %shard_map.97.refs_1_.x0), channel_id=1, source_target_pairs={{0,4},{4,0},{8,12},{12,8},{1,5},{5,1},{9,13},{13,9},{2,6},{6,2},{1... | collective-permute-start | bytes 294920 | tf_op jit(solution)/shard_map/ppermute | solution.py:202
  43.6 8.4 %collective-permute-start.15 = (bf16[16,3072]{1,0:T(8,128)(2,1)S(1)}, bf16[16,3072]{1,0:T(8,128)(2,1)S(1)}, u32[]{:S(2)}, u32[]{:S(2)}) collective-permute-start(bf16[16,3072]{1,0:T(8,128)(2,1)S(1)} %shard_map.97.refs_1_.x0), channel_id=1, source_target_pairs={{0,8},{4,12},{8,0},{12,4},{1,9},{5,13},{9,1},{13,5},{2,10},{6,14},... | collective-permute-start | bytes 294920 | tf_op jit(solution)/shard_map/ppermute | solution.py:202
  54.3 2.6 %collective-permute-start.16 = (f32[32,1536]{1,0:T(8,128)S(1)}, f32[32,1536]{1,0:T(8,128)S(1)}, u32[]{:S(2)}, u32[]{:S(2)}) collective-permute-start(f32[32,1536]{1,0:T(8,128)S(1)} %get-tuple-element.54), channel_id=1, source_target_pairs={{0,1},{1,0},{2,3},{3,2},{4,5},{5,4},{6,7},{7,6},{8,9},{9,8},{10,11... | collective-permute-start | bytes 589832 | tf_op jit(solution)/shard_map/ppermute | solution.py:494
  56.4 2.1 %collective-permute-start.18 = (f32[32,1536]{1,0:T(8,128)S(1)}, f32[32,1536]{1,0:T(8,128)S(1)}, u32[]{:S(2)}, u32[]{:S(2)}) collective-permute-start(f32[32,1536]{1,0:T(8,128)S(1)} %get-tuple-element.58), channel_id=1, source_target_pairs={{0,1},{1,0},{2,3},{3,2},{4,5},{5,4},{6,7},{7,6},{8,9},{9,8},{10,11... | collective-permute-start | bytes 589832 | tf_op jit(solution)/shard_map/ppermute | solution.py:494
  56.9 4.3 %collective-permute-start.17 = (bf16[16,1536]{1,0:T(8,128)(2,1)S(1)}, bf16[16,1536]{1,0:T(8,128)(2,1)S(1)}, u32[]{:S(2)}, u32[]{:S(2)}) collective-permute-start(bf16[16,1536]{1,0:T(8,128)(2,1)S(1)} %fusion.2), channel_id=1, source_target_pairs={{0,2},{1,3},{2,0},{3,1},{4,6},{5,7},{6,4},{7,5},{8,10},{9,11},{10,... | collective-permute-start | bytes 147464 | tf_op jit(solution)/shard_map/ppermute | solution.py:496
  58.4 4.2 %collective-permute-start.19 = (bf16[16,1536]{1,0:T(8,128)(2,1)S(1)}, bf16[16,1536]{1,0:T(8,128)(2,1)S(1)}, u32[]{:S(2)}, u32[]{:S(2)}) collective-permute-start(bf16[16,1536]{1,0:T(8,128)(2,1)S(1)} %fusion.1), channel_id=1, source_target_pairs={{0,2},{1,3},{2,0},{3,1},{4,6},{5,7},{6,4},{7,5},{8,10},{9,11},{10,... | collective-permute-start | bytes 147464 | tf_op jit(solution)/shard_map/ppermute | solution.py:496
  (1 other events, 5.3 us)

commit v4 on v3

--- a/solution.py
+++ b/solution.py
@@ -138,6 +138,7 @@
 ROWS = 4
 BLOCK = SIDE * ROWS
 SLOTS = 16
+TOKENS_FROM = (0, 1, 2, 3)
 FROM = (0, 3, 1, 2)
 HEADS_FROM = (0, 2, 3, 1)
 CONTEXT_FROM = (0, 2, 3, 1)
@@ -206,7 +207,7 @@
     weights = refs[:count]
     keep, send, rows = refs[count:]
     m = lax.axis_index("gx") ^ lax.axis_index("gy")
-    for s, x in zip(FROM, (x0, x1, x2, x3)):
+    for s, x in zip(TOKENS_FROM, (x0, x1, x2, x3)):
         d = s ^ m
         place = ((d & 1) << 1) | (d >> 1)
         rows[pl.ds(pl.multiple_of(place * BLOCK, BLOCK), BLOCK), :] = x[...]
@@ -414,12 +415,10 @@
     cosine = jnp.concatenate([cosine, cosine], axis=1)
     sine = jnp.concatenate([-sine, sine], axis=1)
 
-    near = partners(lambda k: tokens, "gx", FROM)
+    near = partners(lambda k: tokens, "gx", TOKENS_FROM)
     tile = 512
     part = q_width // 2
-    w_first, w_second, key_matrix, value_matrix, _ = fetch(
-        [(w_query, 0, part), (w_query, part, part), (key_matrix,), (value_matrix,)]
-    )
+    w_first, w_second, _ = fetch([(w_query, 0, part), (w_query, part, part)])
     sums = []
     for weights in ((w_first,), (w_second, key_matrix, value_matrix)):
         columns = sum(w.shape[1] for w in weights)

time: 63.4 us -> 62.8 us (level)
  waiting for transfers between devices: 12.4 us -> 13.9 us
  starting transfers between devices: 23.4 us -> 22.1 us
  Pallas kernels: 27 us -> 26.2 us
    ppermute x4, waiting for transfers between devices: 0.01 us -> 0.94 us  [square_shards(): got = lax.ppermute(send, 'gy', [(p, p ^ 1) for p in range(SIDE)])]
    pallas_call x3, Pallas kernels: 15.8 us -> 14.9 us  [fetch(): pl.pallas_call(functools.partial(fetch_body, plan), out_shape=[*outs, don...]
    ppermute x4, waiting for transfers between devices: 3.66 us -> 4.45 us  [square_shards(): lax.ppermute(summed, 'gy', [(p, p ^ 2) for p in range(SIDE)])]
    ppermute x12, starting transfers between devices: 16.7 us -> 16.1 us  [partners(): lax.ppermute(block(k), axis, [(p, p ^ k) for p in range(SIDE)])]
  transfers between devices with their start and end apart: 20 -> 20, of which waited for: 9 -> 10; matrix products, arithmetic and copies ran while one was open for 0% -> 0% of each run, Pallas kernels for 32% -> 28%
where the time goes in v4:
time: 62.8 us; the launch traced here: 62.7 us
  Pallas kernels  26.2 us (42%)
  starting transfers between devices  22.1 us (35%)
  waiting for transfers between devices  13.9 us (22%)
    ppermute x12, starting transfers between devices, partners(): lax.ppermute(block(k), axis, [(p, p ^ k) for p in range(SIDE)])  16.1 us
    pallas_call x3, Pallas kernels, fetch(): pl.pallas_call(functools.partial(fetch_body, plan), out_shape=[*outs, don...  14.9 us
    pallas_call x8, Pallas kernels, call(): pl.pallas_call(body, out_shape=outs, in_specs=specs, out_specs=jax.tree.m...  11.2 us
    ppermute x12, waiting for transfers between devices, partners(): lax.ppermute(block(k), axis, [(p, p ^ k) for p in range(SIDE)])  8.48 us
    ppermute x4, starting transfers between devices, square_shards(): lax.ppermute(summed, 'gy', [(p, p ^ 2) for p in range(SIDE)])  4.83 us
    ppermute x4, waiting for transfers between devices, square_shards(): lax.ppermute(summed, 'gy', [(p, p ^ 2) for p in range(SIDE)])  4.45 us
  transfers between devices with their start and end apart: 20, of which 10 were waited for; matrix products, arithmetic and copies ran while one was open for 0% of the time, Pallas kernels for 28%

profile of v4, /device:TPU:0, one launch (start us, length us, event | category | flops | bytes accessed | tf_op | source)
XLA Modules:
  0.0 62.7 jit_solution(6073229187695663317)
XLA Ops:
  0.0 5.0 %collective-permute-start.2 = (bf16[16,3072]{1,0:T(8,128)(2,1)}, bf16[16,3072]{1,0:T(8,128)(2,1)S(1)}, u32[]{:S(2)}, u32[]{:S(2)}) collective-permute-start(bf16[16,3072]{1,0:T(8,128)(2,1)} %x0.3), channel_id=1, source_target_pairs={{0,12},{4,8},{8,4},{12,0},{1,13},{5,9},{9,5},{13,1},{2,14},{6,10},... | collective-permute-start | bytes 294920 | tf_op jit(solution)/shard_map/ppermute | solution.py:203
  5.7 7.1 %shard_map.91 = (bf16[3072,1536]{1,0:T(8,128)(2,1)S(1)}, bf16[3072,1536]{1,0:T(8,128)(2,1)S(1)}, f32[8,128]{1,0:T(8,128)}) custom-call(bf16[3072,3072]{1,0:T(8,128)(2,1)} %refs_0_.3), custom_call_target="tpu_custom_call" | custom-call | bytes 18874368 | tf_op jit(solution)/shard_map/pallas_call | solution.py:191
  13.6 2.0 %shard_map.92 = (f32[2,192,128]{2,1,0:T(8,128)S(1)}, f32[2,192,128]{2,1,0:T(8,128)S(1)}) custom-call(bf16[16,3072]{1,0:T(8,128)(2,1)S(1)} %copy-done.4, bf16[16,3072]{1,0:T(8,128)(2,1)S(1)} %collective-permute-done.x1, bf16[16,3072]{1,0:T(8,128)(2,1)S(1)} %collective-permute-done.1.x2, bf16[16,3072]{1,0:T(8,128)(2,1)S(1)} %collective-permute-done.2.x3, ...), custom_call_target="tpu_custom_call" | custom-call | flops 603979776 | bytes 9437184 | tf_op jit(solution)/shard_map/pallas_call | solution.py:148
  15.7 2.6 %shard_map.93 = (f32[2,256,128]{2,1,0:T(8,128)S(1)}, f32[2,256,128]{2,1,0:T(8,128)S(1)}) custom-call(bf16[16,3072]{1,0:T(8,128)(2,1)S(1)} %copy-done.4, bf16[16,3072]{1,0:T(8,128)(2,1)S(1)} %collective-permute-done.x1, bf16[16,3072]{1,0:T(8,128)(2,1)S(1)} %collective-permute-done.1.x2, bf16[16,3072]{1,0:T(8,128)(2,1)S(1)} %collective-permute-done.2.x3, ...), custom_call_target="tpu_custom_call" | custom-call | flops 805306368 | bytes 12582912 | tf_op jit(solution)/shard_map/pallas_call | solution.py:148
  18.9 1.6 %collective-permute-start.4 = (f32[192,128]{1,0:T(8,128)S(1)}, f32[192,128]{1,0:T(8,128)S(1)}, u32[]{:S(2)}, u32[]{:S(2)}) collective-permute-start(f32[192,128]{1,0:T(8,128)S(1)} %fusion.3), channel_id=1, source_target_pairs={{0,2},{1,3},{2,0},{3,1},{4,6},{5,7},{6,4},{7,5},{8,10},{9,11},{10,... | collective-permute-start | bytes 294920 | tf_op jit(solution)/shard_map/ppermute | solution.py:437
  20.5 1.1 %collective-permute-start.6 = (f32[256,128]{1,0:T(8,128)S(1)}, f32[256,128]{1,0:T(8,128)S(1)}, u32[]{:S(2)}, u32[]{:S(2)}) collective-permute-start(f32[256,128]{1,0:T(8,128)S(1)} %fusion.refs_3_), channel_id=1, source_target_pairs={{0,2},{1,3},{2,0},{3,1},{4,6},{5,7},{6,4},{7,5},{8,10},{9,11},{10,... | collective-permute-start | bytes 393224 | tf_op jit(solution)/shard_map/ppermute | solution.py:437
  21.7 4.0 %shard_map.94 = (bf16[4,128,1024]{2,1,0:T(8,128)(2,1)S(1)}, bf16[4,128,1024]{2,1,0:T(8,128)(2,1)S(1)}, bf16[3072,1536]{1,0:T(8,128)(2,1)S(1)}, f32[8,128]{1,0:T(8,128)S(1)}) custom-call(bf16[4,128,1024]{2,1,0:T(8,128)(2,1)S(1)} %copy-done.2, bf16[4,128,1024]{2,1,0:T(8,128)(2,1)S(1)} %copy-done.3, bf16[3072,3072]{1,0:T(8,128)(2,1)} %refs_0_.5, ...), custom_call_target="tpu_custom_call" | custom-call | bytes 11534336 | tf_op jit(solution)/shard_map/pallas_call | solution.py:191
  26.6 1.7 %collective-permute-start.7 = (bf16[128,128]{1,0:T(8,128)(2,1)S(1)}, bf16[128,128]{1,0:T(8,128)(2,1)S(1)}, u32[]{:S(2)}, u32[]{:S(2)}) collective-permute-start(bf16[128,128]{1,0:T(8,128)(2,1)S(1)} %get-tuple-element.38), channel_id=1, source_target_pairs={{0,8},{4,12},{8,0},{12,4},{1,9},{5,13},{9,1},{13,5},{2,10},{6,14},... | collective-permute-start | bytes 98312 | tf_op jit(solution)/shard_map/ppermute | solution.py:203
  28.4 1.5 %collective-permute-start.8 = (bf16[128,128]{1,0:T(8,128)(2,1)S(1)}, bf16[128,128]{1,0:T(8,128)(2,1)S(1)}, u32[]{:S(2)}, u32[]{:S(2)}) collective-permute-start(bf16[128,128]{1,0:T(8,128)(2,1)S(1)} %get-tuple-element.39), channel_id=1, source_target_pairs={{0,12},{4,8},{8,4},{12,0},{1,13},{5,9},{9,5},{13,1},{2,14},{6,10},... | collective-permute-start | bytes 98312 | tf_op jit(solution)/shard_map/ppermute | solution.py:203
  30.5 1.9 %collective-permute-done.7.a1 = bf16[128,128]{1,0:T(8,128)(2,1)S(1)} collective-permute-done((bf16[128,128]{1,0:T(8,128)(2,1)S(1)}, bf16[128,128]{1,0:T(8,128)(2,1)S(1)}, u32[]{:S(2)}, u32[]{:S(2)}) %collective-permute-start.7) | collective-permute-done | bytes 32800 | tf_op jit(solution)/shard_map/ppermute | solution.py:203
  32.4 1.8 %collective-permute-done.8.a2 = bf16[128,128]{1,0:T(8,128)(2,1)S(1)} collective-permute-done((bf16[128,128]{1,0:T(8,128)(2,1)S(1)}, bf16[128,128]{1,0:T(8,128)(2,1)S(1)}, u32[]{:S(2)}, u32[]{:S(2)}) %collective-permute-start.8) | collective-permute-done | bytes 32800 | tf_op jit(solution)/shard_map/ppermute | solution.py:203
  34.2 1.4 %shard_map.96 = (bf16[128,128]{1,0:T(8,128)(2,1)S(1)}, bf16[128,128]{1,0:T(8,128)(2,1)S(1)}, bf16[128,128]{1,0:T(8,128)(2,1)S(1)}, bf16[128,128]{1,0:T(8,128)(2,1)S(1)}) custom-call(s32[4]{0:T(128)S(1)} %copy-done.5, bf16[128,128]{1,0:T(8,128)(2,1)S(1)} %get-tuple-element.37.a0, bf16[128,128]{1,0:T(8,128)(2,1)S(1)} %collective-permute-done.7.a1, ...), custom_call_target="tpu_custom_call" | custom-call | tf_op jit(solution)/shard_map/pallas_call | solution.py:148
  35.6 1.6 %collective-permute-start.10 = (bf16[128,128]{1,0:T(8,128)(2,1)S(1)}, bf16[128,128]{1,0:T(8,128)(2,1)S(1)}, u32[]{:S(2)}, u32[]{:S(2)}) collective-permute-start(bf16[128,128]{1,0:T(8,128)(2,1)S(1)} %get-tuple-element.44), channel_id=1, source_target_pairs={{0,2},{1,3},{2,0},{3,1},{4,6},{5,7},{6,4},{7,5},{8,10},{9,11},{10,... | collective-permute-start | bytes 98312 | tf_op jit(solution)/shard_map/ppermute | solution.py:203
  37.8 1.8 %collective-permute-done.10.c1 = bf16[128,128]{1,0:T(8,128)(2,1)S(1)} collective-permute-done((bf16[128,128]{1,0:T(8,128)(2,1)S(1)}, bf16[128,128]{1,0:T(8,128)(2,1)S(1)}, u32[]{:S(2)}, u32[]{:S(2)}) %collective-permute-start.10) | collective-permute-done | bytes 32800 | tf_op jit(solution)/shard_map/ppermute | solution.py:203
  40.6 1.7 %collective-permute-start.15 = (bf16[16,3072]{1,0:T(8,128)(2,1)S(1)}, bf16[16,3072]{1,0:T(8,128)(2,1)S(1)}, u32[]{:S(2)}, u32[]{:S(2)}) collective-permute-start(bf16[16,3072]{1,0:T(8,128)(2,1)S(1)} %shard_map.97.refs_1_.x0), channel_id=1, source_target_pairs={{0,8},{4,12},{8,0},{12,4},{1,9},{5,13},{9,1},{13,5},{2,10},{6,14},... | collective-permute-start | bytes 294920 | tf_op jit(solution)/shard_map/ppermute | solution.py:203
  43.2 1.9 %collective-permute-start.13 = (bf16[16,3072]{1,0:T(8,128)(2,1)S(1)}, bf16[16,3072]{1,0:T(8,128)(2,1)S(1)}, u32[]{:S(2)}, u32[]{:S(2)}) collective-permute-start(bf16[16,3072]{1,0:T(8,128)(2,1)S(1)} %shard_map.97.refs_1_.x0), channel_id=1, source_target_pairs={{0,12},{4,8},{8,4},{12,0},{1,13},{5,9},{9,5},{13,1},{2,14},{6,10},... | collective-permute-start | bytes 294920 | tf_op jit(solution)/shard_map/ppermute | solution.py:203
  45.1 3.8 %shard_map.98 = (bf16[3072,1536]{1,0:T(8,128)(2,1)S(1)}, f32[8,128]{1,0:T(8,128)S(1)}) custom-call(bf16[3072,3072]{1,0:T(8,128)(2,1)} %refs_0_.5, bf16[16,3072]{1,0:T(8,128)(2,1)S(1)} %shard_map.97.refs_1_.x0), custom_call_target="tpu_custom_call" | custom-call | bytes 9437184 | tf_op jit(solution)/shard_map/pallas_call | solution.py:191
  48.9 1.4 %collective-permute-done.15.x3 = bf16[16,3072]{1,0:T(8,128)(2,1)S(1)} collective-permute-done((bf16[16,3072]{1,0:T(8,128)(2,1)S(1)}, bf16[16,3072]{1,0:T(8,128)(2,1)S(1)}, u32[]{:S(2)}, u32[]{:S(2)}) %collective-permute-start.15) | collective-permute-done | bytes 98336 | tf_op jit(solution)/shard_map/ppermute | solution.py:203
  50.3 2.3 %shard_map.99 = (f32[32,1536]{1,0:T(8,128)S(1)}, f32[32,1536]{1,0:T(8,128)S(1)}, bf16[64,3072]{1,0:T(8,128)(2,1)S(1)}) custom-call(bf16[16,3072]{1,0:T(8,128)(2,1)S(1)} %shard_map.97.refs_1_.x0, bf16[16,3072]{1,0:T(8,128)(2,1)S(1)} %collective-permute-done.13.x1, bf16[16,3072]{1,0:T(8,128)(2,1)S(1)} %collective-permute-done.14.x2, ...), custom_call_target="tpu_custom_call" | custom-call | flops 603979776 | bytes 9437184 | tf_op jit(solution)/shard_map/pallas_call | solution.py:148
  52.5 2.0 %shard_map.100 = (f32[32,1536]{1,0:T(8,128)S(1)}, f32[32,1536]{1,0:T(8,128)S(1)}) custom-call(bf16[64,3072]{1,0:T(8,128)(2,1)S(1)} %get-tuple-element.51.ordered, bf16[3072,1536]{1,0:T(8,128)(2,1)S(1)} %get-tuple-element.52.w), custom_call_target="tpu_custom_call" | custom-call | flops 603979776 | bytes 9437184 | tf_op jit(solution)/shard_map/pallas_call | solution.py:148
  55.1 0.9 %collective-permute-done.18.got1 = f32[32,1536]{1,0:T(8,128)S(1)} collective-permute-done((f32[32,1536]{1,0:T(8,128)S(1)}, f32[32,1536]{1,0:T(8,128)S(1)}, u32[]{:S(2)}, u32[]{:S(2)}) %collective-permute-start.18) | collective-permute-done | bytes 196640 | tf_op jit(solution)/shard_map/ppermute | solution.py:493
  56.1 1.7 %collective-permute-start.19 = (bf16[16,1536]{1,0:T(8,128)(2,1)S(1)}, bf16[16,1536]{1,0:T(8,128)(2,1)S(1)}, u32[]{:S(2)}, u32[]{:S(2)}) collective-permute-start(bf16[16,1536]{1,0:T(8,128)(2,1)S(1)} %fusion.1), channel_id=1, source_target_pairs={{0,2},{1,3},{2,0},{3,1},{4,6},{5,7},{6,4},{7,5},{8,10},{9,11},{10,... | collective-permute-start | bytes 147464 | tf_op jit(solution)/shard_map/ppermute | solution.py:495
  58.3 2.0 %collective-permute-done.19.across1 = bf16[16,1536]{1,0:T(8,128)(2,1)S(1)} collective-permute-done((bf16[16,1536]{1,0:T(8,128)(2,1)S(1)}, bf16[16,1536]{1,0:T(8,128)(2,1)S(1)}, u32[]{:S(2)}, u32[]{:S(2)}) %collective-permute-start.19) | collective-permute-done | bytes 49184 | tf_op jit(solution)/shard_map/ppermute | solution.py:495
  60.2 1.7 %collective-permute-done.17.across0 = bf16[16,1536]{1,0:T(8,128)(2,1)S(1)} collective-permute-done((bf16[16,1536]{1,0:T(8,128)(2,1)S(1)}, bf16[16,1536]{1,0:T(8,128)(2,1)S(1)}, u32[]{:S(2)}, u32[]{:S(2)}) %collective-permute-start.17) | collective-permute-done | bytes 49184 | tf_op jit(solution)/shard_map/ppermute | solution.py:495
  (49 shorter events, 7.9 us)
Async XLA Ops:
  0.0 13.5 %copy-start.4 = (bf16[16,3072]{1,0:T(8,128)(2,1)S(1)}, bf16[16,3072]{1,0:T(8,128)(2,1)}, u32[]{:S(2)}) copy-start(bf16[16,3072]{1,0:T(8,128)(2,1)} %x0.3) | copy-start | bytes 294916
  0.0 12.8 %collective-permute-start.2 = (bf16[16,3072]{1,0:T(8,128)(2,1)}, bf16[16,3072]{1,0:T(8,128)(2,1)S(1)}, u32[]{:S(2)}, u32[]{:S(2)}) collective-permute-start(bf16[16,3072]{1,0:T(8,128)(2,1)} %x0.3), channel_id=1, source_target_pairs={{0,12},{4,8},{8,4},{12,0},{1,13},{5,9},{9,5},{13,1},{2,14},{6,10},... | collective-permute-start | bytes 294920 | tf_op jit(solution)/shard_map/ppermute | solution.py:203
  5.1 8.5 %collective-permute-start.1 = (bf16[16,3072]{1,0:T(8,128)(2,1)}, bf16[16,3072]{1,0:T(8,128)(2,1)S(1)}, u32[]{:S(2)}, u32[]{:S(2)}) collective-permute-start(bf16[16,3072]{1,0:T(8,128)(2,1)} %x0.3), channel_id=1, source_target_pairs={{0,8},{4,12},{8,0},{12,4},{1,9},{5,13},{9,1},{13,5},{2,10},{6,14},... | collective-permute-start | bytes 294920 | tf_op jit(solution)/shard_map/ppermute | solution.py:203
  5.1 8.5 %collective-permute-start = (bf16[16,3072]{1,0:T(8,128)(2,1)}, bf16[16,3072]{1,0:T(8,128)(2,1)S(1)}, u32[]{:S(2)}, u32[]{:S(2)}) collective-permute-start(bf16[16,3072]{1,0:T(8,128)(2,1)} %x0.3), channel_id=1, source_target_pairs={{0,4},{4,0},{8,12},{12,8},{1,5},{5,1},{9,13},{13,9},{2,6},{6,2},{1... | collective-permute-start | bytes 294920 | tf_op jit(solution)/shard_map/ppermute | solution.py:203
  13.5 8.2 %copy-start.2 = (bf16[4,128,1024]{2,1,0:T(8,128)(2,1)S(1)}, bf16[4,128,1024]{2,1,0:T(8,128)(2,1)}, u32[]{:S(2)}) copy-start(bf16[4,128,1024]{2,1,0:T(8,128)(2,1)} %refs_0_.4) | copy-start | bytes 3145732
  13.6 8.2 %copy-start.3 = (bf16[4,128,1024]{2,1,0:T(8,128)(2,1)S(1)}, bf16[4,128,1024]{2,1,0:T(8,128)(2,1)}, u32[]{:S(2)}) copy-start(bf16[4,128,1024]{2,1,0:T(8,128)(2,1)} %refs_1_.3) | copy-start | bytes 3145732
  15.6 3.3 %collective-permute-start.3 = (f32[2,192,128]{2,1,0:T(8,128)S(1)}, f32[2,192,128]{2,1,0:T(8,128)S(1)}, u32[]{:S(2)}, u32[]{:S(2)}) collective-permute-start(f32[2,192,128]{2,1,0:T(8,128)S(1)} %get-tuple-element.32), channel_id=1, source_target_pairs={{0,1},{1,0},{2,3},{3,2},{4,5},{5,4},{6,7},{7,6},{8,9},{9,8},{10,11... | collective-permute-start | bytes 589832 | tf_op jit(solution)/shard_map/ppermute | solution.py:435
  18.3 2.2 %collective-permute-start.5 = (f32[2,256,128]{2,1,0:T(8,128)S(1)}, f32[2,256,128]{2,1,0:T(8,128)S(1)}, u32[]{:S(2)}, u32[]{:S(2)}) collective-permute-start(f32[2,256,128]{2,1,0:T(8,128)S(1)} %get-tuple-element.35), channel_id=1, source_target_pairs={{0,1},{1,0},{2,3},{3,2},{4,5},{5,4},{6,7},{7,6},{8,9},{9,8},{10,11... | collective-permute-start | bytes 786440 | tf_op jit(solution)/shard_map/ppermute | solution.py:435
  18.9 6.9 %collective-permute-start.4 = (f32[192,128]{1,0:T(8,128)S(1)}, f32[192,128]{1,0:T(8,128)S(1)}, u32[]{:S(2)}, u32[]{:S(2)}) collective-permute-start(f32[192,128]{1,0:T(8,128)S(1)} %fusion.3), channel_id=1, source_target_pairs={{0,2},{1,3},{2,0},{3,1},{4,6},{5,7},{6,4},{7,5},{8,10},{9,11},{10,... | collective-permute-start | bytes 294920 | tf_op jit(solution)/shard_map/ppermute | solution.py:437
  20.5 6.0 %collective-permute-start.6 = (f32[256,128]{1,0:T(8,128)S(1)}, f32[256,128]{1,0:T(8,128)S(1)}, u32[]{:S(2)}, u32[]{:S(2)}) collective-permute-start(f32[256,128]{1,0:T(8,128)S(1)} %fusion.refs_3_), channel_id=1, source_target_pairs={{0,2},{1,3},{2,0},{3,1},{4,6},{5,7},{6,4},{7,5},{8,10},{9,11},{10,... | collective-permute-start | bytes 393224 | tf_op jit(solution)/shard_map/ppermute | solution.py:437
  21.7 12.4 %copy-start.5 = (s32[4]{0:T(128)S(1)}, s32[4]{0:T(128)}, u32[]{:S(2)}) copy-start(s32[4]{0:T(128)} %lengths.1) | copy-start | bytes 52
  26.6 5.7 %collective-permute-start.7 = (bf16[128,128]{1,0:T(8,128)(2,1)S(1)}, bf16[128,128]{1,0:T(8,128)(2,1)S(1)}, u32[]{:S(2)}, u32[]{:S(2)}) collective-permute-start(bf16[128,128]{1,0:T(8,128)(2,1)S(1)} %get-tuple-element.38), channel_id=1, source_target_pairs={{0,8},{4,12},{8,0},{12,4},{1,9},{5,13},{9,1},{13,5},{2,10},{6,14},... | collective-permute-start | bytes 98312 | tf_op jit(solution)/shard_map/ppermute | solution.py:203
  28.4 5.8 %collective-permute-start.8 = (bf16[128,128]{1,0:T(8,128)(2,1)S(1)}, bf16[128,128]{1,0:T(8,128)(2,1)S(1)}, u32[]{:S(2)}, u32[]{:S(2)}) collective-permute-start(bf16[128,128]{1,0:T(8,128)(2,1)S(1)} %get-tuple-element.39), channel_id=1, source_target_pairs={{0,12},{4,8},{8,4},{12,0},{1,13},{5,9},{9,5},{13,1},{2,14},{6,10},... | collective-permute-start | bytes 98312 | tf_op jit(solution)/shard_map/ppermute | solution.py:203
  29.9 4.3 %collective-permute-start.9 = (bf16[128,128]{1,0:T(8,128)(2,1)S(1)}, bf16[128,128]{1,0:T(8,128)(2,1)S(1)}, u32[]{:S(2)}, u32[]{:S(2)}) collective-permute-start(bf16[128,128]{1,0:T(8,128)(2,1)S(1)} %get-tuple-element.40), channel_id=1, source_target_pairs={{0,4},{4,0},{8,12},{12,8},{1,5},{5,1},{9,13},{13,9},{2,6},{6,2},{1... | collective-permute-start | bytes 98312 | tf_op jit(solution)/shard_map/ppermute | solution.py:203
  35.6 4.0 %collective-permute-start.10 = (bf16[128,128]{1,0:T(8,128)(2,1)S(1)}, bf16[128,128]{1,0:T(8,128)(2,1)S(1)}, u32[]{:S(2)}, u32[]{:S(2)}) collective-permute-start(bf16[128,128]{1,0:T(8,128)(2,1)S(1)} %get-tuple-element.44), channel_id=1, source_target_pairs={{0,2},{1,3},{2,0},{3,1},{4,6},{5,7},{6,4},{7,5},{8,10},{9,11},{10,... | collective-permute-start | bytes 98312 | tf_op jit(solution)/shard_map/ppermute | solution.py:203
  37.1 3.3 %collective-permute-start.11 = (bf16[128,128]{1,0:T(8,128)(2,1)S(1)}, bf16[128,128]{1,0:T(8,128)(2,1)S(1)}, u32[]{:S(2)}, u32[]{:S(2)}) collective-permute-start(bf16[128,128]{1,0:T(8,128)(2,1)S(1)} %get-tuple-element.45), channel_id=1, source_target_pairs={{0,3},{1,2},{2,1},{3,0},{4,7},{5,6},{6,5},{7,4},{8,11},{9,10},{10,... | collective-permute-start | bytes 98312 | tf_op jit(solution)/shard_map/ppermute | solution.py:203
  37.1 3.3 %collective-permute-start.12 = (bf16[128,128]{1,0:T(8,128)(2,1)S(1)}, bf16[128,128]{1,0:T(8,128)(2,1)S(1)}, u32[]{:S(2)}, u32[]{:S(2)}) collective-permute-start(bf16[128,128]{1,0:T(8,128)(2,1)S(1)} %get-tuple-element.46), channel_id=1, source_target_pairs={{0,1},{1,0},{2,3},{3,2},{4,5},{5,4},{6,7},{7,6},{8,9},{9,8},{10,11... | collective-permute-start | bytes 98312 | tf_op jit(solution)/shard_map/ppermute | solution.py:203
  40.6 9.6 %collective-permute-start.15 = (bf16[16,3072]{1,0:T(8,128)(2,1)S(1)}, bf16[16,3072]{1,0:T(8,128)(2,1)S(1)}, u32[]{:S(2)}, u32[]{:S(2)}) collective-permute-start(bf16[16,3072]{1,0:T(8,128)(2,1)S(1)} %shard_map.97.refs_1_.x0), channel_id=1, source_target_pairs={{0,8},{4,12},{8,0},{12,4},{1,9},{5,13},{9,1},{13,5},{2,10},{6,14},... | collective-permute-start | bytes 294920 | tf_op jit(solution)/shard_map/ppermute | solution.py:203
  42.3 8.0 %collective-permute-start.14 = (bf16[16,3072]{1,0:T(8,128)(2,1)S(1)}, bf16[16,3072]{1,0:T(8,128)(2,1)S(1)}, u32[]{:S(2)}, u32[]{:S(2)}) collective-permute-start(bf16[16,3072]{1,0:T(8,128)(2,1)S(1)} %shard_map.97.refs_1_.x0), channel_id=1, source_target_pairs={{0,4},{4,0},{8,12},{12,8},{1,5},{5,1},{9,13},{13,9},{2,6},{6,2},{1... | collective-permute-start | bytes 294920 | tf_op jit(solution)/shard_map/ppermute | solution.py:203
  43.2 7.1 %collective-permute-start.13 = (bf16[16,3072]{1,0:T(8,128)(2,1)S(1)}, bf16[16,3072]{1,0:T(8,128)(2,1)S(1)}, u32[]{:S(2)}, u32[]{:S(2)}) collective-permute-start(bf16[16,3072]{1,0:T(8,128)(2,1)S(1)} %shard_map.97.refs_1_.x0), channel_id=1, source_target_pairs={{0,12},{4,8},{8,4},{12,0},{1,13},{5,9},{9,5},{13,1},{2,14},{6,10},... | collective-permute-start | bytes 294920 | tf_op jit(solution)/shard_map/ppermute | solution.py:203
  54.6 1.5 %collective-permute-start.18 = (f32[32,1536]{1,0:T(8,128)S(1)}, f32[32,1536]{1,0:T(8,128)S(1)}, u32[]{:S(2)}, u32[]{:S(2)}) collective-permute-start(f32[32,1536]{1,0:T(8,128)S(1)} %get-tuple-element.54), channel_id=1, source_target_pairs={{0,1},{1,0},{2,3},{3,2},{4,5},{5,4},{6,7},{7,6},{8,9},{9,8},{10,11... | collective-permute-start | bytes 589832 | tf_op jit(solution)/shard_map/ppermute | solution.py:493
  54.6 3.2 %collective-permute-start.16 = (f32[32,1536]{1,0:T(8,128)S(1)}, f32[32,1536]{1,0:T(8,128)S(1)}, u32[]{:S(2)}, u32[]{:S(2)}) collective-permute-start(f32[32,1536]{1,0:T(8,128)S(1)} %get-tuple-element.50), channel_id=1, source_target_pairs={{0,1},{1,0},{2,3},{3,2},{4,5},{5,4},{6,7},{7,6},{8,9},{9,8},{10,11... | collective-permute-start | bytes 589832 | tf_op jit(solution)/shard_map/ppermute | solution.py:493
  56.1 4.2 %collective-permute-start.19 = (bf16[16,1536]{1,0:T(8,128)(2,1)S(1)}, bf16[16,1536]{1,0:T(8,128)(2,1)S(1)}, u32[]{:S(2)}, u32[]{:S(2)}) collective-permute-start(bf16[16,1536]{1,0:T(8,128)(2,1)S(1)} %fusion.1), channel_id=1, source_target_pairs={{0,2},{1,3},{2,0},{3,1},{4,6},{5,7},{6,4},{7,5},{8,10},{9,11},{10,... | collective-permute-start | bytes 147464 | tf_op jit(solution)/shard_map/ppermute | solution.py:495
  57.8 4.2 %collective-permute-start.17 = (bf16[16,1536]{1,0:T(8,128)(2,1)S(1)}, bf16[16,1536]{1,0:T(8,128)(2,1)S(1)}, u32[]{:S(2)}, u32[]{:S(2)}) collective-permute-start(bf16[16,1536]{1,0:T(8,128)(2,1)S(1)} %fusion.2), channel_id=1, source_target_pairs={{0,2},{1,3},{2,0},{3,1},{4,6},{5,7},{6,4},{7,5},{8,10},{9,11},{10,... | collective-permute-start | bytes 147464 | tf_op jit(solution)/shard_map/ppermute | solution.py:495
  (3 other events, 11.0 us)

commit v5 on v4

--- a/solution.py
+++ b/solution.py
@@ -416,7 +416,7 @@
     sine = jnp.concatenate([-sine, sine], axis=1)
 
     near = partners(lambda k: tokens, "gx", TOKENS_FROM)
-    tile = 512
+    tile = q_width // 2
     part = q_width // 2
     w_first, w_second, _ = fetch([(w_query, 0, part), (w_query, part, part)])
     sums = []
@@ -510,7 +510,7 @@
         and whole_heads
         and groups * HEAD_WIDTH == key_matrix.shape[1]
         and groups * GROUP * HEAD_WIDTH == w_query.shape[1] == w_output.shape[0]
-        and w_output.shape[1] % 1024 == 0
+        and w_output.shape[1] == w_query.shape[1]
         and w_query.shape[1] % 1024 == 0
     )
     return square_shards(*args) if square else general_shards(*args)

time: 62.8 us -> 61.6 us (0.981)
  Pallas kernels: 26.2 us -> 25 us
    pallas_call x8, Pallas kernels: 11.2 us -> 10 us  [call(): pl.pallas_call(body, out_shape=outs, in_specs=specs, out_specs=jax.tree.m...]
where the time goes in v5:
time: 61.6 us; the launch traced here: 61.4 us
  Pallas kernels  25 us (41%)
  starting transfers between devices  22.1 us (36%)
  waiting for transfers between devices  13.9 us (23%)
    ppermute x12, starting transfers between devices, partners(): lax.ppermute(block(k), axis, [(p, p ^ k) for p in range(SIDE)])  16.1 us
    pallas_call x3, Pallas kernels, fetch(): pl.pallas_call(functools.partial(fetch_body, plan), out_shape=[*outs, don...  14.9 us
    pallas_call x8, Pallas kernels, call(): pl.pallas_call(body, out_shape=outs, in_specs=specs, out_specs=jax.tree.m...  10 us
    ppermute x12, waiting for transfers between devices, partners(): lax.ppermute(block(k), axis, [(p, p ^ k) for p in range(SIDE)])  8.48 us
    ppermute x4, starting transfers between devices, square_shards(): lax.ppermute(summed, 'gy', [(p, p ^ 2) for p in range(SIDE)])  4.83 us
    ppermute x4, waiting for transfers between devices, square_shards(): lax.ppermute(summed, 'gy', [(p, p ^ 2) for p in range(SIDE)])  4.45 us
  transfers between devices with their start and end apart: 20, of which 10 were waited for; matrix products, arithmetic and copies ran while one was open for 0% of the time, Pallas kernels for 28%

profile of v5, /device:TPU:0, one launch (start us, length us, event | category | flops | bytes accessed | tf_op | source)
XLA Modules:
  0.0 61.4 jit_solution(15916412524636255941)
XLA Ops:
  0.0 5.0 %collective-permute-start.2 = (bf16[16,3072]{1,0:T(8,128)(2,1)}, bf16[16,3072]{1,0:T(8,128)(2,1)S(1)}, u32[]{:S(2)}, u32[]{:S(2)}) collective-permute-start(bf16[16,3072]{1,0:T(8,128)(2,1)} %x0.3), channel_id=1, source_target_pairs={{0,12},{4,8},{8,4},{12,0},{1,13},{5,9},{9,5},{13,1},{2,14},{6,10},... | collective-permute-start | bytes 294920 | tf_op jit(solution)/shard_map/ppermute | solution.py:203
  5.7 7.1 %shard_map.91 = (bf16[3072,1536]{1,0:T(8,128)(2,1)S(1)}, bf16[3072,1536]{1,0:T(8,128)(2,1)S(1)}, f32[8,128]{1,0:T(8,128)}) custom-call(bf16[3072,3072]{1,0:T(8,128)(2,1)} %refs_0_.3), custom_call_target="tpu_custom_call" | custom-call | bytes 18874368 | tf_op jit(solution)/shard_map/pallas_call | solution.py:191
  13.6 1.7 %shard_map.92 = (f32[2,192,128]{2,1,0:T(8,128)S(1)}, f32[2,192,128]{2,1,0:T(8,128)S(1)}) custom-call(bf16[16,3072]{1,0:T(8,128)(2,1)S(1)} %copy-done.4, bf16[16,3072]{1,0:T(8,128)(2,1)S(1)} %collective-permute-done.x1, bf16[16,3072]{1,0:T(8,128)(2,1)S(1)} %collective-permute-done.1.x2, bf16[16,3072]{1,0:T(8,128)(2,1)S(1)} %collective-permute-done.2.x3, ...), custom_call_target="tpu_custom_call" | custom-call | flops 603979776 | bytes 9437184 | tf_op jit(solution)/shard_map/pallas_call | solution.py:148
  15.4 2.3 %shard_map.93 = (f32[2,256,128]{2,1,0:T(8,128)S(1)}, f32[2,256,128]{2,1,0:T(8,128)S(1)}) custom-call(bf16[16,3072]{1,0:T(8,128)(2,1)S(1)} %copy-done.4, bf16[16,3072]{1,0:T(8,128)(2,1)S(1)} %collective-permute-done.x1, bf16[16,3072]{1,0:T(8,128)(2,1)S(1)} %collective-permute-done.1.x2, bf16[16,3072]{1,0:T(8,128)(2,1)S(1)} %collective-permute-done.2.x3, ...), custom_call_target="tpu_custom_call" | custom-call | flops 805306368 | bytes 12582912 | tf_op jit(solution)/shard_map/pallas_call | solution.py:148
  18.3 1.6 %collective-permute-start.4 = (f32[192,128]{1,0:T(8,128)S(1)}, f32[192,128]{1,0:T(8,128)S(1)}, u32[]{:S(2)}, u32[]{:S(2)}) collective-permute-start(f32[192,128]{1,0:T(8,128)S(1)} %fusion.3), channel_id=1, source_target_pairs={{0,2},{1,3},{2,0},{3,1},{4,6},{5,7},{6,4},{7,5},{8,10},{9,11},{10,... | collective-permute-start | bytes 294920 | tf_op jit(solution)/shard_map/ppermute | solution.py:437
  19.9 1.1 %collective-permute-start.6 = (f32[256,128]{1,0:T(8,128)S(1)}, f32[256,128]{1,0:T(8,128)S(1)}, u32[]{:S(2)}, u32[]{:S(2)}) collective-permute-start(f32[256,128]{1,0:T(8,128)S(1)} %fusion.refs_3_), channel_id=1, source_target_pairs={{0,2},{1,3},{2,0},{3,1},{4,6},{5,7},{6,4},{7,5},{8,10},{9,11},{10,... | collective-permute-start | bytes 393224 | tf_op jit(solution)/shard_map/ppermute | solution.py:437
  21.1 4.0 %shard_map.94 = (bf16[4,128,1024]{2,1,0:T(8,128)(2,1)S(1)}, bf16[4,128,1024]{2,1,0:T(8,128)(2,1)S(1)}, bf16[3072,1536]{1,0:T(8,128)(2,1)S(1)}, f32[8,128]{1,0:T(8,128)S(1)}) custom-call(bf16[4,128,1024]{2,1,0:T(8,128)(2,1)S(1)} %copy-done.2, bf16[4,128,1024]{2,1,0:T(8,128)(2,1)S(1)} %copy-done.3, bf16[3072,3072]{1,0:T(8,128)(2,1)} %refs_0_.5, ...), custom_call_target="tpu_custom_call" | custom-call | bytes 11534336 | tf_op jit(solution)/shard_map/pallas_call | solution.py:191
  26.0 1.7 %collective-permute-start.7 = (bf16[128,128]{1,0:T(8,128)(2,1)S(1)}, bf16[128,128]{1,0:T(8,128)(2,1)S(1)}, u32[]{:S(2)}, u32[]{:S(2)}) collective-permute-start(bf16[128,128]{1,0:T(8,128)(2,1)S(1)} %get-tuple-element.38), channel_id=1, source_target_pairs={{0,8},{4,12},{8,0},{12,4},{1,9},{5,13},{9,1},{13,5},{2,10},{6,14},... | collective-permute-start | bytes 98312 | tf_op jit(solution)/shard_map/ppermute | solution.py:203
  27.7 1.5 %collective-permute-start.8 = (bf16[128,128]{1,0:T(8,128)(2,1)S(1)}, bf16[128,128]{1,0:T(8,128)(2,1)S(1)}, u32[]{:S(2)}, u32[]{:S(2)}) collective-permute-start(bf16[128,128]{1,0:T(8,128)(2,1)S(1)} %get-tuple-element.39), channel_id=1, source_target_pairs={{0,12},{4,8},{8,4},{12,0},{1,13},{5,9},{9,5},{13,1},{2,14},{6,10},... | collective-permute-start | bytes 98312 | tf_op jit(solution)/shard_map/ppermute | solution.py:203
  29.8 1.9 %collective-permute-done.7.a1 = bf16[128,128]{1,0:T(8,128)(2,1)S(1)} collective-permute-done((bf16[128,128]{1,0:T(8,128)(2,1)S(1)}, bf16[128,128]{1,0:T(8,128)(2,1)S(1)}, u32[]{:S(2)}, u32[]{:S(2)}) %collective-permute-start.7) | collective-permute-done | bytes 32800 | tf_op jit(solution)/shard_map/ppermute | solution.py:203
  31.8 1.8 %collective-permute-done.8.a2 = bf16[128,128]{1,0:T(8,128)(2,1)S(1)} collective-permute-done((bf16[128,128]{1,0:T(8,128)(2,1)S(1)}, bf16[128,128]{1,0:T(8,128)(2,1)S(1)}, u32[]{:S(2)}, u32[]{:S(2)}) %collective-permute-start.8) | collective-permute-done | bytes 32800 | tf_op jit(solution)/shard_map/ppermute | solution.py:203
  33.5 1.4 %shard_map.96 = (bf16[128,128]{1,0:T(8,128)(2,1)S(1)}, bf16[128,128]{1,0:T(8,128)(2,1)S(1)}, bf16[128,128]{1,0:T(8,128)(2,1)S(1)}, bf16[128,128]{1,0:T(8,128)(2,1)S(1)}) custom-call(s32[4]{0:T(128)S(1)} %copy-done.5, bf16[128,128]{1,0:T(8,128)(2,1)S(1)} %get-tuple-element.37.a0, bf16[128,128]{1,0:T(8,128)(2,1)S(1)} %collective-permute-done.7.a1, ...), custom_call_target="tpu_custom_call" | custom-call | tf_op jit(solution)/shard_map/pallas_call | solution.py:148
  35.0 1.6 %collective-permute-start.10 = (bf16[128,128]{1,0:T(8,128)(2,1)S(1)}, bf16[128,128]{1,0:T(8,128)(2,1)S(1)}, u32[]{:S(2)}, u32[]{:S(2)}) collective-permute-start(bf16[128,128]{1,0:T(8,128)(2,1)S(1)} %get-tuple-element.44), channel_id=1, source_target_pairs={{0,2},{1,3},{2,0},{3,1},{4,6},{5,7},{6,4},{7,5},{8,10},{9,11},{10,... | collective-permute-start | bytes 98312 | tf_op jit(solution)/shard_map/ppermute | solution.py:203
  37.2 1.8 %collective-permute-done.10.c1 = bf16[128,128]{1,0:T(8,128)(2,1)S(1)} collective-permute-done((bf16[128,128]{1,0:T(8,128)(2,1)S(1)}, bf16[128,128]{1,0:T(8,128)(2,1)S(1)}, u32[]{:S(2)}, u32[]{:S(2)}) %collective-permute-start.10) | collective-permute-done | bytes 32800 | tf_op jit(solution)/shard_map/ppermute | solution.py:203
  40.0 1.7 %collective-permute-start.15 = (bf16[16,3072]{1,0:T(8,128)(2,1)S(1)}, bf16[16,3072]{1,0:T(8,128)(2,1)S(1)}, u32[]{:S(2)}, u32[]{:S(2)}) collective-permute-start(bf16[16,3072]{1,0:T(8,128)(2,1)S(1)} %shard_map.97.refs_1_.x0), channel_id=1, source_target_pairs={{0,8},{4,12},{8,0},{12,4},{1,9},{5,13},{9,1},{13,5},{2,10},{6,14},... | collective-permute-start | bytes 294920 | tf_op jit(solution)/shard_map/ppermute | solution.py:203
  42.6 1.9 %collective-permute-start.13 = (bf16[16,3072]{1,0:T(8,128)(2,1)S(1)}, bf16[16,3072]{1,0:T(8,128)(2,1)S(1)}, u32[]{:S(2)}, u32[]{:S(2)}) collective-permute-start(bf16[16,3072]{1,0:T(8,128)(2,1)S(1)} %shard_map.97.refs_1_.x0), channel_id=1, source_target_pairs={{0,12},{4,8},{8,4},{12,0},{1,13},{5,9},{9,5},{13,1},{2,14},{6,10},... | collective-permute-start | bytes 294920 | tf_op jit(solution)/shard_map/ppermute | solution.py:203
  44.5 3.8 %shard_map.98 = (bf16[3072,1536]{1,0:T(8,128)(2,1)S(1)}, f32[8,128]{1,0:T(8,128)S(1)}) custom-call(bf16[3072,3072]{1,0:T(8,128)(2,1)} %refs_0_.5, bf16[16,3072]{1,0:T(8,128)(2,1)S(1)} %shard_map.97.refs_1_.x0), custom_call_target="tpu_custom_call" | custom-call | bytes 9437184 | tf_op jit(solution)/shard_map/pallas_call | solution.py:191
  48.3 1.4 %collective-permute-done.15.x3 = bf16[16,3072]{1,0:T(8,128)(2,1)S(1)} collective-permute-done((bf16[16,3072]{1,0:T(8,128)(2,1)S(1)}, bf16[16,3072]{1,0:T(8,128)(2,1)S(1)}, u32[]{:S(2)}, u32[]{:S(2)}) %collective-permute-start.15) | collective-permute-done | bytes 98336 | tf_op jit(solution)/shard_map/ppermute | solution.py:203
  49.7 1.9 %shard_map.99 = (f32[32,1536]{1,0:T(8,128)S(1)}, f32[32,1536]{1,0:T(8,128)S(1)}, bf16[64,3072]{1,0:T(8,128)(2,1)S(1)}) custom-call(bf16[16,3072]{1,0:T(8,128)(2,1)S(1)} %shard_map.97.refs_1_.x0, bf16[16,3072]{1,0:T(8,128)(2,1)S(1)} %collective-permute-done.13.x1, bf16[16,3072]{1,0:T(8,128)(2,1)S(1)} %collective-permute-done.14.x2, ...), custom_call_target="tpu_custom_call" | custom-call | flops 603979776 | bytes 9437184 | tf_op jit(solution)/shard_map/pallas_call | solution.py:148
  51.6 1.7 %shard_map.100 = (f32[32,1536]{1,0:T(8,128)S(1)}, f32[32,1536]{1,0:T(8,128)S(1)}) custom-call(bf16[64,3072]{1,0:T(8,128)(2,1)S(1)} %get-tuple-element.51.ordered, bf16[3072,1536]{1,0:T(8,128)(2,1)S(1)} %get-tuple-element.52.w), custom_call_target="tpu_custom_call" | custom-call | flops 603979776 | bytes 9437184 | tf_op jit(solution)/shard_map/pallas_call | solution.py:148
  53.9 0.9 %collective-permute-done.18.got1 = f32[32,1536]{1,0:T(8,128)S(1)} collective-permute-done((f32[32,1536]{1,0:T(8,128)S(1)}, f32[32,1536]{1,0:T(8,128)S(1)}, u32[]{:S(2)}, u32[]{:S(2)}) %collective-permute-start.18) | collective-permute-done | bytes 196640 | tf_op jit(solution)/shard_map/ppermute | solution.py:493
  54.9 1.7 %collective-permute-start.19 = (bf16[16,1536]{1,0:T(8,128)(2,1)S(1)}, bf16[16,1536]{1,0:T(8,128)(2,1)S(1)}, u32[]{:S(2)}, u32[]{:S(2)}) collective-permute-start(bf16[16,1536]{1,0:T(8,128)(2,1)S(1)} %fusion.1), channel_id=1, source_target_pairs={{0,2},{1,3},{2,0},{3,1},{4,6},{5,7},{6,4},{7,5},{8,10},{9,11},{10,... | collective-permute-start | bytes 147464 | tf_op jit(solution)/shard_map/ppermute | solution.py:495
  57.0 2.0 %collective-permute-done.19.across1 = bf16[16,1536]{1,0:T(8,128)(2,1)S(1)} collective-permute-done((bf16[16,1536]{1,0:T(8,128)(2,1)S(1)}, bf16[16,1536]{1,0:T(8,128)(2,1)S(1)}, u32[]{:S(2)}, u32[]{:S(2)}) %collective-permute-start.19) | collective-permute-done | bytes 49184 | tf_op jit(solution)/shard_map/ppermute | solution.py:495
  59.0 1.7 %collective-permute-done.17.across0 = bf16[16,1536]{1,0:T(8,128)(2,1)S(1)} collective-permute-done((bf16[16,1536]{1,0:T(8,128)(2,1)S(1)}, bf16[16,1536]{1,0:T(8,128)(2,1)S(1)}, u32[]{:S(2)}, u32[]{:S(2)}) %collective-permute-start.17) | collective-permute-done | bytes 49184 | tf_op jit(solution)/shard_map/ppermute | solution.py:495
  (49 shorter events, 7.9 us)
Async XLA Ops:
  0.0 13.5 %copy-start.4 = (bf16[16,3072]{1,0:T(8,128)(2,1)S(1)}, bf16[16,3072]{1,0:T(8,128)(2,1)}, u32[]{:S(2)}) copy-start(bf16[16,3072]{1,0:T(8,128)(2,1)} %x0.3) | copy-start | bytes 294916
  0.0 12.8 %collective-permute-start.2 = (bf16[16,3072]{1,0:T(8,128)(2,1)}, bf16[16,3072]{1,0:T(8,128)(2,1)S(1)}, u32[]{:S(2)}, u32[]{:S(2)}) collective-permute-start(bf16[16,3072]{1,0:T(8,128)(2,1)} %x0.3), channel_id=1, source_target_pairs={{0,12},{4,8},{8,4},{12,0},{1,13},{5,9},{9,5},{13,1},{2,14},{6,10},... | collective-permute-start | bytes 294920 | tf_op jit(solution)/shard_map/ppermute | solution.py:203
  5.1 8.5 %collective-permute-start.1 = (bf16[16,3072]{1,0:T(8,128)(2,1)}, bf16[16,3072]{1,0:T(8,128)(2,1)S(1)}, u32[]{:S(2)}, u32[]{:S(2)}) collective-permute-start(bf16[16,3072]{1,0:T(8,128)(2,1)} %x0.3), channel_id=1, source_target_pairs={{0,8},{4,12},{8,0},{12,4},{1,9},{5,13},{9,1},{13,5},{2,10},{6,14},... | collective-permute-start | bytes 294920 | tf_op jit(solution)/shard_map/ppermute | solution.py:203
  5.1 8.5 %collective-permute-start = (bf16[16,3072]{1,0:T(8,128)(2,1)}, bf16[16,3072]{1,0:T(8,128)(2,1)S(1)}, u32[]{:S(2)}, u32[]{:S(2)}) collective-permute-start(bf16[16,3072]{1,0:T(8,128)(2,1)} %x0.3), channel_id=1, source_target_pairs={{0,4},{4,0},{8,12},{12,8},{1,5},{5,1},{9,13},{13,9},{2,6},{6,2},{1... | collective-permute-start | bytes 294920 | tf_op jit(solution)/shard_map/ppermute | solution.py:203
  13.5 7.6 %copy-start.2 = (bf16[4,128,1024]{2,1,0:T(8,128)(2,1)S(1)}, bf16[4,128,1024]{2,1,0:T(8,128)(2,1)}, u32[]{:S(2)}) copy-start(bf16[4,128,1024]{2,1,0:T(8,128)(2,1)} %refs_0_.4) | copy-start | bytes 3145732
  13.6 7.6 %copy-start.3 = (bf16[4,128,1024]{2,1,0:T(8,128)(2,1)S(1)}, bf16[4,128,1024]{2,1,0:T(8,128)(2,1)}, u32[]{:S(2)}) copy-start(bf16[4,128,1024]{2,1,0:T(8,128)(2,1)} %refs_1_.3) | copy-start | bytes 3145732
  15.3 3.0 %collective-permute-start.3 = (f32[2,192,128]{2,1,0:T(8,128)S(1)}, f32[2,192,128]{2,1,0:T(8,128)S(1)}, u32[]{:S(2)}, u32[]{:S(2)}) collective-permute-start(f32[2,192,128]{2,1,0:T(8,128)S(1)} %get-tuple-element.32), channel_id=1, source_target_pairs={{0,1},{1,0},{2,3},{3,2},{4,5},{5,4},{6,7},{7,6},{8,9},{9,8},{10,11... | collective-permute-start | bytes 589832 | tf_op jit(solution)/shard_map/ppermute | solution.py:435
  17.7 2.2 %collective-permute-start.5 = (f32[2,256,128]{2,1,0:T(8,128)S(1)}, f32[2,256,128]{2,1,0:T(8,128)S(1)}, u32[]{:S(2)}, u32[]{:S(2)}) collective-permute-start(f32[2,256,128]{2,1,0:T(8,128)S(1)} %get-tuple-element.35), channel_id=1, source_target_pairs={{0,1},{1,0},{2,3},{3,2},{4,5},{5,4},{6,7},{7,6},{8,9},{9,8},{10,11... | collective-permute-start | bytes 786440 | tf_op jit(solution)/shard_map/ppermute | solution.py:435
  18.3 6.9 %collective-permute-start.4 = (f32[192,128]{1,0:T(8,128)S(1)}, f32[192,128]{1,0:T(8,128)S(1)}, u32[]{:S(2)}, u32[]{:S(2)}) collective-permute-start(f32[192,128]{1,0:T(8,128)S(1)} %fusion.3), channel_id=1, source_target_pairs={{0,2},{1,3},{2,0},{3,1},{4,6},{5,7},{6,4},{7,5},{8,10},{9,11},{10,... | collective-permute-start | bytes 294920 | tf_op jit(solution)/shard_map/ppermute | solution.py:437
  19.9 6.0 %collective-permute-start.6 = (f32[256,128]{1,0:T(8,128)S(1)}, f32[256,128]{1,0:T(8,128)S(1)}, u32[]{:S(2)}, u32[]{:S(2)}) collective-permute-start(f32[256,128]{1,0:T(8,128)S(1)} %fusion.refs_3_), channel_id=1, source_target_pairs={{0,2},{1,3},{2,0},{3,1},{4,6},{5,7},{6,4},{7,5},{8,10},{9,11},{10,... | collective-permute-start | bytes 393224 | tf_op jit(solution)/shard_map/ppermute | solution.py:437
  21.1 12.4 %copy-start.5 = (s32[4]{0:T(128)S(1)}, s32[4]{0:T(128)}, u32[]{:S(2)}) copy-start(s32[4]{0:T(128)} %lengths.1) | copy-start | bytes 52
  26.0 5.7 %collective-permute-start.7 = (bf16[128,128]{1,0:T(8,128)(2,1)S(1)}, bf16[128,128]{1,0:T(8,128)(2,1)S(1)}, u32[]{:S(2)}, u32[]{:S(2)}) collective-permute-start(bf16[128,128]{1,0:T(8,128)(2,1)S(1)} %get-tuple-element.38), channel_id=1, source_target_pairs={{0,8},{4,12},{8,0},{12,4},{1,9},{5,13},{9,1},{13,5},{2,10},{6,14},... | collective-permute-start | bytes 98312 | tf_op jit(solution)/shard_map/ppermute | solution.py:203
  27.7 5.8 %collective-permute-start.8 = (bf16[128,128]{1,0:T(8,128)(2,1)S(1)}, bf16[128,128]{1,0:T(8,128)(2,1)S(1)}, u32[]{:S(2)}, u32[]{:S(2)}) collective-permute-start(bf16[128,128]{1,0:T(8,128)(2,1)S(1)} %get-tuple-element.39), channel_id=1, source_target_pairs={{0,12},{4,8},{8,4},{12,0},{1,13},{5,9},{9,5},{13,1},{2,14},{6,10},... | collective-permute-start | bytes 98312 | tf_op jit(solution)/shard_map/ppermute | solution.py:203
  29.3 4.3 %collective-permute-start.9 = (bf16[128,128]{1,0:T(8,128)(2,1)S(1)}, bf16[128,128]{1,0:T(8,128)(2,1)S(1)}, u32[]{:S(2)}, u32[]{:S(2)}) collective-permute-start(bf16[128,128]{1,0:T(8,128)(2,1)S(1)} %get-tuple-element.40), channel_id=1, source_target_pairs={{0,4},{4,0},{8,12},{12,8},{1,5},{5,1},{9,13},{13,9},{2,6},{6,2},{1... | collective-permute-start | bytes 98312 | tf_op jit(solution)/shard_map/ppermute | solution.py:203
  35.0 4.0 %collective-permute-start.10 = (bf16[128,128]{1,0:T(8,128)(2,1)S(1)}, bf16[128,128]{1,0:T(8,128)(2,1)S(1)}, u32[]{:S(2)}, u32[]{:S(2)}) collective-permute-start(bf16[128,128]{1,0:T(8,128)(2,1)S(1)} %get-tuple-element.44), channel_id=1, source_target_pairs={{0,2},{1,3},{2,0},{3,1},{4,6},{5,7},{6,4},{7,5},{8,10},{9,11},{10,... | collective-permute-start | bytes 98312 | tf_op jit(solution)/shard_map/ppermute | solution.py:203
  36.5 3.3 %collective-permute-start.11 = (bf16[128,128]{1,0:T(8,128)(2,1)S(1)}, bf16[128,128]{1,0:T(8,128)(2,1)S(1)}, u32[]{:S(2)}, u32[]{:S(2)}) collective-permute-start(bf16[128,128]{1,0:T(8,128)(2,1)S(1)} %get-tuple-element.45), channel_id=1, source_target_pairs={{0,3},{1,2},{2,1},{3,0},{4,7},{5,6},{6,5},{7,4},{8,11},{9,10},{10,... | collective-permute-start | bytes 98312 | tf_op jit(solution)/shard_map/ppermute | solution.py:203
  36.5 3.3 %collective-permute-start.12 = (bf16[128,128]{1,0:T(8,128)(2,1)S(1)}, bf16[128,128]{1,0:T(8,128)(2,1)S(1)}, u32[]{:S(2)}, u32[]{:S(2)}) collective-permute-start(bf16[128,128]{1,0:T(8,128)(2,1)S(1)} %get-tuple-element.46), channel_id=1, source_target_pairs={{0,1},{1,0},{2,3},{3,2},{4,5},{5,4},{6,7},{7,6},{8,9},{9,8},{10,11... | collective-permute-start | bytes 98312 | tf_op jit(solution)/shard_map/ppermute | solution.py:203
  40.0 9.6 %collective-permute-start.15 = (bf16[16,3072]{1,0:T(8,128)(2,1)S(1)}, bf16[16,3072]{1,0:T(8,128)(2,1)S(1)}, u32[]{:S(2)}, u32[]{:S(2)}) collective-permute-start(bf16[16,3072]{1,0:T(8,128)(2,1)S(1)} %shard_map.97.refs_1_.x0), channel_id=1, source_target_pairs={{0,8},{4,12},{8,0},{12,4},{1,9},{5,13},{9,1},{13,5},{2,10},{6,14},... | collective-permute-start | bytes 294920 | tf_op jit(solution)/shard_map/ppermute | solution.py:203
  41.7 8.0 %collective-permute-start.14 = (bf16[16,3072]{1,0:T(8,128)(2,1)S(1)}, bf16[16,3072]{1,0:T(8,128)(2,1)S(1)}, u32[]{:S(2)}, u32[]{:S(2)}) collective-permute-start(bf16[16,3072]{1,0:T(8,128)(2,1)S(1)} %shard_map.97.refs_1_.x0), channel_id=1, source_target_pairs={{0,4},{4,0},{8,12},{12,8},{1,5},{5,1},{9,13},{13,9},{2,6},{6,2},{1... | collective-permute-start | bytes 294920 | tf_op jit(solution)/shard_map/ppermute | solution.py:203
  42.6 7.1 %collective-permute-start.13 = (bf16[16,3072]{1,0:T(8,128)(2,1)S(1)}, bf16[16,3072]{1,0:T(8,128)(2,1)S(1)}, u32[]{:S(2)}, u32[]{:S(2)}) collective-permute-start(bf16[16,3072]{1,0:T(8,128)(2,1)S(1)} %shard_map.97.refs_1_.x0), channel_id=1, source_target_pairs={{0,12},{4,8},{8,4},{12,0},{1,13},{5,9},{9,5},{13,1},{2,14},{6,10},... | collective-permute-start | bytes 294920 | tf_op jit(solution)/shard_map/ppermute | solution.py:203
  53.3 1.5 %collective-permute-start.18 = (f32[32,1536]{1,0:T(8,128)S(1)}, f32[32,1536]{1,0:T(8,128)S(1)}, u32[]{:S(2)}, u32[]{:S(2)}) collective-permute-start(f32[32,1536]{1,0:T(8,128)S(1)} %get-tuple-element.54), channel_id=1, source_target_pairs={{0,1},{1,0},{2,3},{3,2},{4,5},{5,4},{6,7},{7,6},{8,9},{9,8},{10,11... | collective-permute-start | bytes 589832 | tf_op jit(solution)/shard_map/ppermute | solution.py:493
  53.4 3.2 %collective-permute-start.16 = (f32[32,1536]{1,0:T(8,128)S(1)}, f32[32,1536]{1,0:T(8,128)S(1)}, u32[]{:S(2)}, u32[]{:S(2)}) collective-permute-start(f32[32,1536]{1,0:T(8,128)S(1)} %get-tuple-element.50), channel_id=1, source_target_pairs={{0,1},{1,0},{2,3},{3,2},{4,5},{5,4},{6,7},{7,6},{8,9},{9,8},{10,11... | collective-permute-start | bytes 589832 | tf_op jit(solution)/shard_map/ppermute | solution.py:493
  54.9 4.2 %collective-permute-start.19 = (bf16[16,1536]{1,0:T(8,128)(2,1)S(1)}, bf16[16,1536]{1,0:T(8,128)(2,1)S(1)}, u32[]{:S(2)}, u32[]{:S(2)}) collective-permute-start(bf16[16,1536]{1,0:T(8,128)(2,1)S(1)} %fusion.1), channel_id=1, source_target_pairs={{0,2},{1,3},{2,0},{3,1},{4,6},{5,7},{6,4},{7,5},{8,10},{9,11},{10,... | collective-permute-start | bytes 147464 | tf_op jit(solution)/shard_map/ppermute | solution.py:495
  56.6 4.2 %collective-permute-start.17 = (bf16[16,1536]{1,0:T(8,128)(2,1)S(1)}, bf16[16,1536]{1,0:T(8,128)(2,1)S(1)}, u32[]{:S(2)}, u32[]{:S(2)}) collective-permute-start(bf16[16,1536]{1,0:T(8,128)(2,1)S(1)} %fusion.2), channel_id=1, source_target_pairs={{0,2},{1,3},{2,0},{3,1},{4,6},{5,7},{6,4},{7,5},{8,10},{9,11},{10,... | collective-permute-start | bytes 147464 | tf_op jit(solution)/shard_map/ppermute | solution.py:495
  (3 other events, 9.9 us)

commit v6 on v5

--- a/solution.py
+++ b/solution.py
@@ -437,9 +437,7 @@
         sums += [keep, got, lax.ppermute(summed, "gy", [(p, p ^ 2) for p in range(SIDE)])]
     depth, out_width = w_output.shape
     part = out_width // 2
-    stored_keys, stored_values, w_first, ready = fetch(
-        [(stored_keys,), (stored_values,), (w_output, 0, part)], summed
-    )
+    w_first, ready = fetch([(w_output, 0, part)], summed)
     piece = jax.ShapeDtypeStruct((ROWS * wide, HEAD_WIDTH), bf16)
     mine = call(
         functools.partial(spread_body, groups),

time: 61.6 us -> 61.6 us (level)
  no operation moved by 1% of the time
where the time goes in v6:
time: 61.6 us; the launch traced here: 61.4 us
  Pallas kernels  24.9 us (40%)
  starting transfers between devices  22.1 us (36%)
  waiting for transfers between devices  13.9 us (23%)
    ppermute x12, starting transfers between devices, partners(): lax.ppermute(block(k), axis, [(p, p ^ k) for p in range(SIDE)])  16.1 us
    pallas_call x3, Pallas kernels, fetch(): pl.pallas_call(functools.partial(fetch_body, plan), out_shape=[*outs, don...  14.8 us
    pallas_call x8, Pallas kernels, call(): pl.pallas_call(body, out_shape=outs, in_specs=specs, out_specs=jax.tree.m...  10 us
    ppermute x12, waiting for transfers between devices, partners(): lax.ppermute(block(k), axis, [(p, p ^ k) for p in range(SIDE)])  8.48 us
    ppermute x4, starting transfers between devices, square_shards(): lax.ppermute(summed, 'gy', [(p, p ^ 2) for p in range(SIDE)])  4.83 us
    ppermute x4, waiting for transfers between devices, square_shards(): lax.ppermute(summed, 'gy', [(p, p ^ 2) for p in range(SIDE)])  4.52 us
  transfers between devices with their start and end apart: 20, of which 10 were waited for; matrix products, arithmetic and copies ran while one was open for 0% of the time, Pallas kernels for 28%

profile of v6, /device:TPU:0, one launch (start us, length us, event | category | flops | bytes accessed | tf_op | source)
XLA Modules:
  0.0 61.4 jit_solution(10429892750257061847)
XLA Ops:
  0.0 5.0 %collective-permute-start.2 = (bf16[16,3072]{1,0:T(8,128)(2,1)}, bf16[16,3072]{1,0:T(8,128)(2,1)S(1)}, u32[]{:S(2)}, u32[]{:S(2)}) collective-permute-start(bf16[16,3072]{1,0:T(8,128)(2,1)} %x0.3), channel_id=1, source_target_pairs={{0,12},{4,8},{8,4},{12,0},{1,13},{5,9},{9,5},{13,1},{2,14},{6,10},... | collective-permute-start | bytes 294920 | tf_op jit(solution)/shard_map/ppermute | solution.py:203
  5.7 7.1 %shard_map.91 = (bf16[3072,1536]{1,0:T(8,128)(2,1)S(1)}, bf16[3072,1536]{1,0:T(8,128)(2,1)S(1)}, f32[8,128]{1,0:T(8,128)}) custom-call(bf16[3072,3072]{1,0:T(8,128)(2,1)} %refs_0_.3), custom_call_target="tpu_custom_call" | custom-call | bytes 18874368 | tf_op jit(solution)/shard_map/pallas_call | solution.py:191
  13.5 1.7 %shard_map.92 = (f32[2,192,128]{2,1,0:T(8,128)S(1)}, f32[2,192,128]{2,1,0:T(8,128)S(1)}) custom-call(bf16[16,3072]{1,0:T(8,128)(2,1)S(1)} %copy-done.4, bf16[16,3072]{1,0:T(8,128)(2,1)S(1)} %collective-permute-done.x1, bf16[16,3072]{1,0:T(8,128)(2,1)S(1)} %collective-permute-done.1.x2, bf16[16,3072]{1,0:T(8,128)(2,1)S(1)} %collective-permute-done.2.x3, ...), custom_call_target="tpu_custom_call" | custom-call | flops 603979776 | bytes 9437184 | tf_op jit(solution)/shard_map/pallas_call | solution.py:148
  15.4 2.3 %shard_map.93 = (f32[2,256,128]{2,1,0:T(8,128)S(1)}, f32[2,256,128]{2,1,0:T(8,128)S(1)}) custom-call(bf16[16,3072]{1,0:T(8,128)(2,1)S(1)} %copy-done.4, bf16[16,3072]{1,0:T(8,128)(2,1)S(1)} %collective-permute-done.x1, bf16[16,3072]{1,0:T(8,128)(2,1)S(1)} %collective-permute-done.1.x2, bf16[16,3072]{1,0:T(8,128)(2,1)S(1)} %collective-permute-done.2.x3, ...), custom_call_target="tpu_custom_call" | custom-call | flops 805306368 | bytes 12582912 | tf_op jit(solution)/shard_map/pallas_call | solution.py:148
  18.3 1.6 %collective-permute-start.4 = (f32[192,128]{1,0:T(8,128)S(1)}, f32[192,128]{1,0:T(8,128)S(1)}, u32[]{:S(2)}, u32[]{:S(2)}) collective-permute-start(f32[192,128]{1,0:T(8,128)S(1)} %fusion.3), channel_id=1, source_target_pairs={{0,2},{1,3},{2,0},{3,1},{4,6},{5,7},{6,4},{7,5},{8,10},{9,11},{10,... | collective-permute-start | bytes 294920 | tf_op jit(solution)/shard_map/ppermute | solution.py:437
  19.9 1.1 %collective-permute-start.6 = (f32[256,128]{1,0:T(8,128)S(1)}, f32[256,128]{1,0:T(8,128)S(1)}, u32[]{:S(2)}, u32[]{:S(2)}) collective-permute-start(f32[256,128]{1,0:T(8,128)S(1)} %fusion.refs_1_), channel_id=1, source_target_pairs={{0,2},{1,3},{2,0},{3,1},{4,6},{5,7},{6,4},{7,5},{8,10},{9,11},{10,... | collective-permute-start | bytes 393224 | tf_op jit(solution)/shard_map/ppermute | solution.py:437
  21.1 3.9 %shard_map.94 = (bf16[3072,1536]{1,0:T(8,128)(2,1)S(1)}, f32[8,128]{1,0:T(8,128)S(1)}) custom-call(bf16[3072,3072]{1,0:T(8,128)(2,1)} %refs_0_.5, f32[256,128]{1,0:T(8,128)S(1)} %fusion.refs_1_), custom_call_target="tpu_custom_call" | custom-call | bytes 9437184 | tf_op jit(solution)/shard_map/pallas_call | solution.py:191
  26.0 1.7 %collective-permute-start.7 = (bf16[128,128]{1,0:T(8,128)(2,1)S(1)}, bf16[128,128]{1,0:T(8,128)(2,1)S(1)}, u32[]{:S(2)}, u32[]{:S(2)}) collective-permute-start(bf16[128,128]{1,0:T(8,128)(2,1)S(1)} %get-tuple-element.36), channel_id=1, source_target_pairs={{0,8},{4,12},{8,0},{12,4},{1,9},{5,13},{9,1},{13,5},{2,10},{6,14},... | collective-permute-start | bytes 98312 | tf_op jit(solution)/shard_map/ppermute | solution.py:203
  27.7 1.5 %collective-permute-start.8 = (bf16[128,128]{1,0:T(8,128)(2,1)S(1)}, bf16[128,128]{1,0:T(8,128)(2,1)S(1)}, u32[]{:S(2)}, u32[]{:S(2)}) collective-permute-start(bf16[128,128]{1,0:T(8,128)(2,1)S(1)} %get-tuple-element.37), channel_id=1, source_target_pairs={{0,12},{4,8},{8,4},{12,0},{1,13},{5,9},{9,5},{13,1},{2,14},{6,10},... | collective-permute-start | bytes 98312 | tf_op jit(solution)/shard_map/ppermute | solution.py:203
  29.8 1.9 %collective-permute-done.7.a1 = bf16[128,128]{1,0:T(8,128)(2,1)S(1)} collective-permute-done((bf16[128,128]{1,0:T(8,128)(2,1)S(1)}, bf16[128,128]{1,0:T(8,128)(2,1)S(1)}, u32[]{:S(2)}, u32[]{:S(2)}) %collective-permute-start.7) | collective-permute-done | bytes 32800 | tf_op jit(solution)/shard_map/ppermute | solution.py:203
  31.7 1.8 %collective-permute-done.8.a2 = bf16[128,128]{1,0:T(8,128)(2,1)S(1)} collective-permute-done((bf16[128,128]{1,0:T(8,128)(2,1)S(1)}, bf16[128,128]{1,0:T(8,128)(2,1)S(1)}, u32[]{:S(2)}, u32[]{:S(2)}) %collective-permute-start.8) | collective-permute-done | bytes 32800 | tf_op jit(solution)/shard_map/ppermute | solution.py:203
  33.5 1.4 %shard_map.96 = (bf16[128,128]{1,0:T(8,128)(2,1)S(1)}, bf16[128,128]{1,0:T(8,128)(2,1)S(1)}, bf16[128,128]{1,0:T(8,128)(2,1)S(1)}, bf16[128,128]{1,0:T(8,128)(2,1)S(1)}) custom-call(s32[4]{0:T(128)S(1)} %copy-done.5, bf16[128,128]{1,0:T(8,128)(2,1)S(1)} %get-tuple-element.35.a0, bf16[128,128]{1,0:T(8,128)(2,1)S(1)} %collective-permute-done.7.a1, ...), custom_call_target="tpu_custom_call" | custom-call | tf_op jit(solution)/shard_map/pallas_call | solution.py:148
  35.0 1.6 %collective-permute-start.10 = (bf16[128,128]{1,0:T(8,128)(2,1)S(1)}, bf16[128,128]{1,0:T(8,128)(2,1)S(1)}, u32[]{:S(2)}, u32[]{:S(2)}) collective-permute-start(bf16[128,128]{1,0:T(8,128)(2,1)S(1)} %get-tuple-element.40), channel_id=1, source_target_pairs={{0,2},{1,3},{2,0},{3,1},{4,6},{5,7},{6,4},{7,5},{8,10},{9,11},{10,... | collective-permute-start | bytes 98312 | tf_op jit(solution)/shard_map/ppermute | solution.py:203
  37.2 1.8 %collective-permute-done.10.c1 = bf16[128,128]{1,0:T(8,128)(2,1)S(1)} collective-permute-done((bf16[128,128]{1,0:T(8,128)(2,1)S(1)}, bf16[128,128]{1,0:T(8,128)(2,1)S(1)}, u32[]{:S(2)}, u32[]{:S(2)}) %collective-permute-start.10) | collective-permute-done | bytes 32800 | tf_op jit(solution)/shard_map/ppermute | solution.py:203
  40.0 1.6 %collective-permute-start.15 = (bf16[16,3072]{1,0:T(8,128)(2,1)S(1)}, bf16[16,3072]{1,0:T(8,128)(2,1)S(1)}, u32[]{:S(2)}, u32[]{:S(2)}) collective-permute-start(bf16[16,3072]{1,0:T(8,128)(2,1)S(1)} %shard_map.97.refs_1_.x0), channel_id=1, source_target_pairs={{0,8},{4,12},{8,0},{12,4},{1,9},{5,13},{9,1},{13,5},{2,10},{6,14},... | collective-permute-start | bytes 294920 | tf_op jit(solution)/shard_map/ppermute | solution.py:203
  42.5 1.9 %collective-permute-start.13 = (bf16[16,3072]{1,0:T(8,128)(2,1)S(1)}, bf16[16,3072]{1,0:T(8,128)(2,1)S(1)}, u32[]{:S(2)}, u32[]{:S(2)}) collective-permute-start(bf16[16,3072]{1,0:T(8,128)(2,1)S(1)} %shard_map.97.refs_1_.x0), channel_id=1, source_target_pairs={{0,12},{4,8},{8,4},{12,0},{1,13},{5,9},{9,5},{13,1},{2,14},{6,10},... | collective-permute-start | bytes 294920 | tf_op jit(solution)/shard_map/ppermute | solution.py:203
  44.5 3.8 %shard_map.98 = (bf16[3072,1536]{1,0:T(8,128)(2,1)S(1)}, f32[8,128]{1,0:T(8,128)S(1)}) custom-call(bf16[3072,3072]{1,0:T(8,128)(2,1)} %refs_0_.5, bf16[16,3072]{1,0:T(8,128)(2,1)S(1)} %shard_map.97.refs_1_.x0), custom_call_target="tpu_custom_call" | custom-call | bytes 9437184 | tf_op jit(solution)/shard_map/pallas_call | solution.py:191
  48.3 1.4 %collective-permute-done.15.x3 = bf16[16,3072]{1,0:T(8,128)(2,1)S(1)} collective-permute-done((bf16[16,3072]{1,0:T(8,128)(2,1)S(1)}, bf16[16,3072]{1,0:T(8,128)(2,1)S(1)}, u32[]{:S(2)}, u32[]{:S(2)}) %collective-permute-start.15) | collective-permute-done | bytes 98336 | tf_op jit(solution)/shard_map/ppermute | solution.py:203
  49.7 1.9 %shard_map.99 = (f32[32,1536]{1,0:T(8,128)S(1)}, f32[32,1536]{1,0:T(8,128)S(1)}, bf16[64,3072]{1,0:T(8,128)(2,1)S(1)}) custom-call(bf16[16,3072]{1,0:T(8,128)(2,1)S(1)} %shard_map.97.refs_1_.x0, bf16[16,3072]{1,0:T(8,128)(2,1)S(1)} %collective-permute-done.13.x1, bf16[16,3072]{1,0:T(8,128)(2,1)S(1)} %collective-permute-done.14.x2, ...), custom_call_target="tpu_custom_call" | custom-call | flops 603979776 | bytes 9437184 | tf_op jit(solution)/shard_map/pallas_call | solution.py:148
  51.6 1.7 %shard_map.100 = (f32[32,1536]{1,0:T(8,128)S(1)}, f32[32,1536]{1,0:T(8,128)S(1)}) custom-call(bf16[64,3072]{1,0:T(8,128)(2,1)S(1)} %get-tuple-element.47.ordered, bf16[3072,1536]{1,0:T(8,128)(2,1)S(1)} %get-tuple-element.48.w), custom_call_target="tpu_custom_call" | custom-call | flops 603979776 | bytes 9437184 | tf_op jit(solution)/shard_map/pallas_call | solution.py:148
  53.9 0.9 %collective-permute-done.18.got1 = f32[32,1536]{1,0:T(8,128)S(1)} collective-permute-done((f32[32,1536]{1,0:T(8,128)S(1)}, f32[32,1536]{1,0:T(8,128)S(1)}, u32[]{:S(2)}, u32[]{:S(2)}) %collective-permute-start.18) | collective-permute-done | bytes 196640 | tf_op jit(solution)/shard_map/ppermute | solution.py:491
  54.9 1.7 %collective-permute-start.19 = (bf16[16,1536]{1,0:T(8,128)(2,1)S(1)}, bf16[16,1536]{1,0:T(8,128)(2,1)S(1)}, u32[]{:S(2)}, u32[]{:S(2)}) collective-permute-start(bf16[16,1536]{1,0:T(8,128)(2,1)S(1)} %fusion.1), channel_id=1, source_target_pairs={{0,2},{1,3},{2,0},{3,1},{4,6},{5,7},{6,4},{7,5},{8,10},{9,11},{10,... | collective-permute-start | bytes 147464 | tf_op jit(solution)/shard_map/ppermute | solution.py:493
  57.0 2.0 %collective-permute-done.19.across1 = bf16[16,1536]{1,0:T(8,128)(2,1)S(1)} collective-permute-done((bf16[16,1536]{1,0:T(8,128)(2,1)S(1)}, bf16[16,1536]{1,0:T(8,128)(2,1)S(1)}, u32[]{:S(2)}, u32[]{:S(2)}) %collective-permute-start.19) | collective-permute-done | bytes 49184 | tf_op jit(solution)/shard_map/ppermute | solution.py:493
  59.0 1.7 %collective-permute-done.17.across0 = bf16[16,1536]{1,0:T(8,128)(2,1)S(1)} collective-permute-done((bf16[16,1536]{1,0:T(8,128)(2,1)S(1)}, bf16[16,1536]{1,0:T(8,128)(2,1)S(1)}, u32[]{:S(2)}, u32[]{:S(2)}) %collective-permute-start.17) | collective-permute-done | bytes 49184 | tf_op jit(solution)/shard_map/ppermute | solution.py:493
  (49 shorter events, 8.0 us)
Async XLA Ops:
  0.0 13.5 %copy-start.4 = (bf16[16,3072]{1,0:T(8,128)(2,1)S(1)}, bf16[16,3072]{1,0:T(8,128)(2,1)}, u32[]{:S(2)}) copy-start(bf16[16,3072]{1,0:T(8,128)(2,1)} %x0.3) | copy-start | bytes 294916
  0.0 12.8 %collective-permute-start.2 = (bf16[16,3072]{1,0:T(8,128)(2,1)}, bf16[16,3072]{1,0:T(8,128)(2,1)S(1)}, u32[]{:S(2)}, u32[]{:S(2)}) collective-permute-start(bf16[16,3072]{1,0:T(8,128)(2,1)} %x0.3), channel_id=1, source_target_pairs={{0,12},{4,8},{8,4},{12,0},{1,13},{5,9},{9,5},{13,1},{2,14},{6,10},... | collective-permute-start | bytes 294920 | tf_op jit(solution)/shard_map/ppermute | solution.py:203
  5.1 8.5 %collective-permute-start.1 = (bf16[16,3072]{1,0:T(8,128)(2,1)}, bf16[16,3072]{1,0:T(8,128)(2,1)S(1)}, u32[]{:S(2)}, u32[]{:S(2)}) collective-permute-start(bf16[16,3072]{1,0:T(8,128)(2,1)} %x0.3), channel_id=1, source_target_pairs={{0,8},{4,12},{8,0},{12,4},{1,9},{5,13},{9,1},{13,5},{2,10},{6,14},... | collective-permute-start | bytes 294920 | tf_op jit(solution)/shard_map/ppermute | solution.py:203
  5.1 8.5 %collective-permute-start = (bf16[16,3072]{1,0:T(8,128)(2,1)}, bf16[16,3072]{1,0:T(8,128)(2,1)S(1)}, u32[]{:S(2)}, u32[]{:S(2)}) collective-permute-start(bf16[16,3072]{1,0:T(8,128)(2,1)} %x0.3), channel_id=1, source_target_pairs={{0,4},{4,0},{8,12},{12,8},{1,5},{5,1},{9,13},{13,9},{2,6},{6,2},{1... | collective-permute-start | bytes 294920 | tf_op jit(solution)/shard_map/ppermute | solution.py:203
  15.3 3.0 %collective-permute-start.3 = (f32[2,192,128]{2,1,0:T(8,128)S(1)}, f32[2,192,128]{2,1,0:T(8,128)S(1)}, u32[]{:S(2)}, u32[]{:S(2)}) collective-permute-start(f32[2,192,128]{2,1,0:T(8,128)S(1)} %get-tuple-element.30), channel_id=1, source_target_pairs={{0,1},{1,0},{2,3},{3,2},{4,5},{5,4},{6,7},{7,6},{8,9},{9,8},{10,11... | collective-permute-start | bytes 589832 | tf_op jit(solution)/shard_map/ppermute | solution.py:435
  17.7 2.2 %collective-permute-start.5 = (f32[2,256,128]{2,1,0:T(8,128)S(1)}, f32[2,256,128]{2,1,0:T(8,128)S(1)}, u32[]{:S(2)}, u32[]{:S(2)}) collective-permute-start(f32[2,256,128]{2,1,0:T(8,128)S(1)} %get-tuple-element.33), channel_id=1, source_target_pairs={{0,1},{1,0},{2,3},{3,2},{4,5},{5,4},{6,7},{7,6},{8,9},{9,8},{10,11... | collective-permute-start | bytes 786440 | tf_op jit(solution)/shard_map/ppermute | solution.py:435
  18.3 6.8 %collective-permute-start.4 = (f32[192,128]{1,0:T(8,128)S(1)}, f32[192,128]{1,0:T(8,128)S(1)}, u32[]{:S(2)}, u32[]{:S(2)}) collective-permute-start(f32[192,128]{1,0:T(8,128)S(1)} %fusion.3), channel_id=1, source_target_pairs={{0,2},{1,3},{2,0},{3,1},{4,6},{5,7},{6,4},{7,5},{8,10},{9,11},{10,... | collective-permute-start | bytes 294920 | tf_op jit(solution)/shard_map/ppermute | solution.py:437
  19.9 6.0 %collective-permute-start.6 = (f32[256,128]{1,0:T(8,128)S(1)}, f32[256,128]{1,0:T(8,128)S(1)}, u32[]{:S(2)}, u32[]{:S(2)}) collective-permute-start(f32[256,128]{1,0:T(8,128)S(1)} %fusion.refs_1_), channel_id=1, source_target_pairs={{0,2},{1,3},{2,0},{3,1},{4,6},{5,7},{6,4},{7,5},{8,10},{9,11},{10,... | collective-permute-start | bytes 393224 | tf_op jit(solution)/shard_map/ppermute | solution.py:437
  21.1 12.4 %copy-start.2 = (bf16[4,128,1024]{2,1,0:T(8,128)(2,1)S(1)}, bf16[4,128,1024]{2,1,0:T(8,128)(2,1)}, u32[]{:S(2)}) copy-start(bf16[4,128,1024]{2,1,0:T(8,128)(2,1)} %keys.1) | copy-start | bytes 3145732
  21.1 12.4 %copy-start.3 = (bf16[4,128,1024]{2,1,0:T(8,128)(2,1)S(1)}, bf16[4,128,1024]{2,1,0:T(8,128)(2,1)}, u32[]{:S(2)}) copy-start(bf16[4,128,1024]{2,1,0:T(8,128)(2,1)} %values.1) | copy-start | bytes 3145732
  21.1 12.4 %copy-start.5 = (s32[4]{0:T(128)S(1)}, s32[4]{0:T(128)}, u32[]{:S(2)}) copy-start(s32[4]{0:T(128)} %lengths.1) | copy-start | bytes 52
  26.0 5.7 %collective-permute-start.7 = (bf16[128,128]{1,0:T(8,128)(2,1)S(1)}, bf16[128,128]{1,0:T(8,128)(2,1)S(1)}, u32[]{:S(2)}, u32[]{:S(2)}) collective-permute-start(bf16[128,128]{1,0:T(8,128)(2,1)S(1)} %get-tuple-element.36), channel_id=1, source_target_pairs={{0,8},{4,12},{8,0},{12,4},{1,9},{5,13},{9,1},{13,5},{2,10},{6,14},... | collective-permute-start | bytes 98312 | tf_op jit(solution)/shard_map/ppermute | solution.py:203
  27.7 5.8 %collective-permute-start.8 = (bf16[128,128]{1,0:T(8,128)(2,1)S(1)}, bf16[128,128]{1,0:T(8,128)(2,1)S(1)}, u32[]{:S(2)}, u32[]{:S(2)}) collective-permute-start(bf16[128,128]{1,0:T(8,128)(2,1)S(1)} %get-tuple-element.37), channel_id=1, source_target_pairs={{0,12},{4,8},{8,4},{12,0},{1,13},{5,9},{9,5},{13,1},{2,14},{6,10},... | collective-permute-start | bytes 98312 | tf_op jit(solution)/shard_map/ppermute | solution.py:203
  29.3 4.3 %collective-permute-start.9 = (bf16[128,128]{1,0:T(8,128)(2,1)S(1)}, bf16[128,128]{1,0:T(8,128)(2,1)S(1)}, u32[]{:S(2)}, u32[]{:S(2)}) collective-permute-start(bf16[128,128]{1,0:T(8,128)(2,1)S(1)} %get-tuple-element.38), channel_id=1, source_target_pairs={{0,4},{4,0},{8,12},{12,8},{1,5},{5,1},{9,13},{13,9},{2,6},{6,2},{1... | collective-permute-start | bytes 98312 | tf_op jit(solution)/shard_map/ppermute | solution.py:203
  35.0 4.0 %collective-permute-start.10 = (bf16[128,128]{1,0:T(8,128)(2,1)S(1)}, bf16[128,128]{1,0:T(8,128)(2,1)S(1)}, u32[]{:S(2)}, u32[]{:S(2)}) collective-permute-start(bf16[128,128]{1,0:T(8,128)(2,1)S(1)} %get-tuple-element.40), channel_id=1, source_target_pairs={{0,2},{1,3},{2,0},{3,1},{4,6},{5,7},{6,4},{7,5},{8,10},{9,11},{10,... | collective-permute-start | bytes 98312 | tf_op jit(solution)/shard_map/ppermute | solution.py:203
  36.5 3.3 %collective-permute-start.11 = (bf16[128,128]{1,0:T(8,128)(2,1)S(1)}, bf16[128,128]{1,0:T(8,128)(2,1)S(1)}, u32[]{:S(2)}, u32[]{:S(2)}) collective-permute-start(bf16[128,128]{1,0:T(8,128)(2,1)S(1)} %get-tuple-element.41), channel_id=1, source_target_pairs={{0,3},{1,2},{2,1},{3,0},{4,7},{5,6},{6,5},{7,4},{8,11},{9,10},{10,... | collective-permute-start | bytes 98312 | tf_op jit(solution)/shard_map/ppermute | solution.py:203
  36.5 3.3 %collective-permute-start.12 = (bf16[128,128]{1,0:T(8,128)(2,1)S(1)}, bf16[128,128]{1,0:T(8,128)(2,1)S(1)}, u32[]{:S(2)}, u32[]{:S(2)}) collective-permute-start(bf16[128,128]{1,0:T(8,128)(2,1)S(1)} %get-tuple-element.42), channel_id=1, source_target_pairs={{0,1},{1,0},{2,3},{3,2},{4,5},{5,4},{6,7},{7,6},{8,9},{9,8},{10,11... | collective-permute-start | bytes 98312 | tf_op jit(solution)/shard_map/ppermute | solution.py:203
  40.0 9.6 %collective-permute-start.15 = (bf16[16,3072]{1,0:T(8,128)(2,1)S(1)}, bf16[16,3072]{1,0:T(8,128)(2,1)S(1)}, u32[]{:S(2)}, u32[]{:S(2)}) collective-permute-start(bf16[16,3072]{1,0:T(8,128)(2,1)S(1)} %shard_map.97.refs_1_.x0), channel_id=1, source_target_pairs={{0,8},{4,12},{8,0},{12,4},{1,9},{5,13},{9,1},{13,5},{2,10},{6,14},... | collective-permute-start | bytes 294920 | tf_op jit(solution)/shard_map/ppermute | solution.py:203
  41.6 8.0 %collective-permute-start.14 = (bf16[16,3072]{1,0:T(8,128)(2,1)S(1)}, bf16[16,3072]{1,0:T(8,128)(2,1)S(1)}, u32[]{:S(2)}, u32[]{:S(2)}) collective-permute-start(bf16[16,3072]{1,0:T(8,128)(2,1)S(1)} %shard_map.97.refs_1_.x0), channel_id=1, source_target_pairs={{0,4},{4,0},{8,12},{12,8},{1,5},{5,1},{9,13},{13,9},{2,6},{6,2},{1... | collective-permute-start | bytes 294920 | tf_op jit(solution)/shard_map/ppermute | solution.py:203
  42.5 7.1 %collective-permute-start.13 = (bf16[16,3072]{1,0:T(8,128)(2,1)S(1)}, bf16[16,3072]{1,0:T(8,128)(2,1)S(1)}, u32[]{:S(2)}, u32[]{:S(2)}) collective-permute-start(bf16[16,3072]{1,0:T(8,128)(2,1)S(1)} %shard_map.97.refs_1_.x0), channel_id=1, source_target_pairs={{0,12},{4,8},{8,4},{12,0},{1,13},{5,9},{9,5},{13,1},{2,14},{6,10},... | collective-permute-start | bytes 294920 | tf_op jit(solution)/shard_map/ppermute | solution.py:203
  53.3 1.5 %collective-permute-start.18 = (f32[32,1536]{1,0:T(8,128)S(1)}, f32[32,1536]{1,0:T(8,128)S(1)}, u32[]{:S(2)}, u32[]{:S(2)}) collective-permute-start(f32[32,1536]{1,0:T(8,128)S(1)} %get-tuple-element.50), channel_id=1, source_target_pairs={{0,1},{1,0},{2,3},{3,2},{4,5},{5,4},{6,7},{7,6},{8,9},{9,8},{10,11... | collective-permute-start | bytes 589832 | tf_op jit(solution)/shard_map/ppermute | solution.py:491
  53.4 3.2 %collective-permute-start.16 = (f32[32,1536]{1,0:T(8,128)S(1)}, f32[32,1536]{1,0:T(8,128)S(1)}, u32[]{:S(2)}, u32[]{:S(2)}) collective-permute-start(f32[32,1536]{1,0:T(8,128)S(1)} %get-tuple-element.46), channel_id=1, source_target_pairs={{0,1},{1,0},{2,3},{3,2},{4,5},{5,4},{6,7},{7,6},{8,9},{9,8},{10,11... | collective-permute-start | bytes 589832 | tf_op jit(solution)/shard_map/ppermute | solution.py:491
  54.9 4.2 %collective-permute-start.19 = (bf16[16,1536]{1,0:T(8,128)(2,1)S(1)}, bf16[16,1536]{1,0:T(8,128)(2,1)S(1)}, u32[]{:S(2)}, u32[]{:S(2)}) collective-permute-start(bf16[16,1536]{1,0:T(8,128)(2,1)S(1)} %fusion.1), channel_id=1, source_target_pairs={{0,2},{1,3},{2,0},{3,1},{4,6},{5,7},{6,4},{7,5},{8,10},{9,11},{10,... | collective-permute-start | bytes 147464 | tf_op jit(solution)/shard_map/ppermute | solution.py:493
  56.6 4.2 %collective-permute-start.17 = (bf16[16,1536]{1,0:T(8,128)(2,1)S(1)}, bf16[16,1536]{1,0:T(8,128)(2,1)S(1)}, u32[]{:S(2)}, u32[]{:S(2)}) collective-permute-start(bf16[16,1536]{1,0:T(8,128)(2,1)S(1)} %fusion.2), channel_id=1, source_target_pairs={{0,2},{1,3},{2,0},{3,1},{4,6},{5,7},{6,4},{7,5},{8,10},{9,11},{10,... | collective-permute-start | bytes 147464 | tf_op jit(solution)/shard_map/ppermute | solution.py:493
  (3 other events, 9.8 us)
